TPU v7x, 128 devices: a whole 4x4x4 slice. The times are simulated.
128 devices in a mesh: grp: 16 (over y, x), dev: 8 (over z, core).
Axes of the slice: x: 4, y: 4, z: 4, core: 2. Of those that a mesh axis runs over, the one named last changes fastest.
Arguments:
- panel: float32 [16384, 512], P(('grp', 'dev')), may hold values from -9 to 9
- trailing: float32 [16384, 1792], P(('grp', 'dev')), may hold values from -32 to 32
- counts: int32 [16384], P(('grp', 'dev')), may hold values from 1 to 16
Outputs:
- r_factor: float32 [512, 512], P('dev')
- coupling: float32 [512, 1792], P('dev')
- updated: float32 [16384, 1792], P(('grp', 'dev'))
All inputs are finite; a program needn't handle non-finite values.
Results may differ from a plain program's by a relative error of at most 0.00025.
Values sent between devices are 32-bit elements; how exact they have to be, the bound alone decides.
No kernel may reach another device: no remote copies, remote signals or barrier semaphores. Data moves between devices by JAX's collectives and lax.ppermute only.
A program may use at most 320 MiB of HBM per device.

v0:
```python
import jax
import jax.numpy as jnp
from jax import lax
from jax.sharding import PartitionSpec as P

ridge_shift = 0.05


def prefix(part, axis, combine, identity):
    place = lax.axis_index(axis)
    gathered = lax.all_gather(part, axis)
    state = jnp.zeros_like(part) + jnp.asarray(identity, part.dtype)

    def one(lap, state):
        return combine(state, lax.dynamic_index_in_dim(gathered, lap, 0, False))

    return lax.fori_loop(0, place, one, state)


def broadcast(block, axis, source):
    block = jnp.where(lax.axis_index(axis) == source, block, jnp.zeros_like(block))
    return lax.psum(block, axis)


def matmul(left, right):
    return jnp.dot(left, right, precision=lax.Precision.HIGHEST, preferred_element_type=jnp.float32)


def add_terms(earlier, later):
    return earlier + later


def across_groups(terms):
    before = prefix(terms, "grp", add_terms, jnp.zeros_like(terms))
    totals = before + terms
    return broadcast(totals, "grp", lax.axis_size("grp") - 1)


def factor_block(block):
    size = block.shape[0]
    index = jnp.arange(size, dtype=jnp.int32)

    def column_step(step, carry):
        work, lower = carry
        column = lax.dynamic_slice_in_dim(work, step, 1, 1)[:, 0]
        pivot = lax.dynamic_slice_in_dim(column, step, 1, 0)[0]
        scaled = jnp.where(index >= step, column * lax.rsqrt(pivot), jnp.float32(0.0))
        lower = lax.dynamic_update_slice_in_dim(lower, scaled[:, None], step, 1)
        work = work - scaled[:, None] * scaled[None, :]
        return (work, lower)

    start = (block, jnp.zeros_like(block))
    return lax.fori_loop(0, size, column_step, start)[1]


def invert_lower(lower):
    size = lower.shape[0]
    eye_mat = jnp.eye(size, dtype=jnp.float32)
    diagonal_vals = jnp.diagonal(lower)
    nilpotent = eye_mat - lower / diagonal_vals[:, None]
    result = eye_mat + nilpotent
    power = nilpotent
    reach = 2
    while reach < size:
        power = matmul(power, power)
        result = result + matmul(result, power)
        reach = reach * 2
    return result / diagonal_vals[None, :]


def factor_full(gram):
    width = gram.shape[0]
    block = min(64, width)
    count_blocks = width // block
    lower_full = jnp.zeros_like(gram)
    inverses = []
    work = gram
    for level in range(count_blocks):
        first = level * block
        last = first + block
        diag_lower = factor_block(work[first:last, first:last])
        diag_inverse = invert_lower(diag_lower)
        inverses.append(diag_inverse)
        lower_full = lower_full.at[first:last, first:last].set(diag_lower)
        if last < width:
            below = matmul(work[last:, first:last], diag_inverse.T)
            lower_full = lower_full.at[last:, first:last].set(below)
            work = work.at[last:, last:].add(-matmul(below, below.T))
    return (lower_full, inverses)


def forward_solve(lower_full, inverses, right):
    block = inverses[0].shape[0]
    solved = []
    for level in range(len(inverses)):
        first = level * block
        last = first + block
        section = right[first:last]
        if level > 0:
            section = section - matmul(lower_full[first:last, :first], jnp.concatenate(solved, 0))
        solved.append(matmul(inverses[level], section))
    return jnp.concatenate(solved, 0)


def backward_solve(lower_full, inverses, right):
    block = inverses[0].shape[0]
    count_blocks = len(inverses)
    solved = []
    for level in range(count_blocks - 1, -1, -1):
        first = level * block
        last = first + block
        section = right[first:last]
        if level < count_blocks - 1:
            section = section - matmul(lower_full[last:, first:last].T, jnp.concatenate(solved, 0))
        solved.insert(0, matmul(inverses[level].T, section))
    return jnp.concatenate(solved, 0)


def local(panel, trailing, counts):
    highest = lax.Precision.HIGHEST
    rows_dev, panel_width = panel.shape
    groups = lax.axis_size("grp")
    members = lax.axis_size("dev")
    weights = counts.astype(jnp.float32) / (rows_dev * groups * members)
    weighted = panel * weights[:, None]
    gram_local = jnp.einsum(
        "rp,rq->pq", panel, weighted, precision=highest, preferred_element_type=jnp.float32
    )
    identity_mat = jnp.eye(panel_width, dtype=jnp.float32)
    row_block = panel_width // members
    row_start = lax.axis_index("dev") * row_block
    cross_local = jnp.einsum(
        "rt,rp->tp", trailing, weighted, precision=highest, preferred_element_type=jnp.float32
    )
    summed = lax.psum(jnp.concatenate([gram_local, cross_local], 0), "dev")
    reduced = across_groups(summed)
    lower_factor, inverses = factor_full(reduced[:panel_width] + ridge_shift * identity_mat)
    coupling_full = forward_solve(lower_factor, inverses, reduced[panel_width:].T)
    mixing = backward_solve(lower_factor, inverses, coupling_full)
    updated = trailing - jnp.dot(
        panel, mixing, precision=highest, preferred_element_type=jnp.float32
    )
    coupling = lax.dynamic_slice_in_dim(coupling_full, row_start, row_block, 0)
    r_rows = lax.dynamic_slice_in_dim(lower_factor.T, row_start, row_block, 0)
    return (r_rows, coupling, updated)


def solution(mesh):
    return jax.shard_map(
        local,
        mesh=mesh,
        in_specs=(P(("grp", "dev"), None), P(("grp", "dev"), None), P(("grp", "dev"))),
        out_specs=(P("dev", None), P("dev", None), P(("grp", "dev"), None)),
        check_vma=False,
    )
```

profile of v0, /device:TPU:1, one launch (start us, length us, event | category | flops | bytes accessed | tf_op | source)
XLA Modules:
  0.0 1678.6 jit_solution(2896708494164801613)
XLA Ops:
  7.9 2.1 convolution_bitcast_fusion.2
  10.0 6.3 convolution_bitcast_fusion
  16.6 4.5 pad_maximum_fusion
  21.2 76.4 %all-reduce.4.cloned.1.call-done = f32[2304,512]{0,1:T(8,128)} async-done(((f32[2304,512]{0,1:T(8,128)}), f32[2304,512]{0,1:T(8,128)}) %all-reduce.4.cloned.1.call-update) | async-done | bytes 4718608 | tf_op jit(solution)/shard_map/psum | solution.py:135
  97.7 415.0 %all-gather.3.cloned.1.call-done = f32[36864,512]{0,1:T(8,128)} async-done(((f32[2304,512]{0,1:T(8,128)}), f32[36864,512]{0,1:T(8,128)}) %all-gather.3.cloned.1.call-update) | async-done | bytes 75497488 | tf_op jit(solution)/shard_map/all_gather | solution.py:11
  512.6 73.0 %copy.40 = f32[36864,512]{1,0:T(8,128)} copy(f32[36864,512]{0,1:T(8,128)} %all-gather.3.cloned.1.call-done) | data formatting | bytes 150994944 | tf_op jit(solution)/shard_map/while | solution.py:17
  585.6 2.9 broadcast.864.clone
  588.7 6.2 copy.25
  594.9 6.5 add_select_fusion
  601.4 1.2 copy-done.1
  602.9 213.7 %all-reduce.6.cloned.1.call-done = f32[2304,512]{0,1:T(8,128)} async-done(((f32[2304,512]{0,1:T(8,128)}), f32[2304,512]{0,1:T(8,128)}) %all-reduce.6.cloned.1.call-update) | async-done | bytes 4718608 | tf_op jit(solution)/shard_map/psum | solution.py:22
  816.6 1.3 slice_add_fusion
  817.9 101.1 %while.185 = (s32[]{:T(128)}, f32[64,64]{0,1:T(8,128)S(1)}, f32[64,64]{0,1:T(8,128)S(1)}, s32[]{:T(128)}, s32[]{:T(128)}, /*index=5*/s32[]{:T(128)}) while((s32[]{:T(128)}, f32[64,64]{0,1:T(8,128)S(1)}, f32[64,64]{0,1:T(8,128)S(1)}, s32[]{:T(128)}, s32[]{:T(128)}, /*index=5*/s32[]{:T(128)}) %tuple.445), condition=%wide.region_5.6_spmd.clone, body=%wide.region_4.5_spmd.clone.sunk | while | flops 8771 | bytes 40045 | solution.py:53
  817.9 0.7 dynamic_slice.251
  819.5 0.7 dynamic_slice.251
  821.1 0.7 dynamic_slice.251
  822.7 0.7 dynamic_slice.251
  824.3 0.7 dynamic_slice.251
  825.8 0.7 dynamic_slice.251
  827.4 0.7 dynamic_slice.251
  829.0 0.7 dynamic_slice.251
  919.1 0.8 gather_fusion
  922.1 1.0 fusion.41
  923.1 101.1 %while.186 = (s32[]{:T(128)}, f32[64,64]{0,1:T(8,128)S(1)}, f32[64,64]{0,1:T(8,128)S(1)}, s32[]{:T(128)}, s32[]{:T(128)}, /*index=5*/s32[]{:T(128)}) while((s32[]{:T(128)}, f32[64,64]{0,1:T(8,128)S(1)}, f32[64,64]{0,1:T(8,128)S(1)}, s32[]{:T(128)}, s32[]{:T(128)}, /*index=5*/s32[]{:T(128)}) %tuple.448), condition=%wide.region_7.8_spmd.clone, body=%wide.region_6.7_spmd.clone.sunk | while | flops 8771 | bytes 40045 | solution.py:53
  1024.3 0.8 gather_fusion.1
  1027.0 2.1 scatter.51
  1029.1 1.4 scatter.54
  1031.0 0.7 fusion.42
  1031.7 101.1 %while.187 = (s32[]{:T(128)}, f32[64,64]{0,1:T(8,128)S(1)}, f32[64,64]{0,1:T(8,128)S(1)}, s32[]{:T(128)}, s32[]{:T(128)}, /*index=5*/s32[]{:T(128)}) while((s32[]{:T(128)}, f32[64,64]{0,1:T(8,128)S(1)}, f32[64,64]{0,1:T(8,128)S(1)}, s32[]{:T(128)}, s32[]{:T(128)}, /*index=5*/s32[]{:T(128)}) %tuple.451), condition=%wide.region_9.10_spmd.clone, body=%wide.region_8.9_spmd.clone.sunk | while | flops 8771 | bytes 40045 | solution.py:53
  1132.9 0.8 gather_fusion.2
  1136.6 93.2 %while.188 = (s32[]{:T(128)}, f32[64,64]{0,1:T(8,128)S(1)}, f32[64,64]{0,1:T(8,128)S(1)}, s32[]{:T(128)}, s32[]{:T(128)}, /*index=5*/s32[]{:T(128)}) while((s32[]{:T(128)}, f32[64,64]{0,1:T(8,128)S(1)}, f32[64,64]{0,1:T(8,128)S(1)}, s32[]{:T(128)}, s32[]{:T(128)}, /*index=5*/s32[]{:T(128)}) %tuple.454), condition=%wide.region_11.12_spmd.clone, body=%wide.region_10.11_spmd.clone.sunk | while | flops 8771 | bytes 40045 | solution.py:53
  1229.9 0.8 gather_fusion.3
  1232.4 1.1 scatter.56
  1233.5 1.8 scatter.59
  1235.3 1.4 scatter.60
  1237.6 93.6 %while.189 = (s32[]{:T(128)}, f32[64,64]{0,1:T(8,128)S(1)}, f32[64,64]{0,1:T(8,128)S(1)}, s32[]{:T(128)}, s32[]{:T(128)}, /*index=5*/s32[]{:T(128)}) while((s32[]{:T(128)}, f32[64,64]{0,1:T(8,128)S(1)}, f32[64,64]{0,1:T(8,128)S(1)}, s32[]{:T(128)}, s32[]{:T(128)}, /*index=5*/s32[]{:T(128)}) %tuple.457), condition=%wide.region_13.14_spmd.clone, body=%wide.region_12.13_spmd.clone.sunk | while | flops 8771 | bytes 40045 | solution.py:53
  1331.3 0.8 gather_fusion.4
  1334.6 93.2 %while.190 = (s32[]{:T(128)}, f32[64,64]{0,1:T(8,128)S(1)}, f32[64,64]{0,1:T(8,128)S(1)}, s32[]{:T(128)}, s32[]{:T(128)}, /*index=5*/s32[]{:T(128)}) while((s32[]{:T(128)}, f32[64,64]{0,1:T(8,128)S(1)}, f32[64,64]{0,1:T(8,128)S(1)}, s32[]{:T(128)}, s32[]{:T(128)}, /*index=5*/s32[]{:T(128)}) %tuple.460), condition=%wide.region_15.16_spmd.clone, body=%wide.region_14.15_spmd.clone.sunk | while | flops 8771 | bytes 40045 | solution.py:53
  1427.9 0.8 gather_fusion.5
  1430.4 1.1 scatter.64
  1431.5 1.4 scatter.65
  1433.0 1.4 scatter.66
  1435.2 93.2 %while.191 = (s32[]{:T(128)}, f32[64,64]{0,1:T(8,128)S(1)}, f32[64,64]{0,1:T(8,128)S(1)}, s32[]{:T(128)}, s32[]{:T(128)}, /*index=5*/s32[]{:T(128)}) while((s32[]{:T(128)}, f32[64,64]{0,1:T(8,128)S(1)}, f32[64,64]{0,1:T(8,128)S(1)}, s32[]{:T(128)}, s32[]{:T(128)}, /*index=5*/s32[]{:T(128)}) %tuple.463), condition=%wide.region_17.18_spmd.clone, body=%wide.region_16.17_spmd.clone.sunk | while | flops 8771 | bytes 40045 | solution.py:53
  1528.4 0.8 gather_fusion.6
  1531.6 93.2 %while.192 = (s32[]{:T(128)}, f32[64,64]{0,1:T(8,128)S(1)}, f32[64,64]{0,1:T(8,128)S(1)}, s32[]{:T(128)}, s32[]{:T(128)}, /*index=5*/s32[]{:T(128)}) while((s32[]{:T(128)}, f32[64,64]{0,1:T(8,128)S(1)}, f32[64,64]{0,1:T(8,128)S(1)}, s32[]{:T(128)}, s32[]{:T(128)}, /*index=5*/s32[]{:T(128)}) %tuple.466), condition=%wide.region_19.20_spmd.clone, body=%wide.region_18.19_spmd.clone.sunk | while | flops 8771 | bytes 40045 | solution.py:53
  1624.9 0.8 gather_fusion.7
  1626.4 0.8 scatter.70
  1627.2 1.1 scatter.71
  1628.3 1.1 scatter.74
  1629.5 2.3 slice_bitcast_fusion
  1634.8 1.0 convolution_subtract_fusion.9
  1636.4 1.2 convolution_subtract_fusion.13
  1638.2 1.6 convolution_subtract_fusion.8
  1640.4 1.6 convolution_subtract_fusion.7
  1642.5 1.9 convolution_subtract_fusion.6
  1649.3 1.0 convolution_subtract_fusion.3
  1650.9 1.2 convolution_subtract_fusion.12
  1652.8 1.6 convolution_subtract_fusion.2
  1655.3 1.8 convolution_subtract_fusion.1
  1657.9 2.1 convolution_subtract_fusion
  1659.9 0.8 convolution_dynamic-update-slice_fusion
  1661.7 6.2 fusion.16
  1668.0 1.2 copy.37
  1669.8 1.8 constant_dynamic-slice_fusion
  (3246 shorter events, 417.7 us)
Async XLA Ops:
  7.2 90.4 %all-reduce.4.cloned.1.call-start = ((), (), s32[]{:S(2)}) async-start(), calls=%async_computation | async-start | bytes 9437184 | tf_op jit(solution)/shard_map/psum | solution.py:135
  21.1 491.5 %all-gather.3.cloned.1.call-start = ((), (), s32[]{:S(2)}) async-start(), calls=%async_computation.2 | async-start | bytes 80216064 | tf_op jit(solution)/shard_map/all_gather | solution.py:11
  97.6 719.0 %all-reduce.6.cloned.1.call-start = ((), (), s32[]{:S(2)}) async-start(), calls=%async_computation.1 | async-start | bytes 9437184 | tf_op jit(solution)/shard_map/psum | solution.py:22
  601.4 1.2 copy-start.1
  921.8 104.9 %copy-start.4 = (f32[64,64]{1,0:T(8,128)}, f32[64,64]{1,0:T(8,128)S(1)}, u32[]{:S(2)}) copy-start(f32[64,64]{1,0:T(8,128)S(1)} %fusion.47) | copy-start | bytes 49156
  1030.7 1.0 copy-start.2
  1629.5 2.3 copy-start.5
  1631.8 1.3 copy-start.3
  1646.4 3.9 copy-start.6
  1660.8 1.0 copy-start
Sparse Core Ops, SparseCore 0:
  21.2 76.3 all-reduce.3
  99.7 412.8 all-gather.2
  601.5 214.9 all-reduce.5
where the time goes:
time: 1690 us; the launch traced here: 1680 us
  waiting for transfers between devices  705 us (42%)
  local copies, waits for them, and re-layouts  443 us (26%)
  loops' own time  381 us (23%)
  other arithmetic  72.8 us (4%)
  matrix products  61.3 us (4%)
    all_gather x1, waiting for transfers between devices, prefix(): gathered = lax.all_gather(part, axis)  415 us
    another operation x8, loops' own time, factor_block(): return lax.fori_loop(0, size, column_step, start)[1]  380 us
    dynamic_slice x512, local copies, waits for them, and re-layouts, column_step(): pivot = lax.dynamic_slice_in_dim(column, step, 1, 0)[0]  316 us
    psum x1, waiting for transfers between devices, broadcast(): return lax.psum(block, axis)  214 us
    while x2, local copies, waits for them, and re-layouts, prefix(): return lax.fori_loop(0, place, one, state)  79.1 us
    psum x1, waiting for transfers between devices, local(): summed = lax.psum(jnp.concatenate([gram_local, cross_local], 0), 'dev')  76.4 us
    dot_general x124, matrix products, matmul(): jnp.dot(left, right, precision=lax.Precision.HIGHEST, preferred_element_t...  46.7 us
    sub x512, other arithmetic, column_step(): work = work - scaled[:, None] * scaled[None, :]  38.8 us
  transfers between devices with their start and end apart: 3, of which 3 were waited for; matrix products, arithmetic and copies ran while one was open for 0% of the time, Pallas kernels for 0%

commit v1 on v0

v1 whole, which is shorter than its diff:
```python
import jax
import jax.numpy as jnp
from jax import lax
from jax.experimental import pallas as pl
from jax.experimental.pallas import tpu as pltpu
from jax.sharding import Mesh, PartitionSpec as P

ridge_shift = 0.05
HIGHEST = lax.Precision.HIGHEST
tile = 128
chips = ("grp", "z")


def product(left, right, left_dim=1, right_dim=0):
    return lax.dot_general(
        left,
        right,
        (((left_dim,), (right_dim,)), ((), ())),
        precision=HIGHEST,
        preferred_element_type=jnp.float32,
    )


def factor_diagonal(work):
    sub = lax.broadcasted_iota(jnp.int32, (8, tile), 0)
    for r in range(0, tile, 8):
        left = work[r : r + 8, 0:tile]
        right = work[r : r + 8, tile : 2 * tile]
        a = {}
        for k in range(8):
            for j in range(k, 8):
                a[j, k] = jnp.broadcast_to(left[k : k + 1, r + j : r + j + 1], (8, tile))
        low, inv = {}, {}
        for k in range(8):
            inv[k] = lax.rsqrt(a[k, k])
            for j in range(k + 1, 8):
                low[j, k] = a[j, k] * inv[k]
            for j in range(k + 1, 8):
                for i in range(k + 1, j + 1):
                    a[j, i] = a[j, i] - low[j, k] * low[i, k]
        t = {}
        new_left = jnp.zeros((8, tile), jnp.float32)
        new_right = jnp.zeros((8, tile), jnp.float32)
        for k in range(8):
            t[k, k] = inv[k]
            column = jnp.where(sub == k, inv[k], 0.0)
            for j in range(k + 1, 8):
                total = low[j, k] * t[k, k]
                for i in range(k + 1, j):
                    total = total + low[j, i] * t[i, k]
                t[j, k] = -inv[j] * total
                column = jnp.where(sub == j, t[j, k], column)
            new_left = new_left + column * left[k : k + 1, :]
            new_right = new_right + column * right[k : k + 1, :]
        work[r : r + 8, 0:tile] = new_left
        work[r : r + 8, tile : 2 * tile] = new_right
        if r + 8 < tile:
            update = product(new_left, jnp.concatenate([new_left, new_right], 1), 0, 0)
            work[r + 8 : tile, :] = work[r + 8 : tile, :] - update[r + 8 : tile, :]


def factor_kernel(start_ref, gram_ref, panel_ref, upper_ref, mixed_ref, a_ref, work, tinv, rows_ref):
    rows = lax.broadcasted_iota(jnp.int32, (tile, tile), 0)
    cols = lax.broadcasted_iota(jnp.int32, (tile, tile), 1)
    eye = jnp.where(rows == cols, 1.0, 0.0).astype(jnp.float32)
    width = gram_ref.shape[0]
    own = panel_ref.shape[0]
    picked = mixed_ref.shape[0] - own
    levels = width // tile
    a_ref[...] = gram_ref[...]
    upper_ref[...] = jnp.zeros_like(upper_ref)
    rows_ref[0:own, :] = panel_ref[...]
    unit_row = lax.broadcasted_iota(jnp.int32, (picked, width), 0) + start_ref[0]
    unit_col = lax.broadcasted_iota(jnp.int32, (picked, width), 1)
    rows_ref[own:, :] = jnp.where(unit_row == unit_col, 1.0, 0.0).astype(jnp.float32)

    def load(b):
        work[:, 0:tile] = a_ref[b : b + tile, b : b + tile] + ridge_shift * eye
        work[:, tile:] = eye

    def spread(b):
        e = b + tile
        inverse = work[:, tile:]
        tinv[b:e, :] = inverse
        upper_ref[b:e, b:e] = jnp.where(cols >= rows, work[:, 0:tile], 0.0)
        y = product(rows_ref[0:own, b:e], inverse, 1, 1)
        rows_ref[0:own, b:e] = y
        if e < width:
            u = product(inverse, a_ref[b:e, e:])
            upper_ref[b:e, e:] = u
            for c in range(e, width, tile):
                a_ref[c : c + tile, c:] = a_ref[c : c + tile, c:] - product(
                    u[:, c - e : c - e + tile], u[:, c - e :], 0, 0
                )
            rows_ref[0:own, e:] = rows_ref[0:own, e:] - product(y, u)

    def level(step, carry):
        for i in range(levels):
            pl.when(step == i)(lambda i=i: load(i * tile))
        factor_diagonal(work)
        for i in range(levels):
            pl.when(step == i)(lambda i=i: spread(i * tile))
        return carry

    lax.fori_loop(0, levels, level, 0)
    for b in range(width - tile, -1, -tile):
        e = b + tile
        right = rows_ref[:, b:e]
        if e < width:
            right = right - product(mixed_ref[:, e:], upper_ref[b:e, e:], 1, 1)
        mixed_ref[:, b:e] = product(right, tinv[b:e, :])


def factor(start, gram, panel, picked):
    width = gram.shape[0]
    own = panel.shape[0]
    vmem = pl.BlockSpec(memory_space=pltpu.VMEM)
    return pl.pallas_call(
        factor_kernel,
        out_shape=(
            jax.ShapeDtypeStruct((width, width), jnp.float32),
            jax.ShapeDtypeStruct((own + picked, width), jnp.float32),
        ),
        in_specs=[pl.BlockSpec(memory_space=pltpu.SMEM), vmem, vmem],
        out_specs=(vmem, vmem),
        scratch_shapes=[
            pltpu.VMEM((width, width), jnp.float32),
            pltpu.VMEM((tile, 2 * tile), jnp.float32),
            pltpu.VMEM((width, tile), jnp.float32),
            pltpu.VMEM((own + picked, width), jnp.float32),
        ],
        compiler_params=pltpu.CompilerParams(vmem_limit_bytes=24 * 1024 * 1024),
        cost_estimate=pl.CostEstimate(flops=10**9, bytes_accessed=4 * 10**6, transcendentals=0),
    )(start, gram, panel)


def products_kernel(core_ref, panel_ref, other_ref, trail_ref, far_ref, w_ref, wo_ref, out_ref):
    core = core_ref[0]
    half = panel_ref.shape[1] // 2
    trail_half = trail_ref.shape[1]

    def add(panel, weight, trail):
        near = jnp.where(core == 0, panel[:, :half], panel[:, half:])
        a = product(panel, trail * weight, 0, 0)
        b = product(panel, near * weight, 0, 0)
        return a, b

    a0, b0 = add(panel_ref[...], w_ref[...], trail_ref[...])
    a1, b1 = add(other_ref[...], wo_ref[...], far_ref[...])
    out_ref[:, :trail_half] = a0 + a1
    out_ref[:, trail_half:] = b0 + b1


def products(core, panel, other, trail, far, weights, other_weights):
    vmem = pl.BlockSpec(memory_space=pltpu.VMEM)
    width = panel.shape[1]
    return pl.pallas_call(
        products_kernel,
        out_shape=jax.ShapeDtypeStruct((width, trail.shape[1] + width // 2), jnp.float32),
        in_specs=[pl.BlockSpec(memory_space=pltpu.SMEM)] + [vmem] * 6,
        out_specs=vmem,
        compiler_params=pltpu.CompilerParams(vmem_limit_bytes=32 * 1024 * 1024),
    )(core, panel, other, trail, far, weights, other_weights)


def finish_kernel(core_ref, mixed_ref, near_ref, far_ref, trail_ref, updated_ref, coupling_ref):
    own = trail_ref.shape[0]
    half = near_ref.shape[1]

    def side(place, cross_ref):
        for c in range(0, half, tile):
            out = product(mixed_ref[...], cross_ref[:, c : c + tile])
            at = pl.ds(place * half + c, tile)
            updated_ref[:, at] = trail_ref[:, at] - out[:own]
            coupling_ref[:, at] = out[own:]

    for place in range(2):
        for ref, match in ((near_ref, core_ref[0] == place), (far_ref, core_ref[0] != place)):
            pl.when(match)(lambda place=place, ref=ref: side(place, ref))


def finish(core, mixed, near, far, trailing):
    vmem = pl.BlockSpec(memory_space=pltpu.VMEM)
    own, trail = trailing.shape
    return pl.pallas_call(
        finish_kernel,
        out_shape=(
            jax.ShapeDtypeStruct((own, trail), jnp.float32),
            jax.ShapeDtypeStruct((mixed.shape[0] - own, trail), jnp.float32),
        ),
        in_specs=[pl.BlockSpec(memory_space=pltpu.SMEM)] + [vmem] * 4,
        out_specs=(vmem, vmem),
        compiler_params=pltpu.CompilerParams(vmem_limit_bytes=32 * 1024 * 1024),
    )(core, mixed, near, far, trailing)


def local(panel, trailing, counts):
    width = panel.shape[1]
    half = trailing.shape[1] // 2
    members = lax.axis_size("z") * lax.axis_size("core")
    groups = lax.axis_size("grp")
    chip_count = groups * lax.axis_size("z")
    core = lax.axis_index("core")
    core_one = core.astype(jnp.int32)[None]
    swap = [(0, 1), (1, 0)]
    weights = (counts.astype(jnp.float32) / (panel.shape[0] * groups * members))[:, None]
    near_trail = lax.dynamic_slice_in_dim(trailing, core * half, half, 1)
    sent_trail = lax.dynamic_slice_in_dim(trailing, (1 - core) * half, half, 1)
    with jax.named_scope("swap_inputs"):
        other_panel = lax.ppermute(panel, "core", swap)
        far_trail = lax.ppermute(sent_trail, "core", swap)
        other_weights = lax.ppermute(weights, "core", swap)
    with jax.named_scope("local_products"):
        terms = products(core_one, panel, other_panel, near_trail, far_trail, weights, other_weights)
    piece = width // chip_count
    with jax.named_scope("scatter_sum"):
        pieces = lax.all_to_all(terms.reshape(chip_count, piece, -1), chips, 0, 0, tiled=True)
        mine = jnp.sum(pieces, 0, keepdims=True)
    with jax.named_scope("gather_sums"):
        copies = jnp.broadcast_to(mine, (chip_count,) + mine.shape[1:])
        sums = lax.all_to_all(copies, chips, 0, 0, tiled=True).reshape(width, -1)
    near_cross = sums[:, :half]
    near_gram = sums[:, half:]
    with jax.named_scope("swap_gram"):
        far_gram = lax.ppermute(near_gram, "core", swap)
    with jax.named_scope("swap_cross"):
        far_cross = lax.ppermute(near_cross, "core", swap)
    first = core == 0
    gram = jnp.concatenate(
        [jnp.where(first, near_gram, far_gram), jnp.where(first, far_gram, near_gram)], 1
    )
    picked = width // members
    start = (lax.axis_index("z") * lax.axis_size("core") + core) * picked
    with jax.named_scope("factor_gram"):
        upper, mixed = factor(start.astype(jnp.int32)[None], gram, panel, picked)
    with jax.named_scope("apply_factor"):
        updated, coupling = finish(core_one, mixed, near_cross, far_cross, trailing)
    r_rows = lax.dynamic_slice_in_dim(upper, start, picked, 0)
    return (r_rows, coupling, updated)


def solution(mesh):
    groups, members = mesh.devices.shape
    split = Mesh(mesh.devices.reshape(groups, members // 2, 2), ("grp", "z", "core"))
    rows = P(("grp", "z", "core"))
    return jax.shard_map(
        local,
        mesh=split,
        in_specs=(P(("grp", "z", "core"), None), P(("grp", "z", "core"), None), rows),
        out_specs=(P(("z", "core"), None), P(("z", "core"), None), P(("grp", "z", "core"), None)),
        check_vma=False,
    )
```

time: 1690 us -> 148 us (0.09)
  waiting for transfers between devices: 705 us -> 3.87 us
  local copies, waits for them, and re-layouts: 443 us -> 3.29 us
  loops' own time: 381 us -> 0 us
  blocking collectives: 0 us -> 79.8 us
  other arithmetic: 72.8 us -> 2.06 us
  matrix products: 61.3 us -> 0 us
  Pallas kernels: 0 us -> 52.2 us
    all_gather x1 -> x0, waiting for transfers between devices: 415 us -> none  [prefix(): gathered = lax.all_gather(part, axis)]
    another operation x9 -> x0, loops' own time: 381 us -> none  [the longest x8 380 us: factor_block(): return lax.fori_loop(0, size, column_step, start)[1]]
    dynamic_slice x514 -> x2, local copies, waits for them, and re-layouts: 319 us -> 1.9 us  [the longest x1 1.22 us: local(): sent_trail = lax.dynamic_slice_in_dim(trailing, (1 - core) * half, half, 1)]
    psum x2 -> x0, waiting for transfers between devices: 290 us -> none  [the longest x1 214 us: broadcast(): return lax.psum(block, axis)]
    all_to_all x0 -> x2, blocking collectives: none -> 79.8 us  [the longest x1 43.4 us: local(): lax.all_to_all(terms.reshape(chip_count, piece, -1), chips, 0, 0, tiled=T...]
    while x10 -> x0, local copies, waits for them, and re-layouts: 79.7 us -> none  [the longest x2 79.1 us: prefix(): return lax.fori_loop(0, place, one, state)]
    dot_general x127 -> x0, matrix products: 61.3 us -> none  [the longest x124 46.7 us: matmul(): jnp.dot(left, right, precision=lax.Precision.HIGHEST, preferred_element_t...]
    pallas_call x0 -> x3, Pallas kernels: none -> 52.2 us  [the longest x1 41.1 us: factor(): pl.pallas_call(factor_kernel, out_shape=(jax.ShapeDtypeStruct((width, wid...]
  transfers between devices with their start and end apart: 3 -> 5, of which waited for: 3 -> 2; matrix products, arithmetic and copies ran while one was open for 0% -> 2% of each run, Pallas kernels for 0% -> 28%
where the time goes in v1:
time: 148 us
  blocking collectives  79.8 us (54%)
  Pallas kernels  52.2 us (35%)
  starting transfers between devices  5.94 us (4%)
  waiting for transfers between devices  3.87 us (3%)
  local copies, waits for them, and re-layouts  3.29 us (2%)
  other arithmetic  2.06 us (1%)
    all_to_all x1, blocking collectives, local(): lax.all_to_all(terms.reshape(chip_count, piece, -1), chips, 0, 0, tiled=T...  43.4 us
    pallas_call x1, Pallas kernels, factor(): pl.pallas_call(factor_kernel, out_shape=(jax.ShapeDtypeStruct((width, wid...  41.1 us
    all_to_all x1, blocking collectives, local(): sums = lax.all_to_all(copies, chips, 0, 0, tiled=True).reshape(width, -1)  36.4 us
    pallas_call x1, Pallas kernels, finish(): pl.pallas_call(finish_kernel, out_shape=(jax.ShapeDtypeStruct((own, trail...  7.23 us
    pallas_call x1, Pallas kernels, products(): pl.pallas_call(products_kernel, out_shape=jax.ShapeDtypeStruct((width, tr...  3.93 us
  transfers between devices with their start and end apart: 5, of which 2 were waited for; matrix products, arithmetic and copies ran while one was open for 2% of the time, Pallas kernels for 28%

profile of v1, /device:TPU:1, one launch (start us, length us, event | category | flops | bytes accessed | tf_op | source)
XLA Modules:
  0.0 147.9 jit_solution(18207391500430962545)
XLA Ops:
  0.6 1.2 constant_dynamic-slice_fusion.1
  1.9 1.5 %collective-permute-start.1 = (f32[128,896]{1,0:T(8,128)S(1)}, f32[128,896]{1,0:T(8,128)S(1)}, u32[]{:S(2)}, u32[]{:S(2)}) collective-permute-start(f32[128,896]{1,0:T(8,128)S(1)} %get-tuple-element.13), channel_id=1, source_target_pairs={{0,1},{1,0},{2,3},{3,2},{4,5},{5,4},{6,7},{7,6},{8,9},{9,8},{10,11... | collective-permute-start | bytes 1376264 | tf_op jit(solution)/shard_map/swap_inputs/ppermute | solution.py:211
  3.4 0.1 collective-permute-start
  3.5 0.7 multiply_bitcast_fusion
  4.1 0.1 copy.7.w_ref
  4.2 0.5 collective-permute-start.2
  4.7 0.9 collective-permute-done.2.wo_ref
  5.6 0.0 collective-permute-done.other_ref
  5.6 0.0 collective-permute-done.1.far_ref
  5.6 0.0 copy-start.1
  5.6 0.9 copy-done.1
  6.6 3.9 %local_products.1 = f32[512,1152]{1,0:T(8,128)S(1)} custom-call(s32[1]{0:T(128)} %bitcast.1.core_ref, f32[128,512]{1,0:T(8,128)S(1)} %copy-done.1, f32[128,512]{1,0:T(8,128)S(1)} %collective-permute-done.other_ref, f32[128,896]{1,0:T(8,128)S(1)} %get-tuple-element.14.trail_ref, f32[128,896]{1,0:T(8,128)S(1)} %collective-permute-done.1.far_ref, ...), custom_call_target="tpu_custom_call" | custom-call | tf_op jit(solution)/shard_map/local_products/pallas_call | solution.py:157
  10.5 43.4 %all_to_all.10 = f32[64,8,1152]{2,1,0:T(8,128)S(1)} all-to-all(f32[64,8,1152]{2,1,0:T(8,128)S(1)} %bitcast.6), channel_id=1, replica_groups=mesh['grp'=16,'z'=4,'core'=2] {'grp','z'}, dimensions={0} | all-to-all | bytes 4718592 | tf_op jit(solution)/shard_map/scatter_sum/all_to_all | solution.py:217
  53.9 0.1 reduce_sum.9
  54.1 0.2 broadcast_in_dim.18
  54.2 36.4 %all_to_all.11 = f32[64,8,1152]{2,1,0:T(8,128)S(1)} all-to-all(f32[64,8,1152]{2,1,0:T(8,128)S(1)} %broadcast_in_dim.18), channel_id=1, replica_groups=mesh['grp'=16,'z'=4,'core'=2] {'grp','z'}, dimensions={0} | all-to-all | bytes 4718592 | tf_op jit(solution)/shard_map/gather_sums/all_to_all | solution.py:221
  90.7 0.0 copy-start.3
  90.7 0.1 slice.9.near_ref
  90.8 2.7 %collective-permute-start.4 = (f32[512,896]{1,0:T(8,128)S(1)}, f32[512,896]{1,0:T(8,128)}, u32[]{:S(2)}, u32[]{:S(2)}) collective-permute-start(f32[512,896]{1,0:T(8,128)S(1)} %slice.9.near_ref), channel_id=1, source_target_pairs={{0,1},{1,0},{2,3},{3,2},{4,5},{5,4},{6,7},{7,6},{8,9},{9,8},{10,11... | collective-permute-start | bytes 5505032 | tf_op jit(solution)/shard_map/swap_cross/ppermute | solution.py:227
  93.5 0.0 copy-done.3
  93.6 0.0 copy-start.2
  93.6 1.1 collective-permute-start.3
  94.7 3.0 %collective-permute-done.3 = f32[512,256]{1,0:T(8,128)S(1)} collective-permute-done((f32[512,256]{1,0:T(8,128)S(1)}, f32[512,256]{1,0:T(8,128)S(1)}, u32[]{:S(2)}, u32[]{:S(2)}) %collective-permute-start.3) | collective-permute-done | bytes 524320 | tf_op jit(solution)/shard_map/swap_gram/ppermute | solution.py:225
  97.7 1.1 broadcast_select_fusion.1
  98.8 0.1 pad_maximum_fusion.gram_ref
  98.9 0.0 copy-start
  98.9 0.0 copy-done.2
  99.0 41.1 %factor_gram.1 = (f32[512,512]{1,0:T(8,128)S(1)}, f32[192,512]{1,0:T(8,128)S(1)}) custom-call(s32[1]{0:T(128)} %bitcast.start_ref, f32[512,512]{1,0:T(8,128)S(1)} %pad_maximum_fusion.gram_ref, f32[128,512]{1,0:T(8,128)S(1)} %copy-done.2), custom_call_target="tpu_custom_call" | custom-call | flops 1000000000 | bytes 4000000 | tf_op jit(solution)/shard_map/factor_gram/pallas_call | solution.py:118
  140.0 0.7 constant_dynamic-slice_fusion
  140.7 0.0 collective-permute-done.4.far_ref
  140.7 0.0 copy-done
  140.7 7.2 %apply_factor.1 = (f32[128,1792]{1,0:T(8,128)}, f32[64,1792]{1,0:T(8,128)}) custom-call(s32[1]{0:T(128)} %bitcast.1.core_ref, f32[192,512]{1,0:T(8,128)S(1)} %get-tuple-element.8.mixed_ref, f32[512,896]{1,0:T(8,128)S(1)} %slice.9.near_ref, f32[512,896]{1,0:T(8,128)} %collective-permute-done.4.far_ref, f32[128,1792]{1,0:T(8,128)S(1)} %copy-done), custom_call_target="tpu_custom_call" | custom-call | tf_op jit(solution)/shard_map/apply_factor/pallas_call | solution.py:185
  (1 shorter events, 0.0 us)
Async XLA Ops:
  1.9 3.8 %collective-permute-start.1 = (f32[128,896]{1,0:T(8,128)S(1)}, f32[128,896]{1,0:T(8,128)S(1)}, u32[]{:S(2)}, u32[]{:S(2)}) collective-permute-start(f32[128,896]{1,0:T(8,128)S(1)} %get-tuple-element.13), channel_id=1, source_target_pairs={{0,1},{1,0},{2,3},{3,2},{4,5},{5,4},{6,7},{7,6},{8,9},{9,8},{10,11... | collective-permute-start | bytes 1376264 | tf_op jit(solution)/shard_map/swap_inputs/ppermute | solution.py:211
  3.4 2.3 %collective-permute-start = (f32[128,512]{1,0:T(8,128)}, f32[128,512]{1,0:T(8,128)S(1)}, u32[]{:S(2)}, u32[]{:S(2)}) collective-permute-start(f32[128,512]{1,0:T(8,128)} %panel_ref.3), channel_id=1, source_target_pairs={{0,1},{1,0},{2,3},{3,2},{4,5},{5,4},{6,7},{7,6},{8,9},{9,8},{10,11... | collective-permute-start | bytes 786440 | tf_op jit(solution)/shard_map/swap_inputs/ppermute | solution.py:210
  4.2 1.4 collective-permute-start.2
  5.6 1.0 copy-start.1
  90.7 2.9 %copy-start.3 = (f32[64,8,1152]{2,1,0:T(8,128)}, f32[64,8,1152]{2,1,0:T(8,128)S(1)}, u32[]{:S(2)}) copy-start(f32[64,8,1152]{2,1,0:T(8,128)S(1)} %all_to_all.11) | copy-start | bytes 7077892
  90.8 49.9 %collective-permute-start.4 = (f32[512,896]{1,0:T(8,128)S(1)}, f32[512,896]{1,0:T(8,128)}, u32[]{:S(2)}, u32[]{:S(2)}) collective-permute-start(f32[512,896]{1,0:T(8,128)S(1)} %slice.9.near_ref), channel_id=1, source_target_pairs={{0,1},{1,0},{2,3},{3,2},{4,5},{5,4},{6,7},{7,6},{8,9},{9,8},{10,11... | collective-permute-start | bytes 5505032 | tf_op jit(solution)/shard_map/swap_cross/ppermute | solution.py:227
  93.6 5.4 %copy-start.2 = (f32[128,512]{1,0:T(8,128)S(1)}, f32[128,512]{1,0:T(8,128)}, u32[]{:S(2)}) copy-start(f32[128,512]{1,0:T(8,128)} %panel_ref.3) | copy-start | bytes 786436
  93.6 4.1 %collective-permute-start.3 = (f32[512,256]{1,0:T(8,128)S(1)}, f32[512,256]{1,0:T(8,128)S(1)}, u32[]{:S(2)}, u32[]{:S(2)}) collective-permute-start(f32[512,256]{1,0:T(8,128)S(1)} %slice.8), channel_id=1, source_target_pairs={{0,1},{1,0},{2,3},{3,2},{4,5},{5,4},{6,7},{7,6},{8,9},{9,8},{10,11... | collective-permute-start | bytes 1572872 | tf_op jit(solution)/shard_map/swap_gram/ppermute | solution.py:225
  98.9 41.8 %copy-start = (f32[128,1792]{1,0:T(8,128)S(1)}, f32[128,1792]{1,0:T(8,128)}, u32[]{:S(2)}) copy-start(f32[128,1792]{1,0:T(8,128)} %trail_ref.1) | copy-start | bytes 2752516

commit v2 on v1

--- a/solution.py
+++ b/solution.py
@@ -8,6 +8,7 @@
 ridge_shift = 0.05
 HIGHEST = lax.Precision.HIGHEST
 tile = 128
+strip = 32
 chips = ("grp", "z")
 
 
@@ -23,40 +24,39 @@
 
 def factor_diagonal(work):
     sub = lax.broadcasted_iota(jnp.int32, (8, tile), 0)
-    for r in range(0, tile, 8):
-        left = work[r : r + 8, 0:tile]
-        right = work[r : r + 8, tile : 2 * tile]
-        a = {}
-        for k in range(8):
-            for j in range(k, 8):
-                a[j, k] = jnp.broadcast_to(left[k : k + 1, r + j : r + j + 1], (8, tile))
-        low, inv = {}, {}
-        for k in range(8):
-            inv[k] = lax.rsqrt(a[k, k])
-            for j in range(k + 1, 8):
-                low[j, k] = a[j, k] * inv[k]
-            for j in range(k + 1, 8):
-                for i in range(k + 1, j + 1):
-                    a[j, i] = a[j, i] - low[j, k] * low[i, k]
-        t = {}
-        new_left = jnp.zeros((8, tile), jnp.float32)
-        new_right = jnp.zeros((8, tile), jnp.float32)
-        for k in range(8):
-            t[k, k] = inv[k]
-            column = jnp.where(sub == k, inv[k], 0.0)
-            for j in range(k + 1, 8):
-                total = low[j, k] * t[k, k]
-                for i in range(k + 1, j):
-                    total = total + low[j, i] * t[i, k]
-                t[j, k] = -inv[j] * total
-                column = jnp.where(sub == j, t[j, k], column)
-            new_left = new_left + column * left[k : k + 1, :]
-            new_right = new_right + column * right[k : k + 1, :]
-        work[r : r + 8, 0:tile] = new_left
-        work[r : r + 8, tile : 2 * tile] = new_right
-        if r + 8 < tile:
+    groups = strip // 8
+
+    def spread_row(array, row):
+        return jnp.broadcast_to(array[row : row + 1, :], (8, tile))
+
+    for r in range(0, tile, strip):
+        left = [work[r + 8 * g : r + 8 * g + 8, 0:tile] for g in range(groups)]
+        right = [work[r + 8 * g : r + 8 * g + 8, tile : 2 * tile] for g in range(groups)]
+        col = {}
+        for c in range(strip):
+            for g in range(c // 8, groups):
+                col[c, g] = jnp.broadcast_to(left[g][:, r + c : r + c + 1], (8, tile))
+        for k in range(strip):
+            at, row = k // 8, k % 8
+            inv = lax.rsqrt(spread_row(col[k, at], row))
+            low = {g: col[k, g] * inv for g in range(at, groups)}
+            for c in range(k + 1, strip):
+                factor_c = spread_row(low[c // 8], c % 8)
+                for g in range(c // 8, groups):
+                    col[c, g] = col[c, g] - low[g] * factor_c
+            below = jnp.where(sub > row, low[at], 0.0)
+            for side in (left, right):
+                pivot = spread_row(side[at], row) * inv
+                side[at] = jnp.where(sub == row, pivot, side[at] - below * pivot)
+                for g in range(at + 1, groups):
+                    side[g] = side[g] - low[g] * pivot
+        new_left = jnp.concatenate(left, 0)
+        new_right = jnp.concatenate(right, 0)
+        work[r : r + strip, 0:tile] = new_left
+        work[r : r + strip, tile : 2 * tile] = new_right
+        if r + strip < tile:
             update = product(new_left, jnp.concatenate([new_left, new_right], 1), 0, 0)
-            work[r + 8 : tile, :] = work[r + 8 : tile, :] - update[r + 8 : tile, :]
+            work[r + strip : tile, :] = work[r + strip : tile, :] - update[r + strip : tile, :]
 
 
 def factor_kernel(start_ref, gram_ref, panel_ref, upper_ref, mixed_ref, a_ref, work, tinv, rows_ref):

time: 148 us -> 126 us (0.85)
  Pallas kernels: 52.2 us -> 29.9 us
    pallas_call x1, Pallas kernels: 41.1 us -> 18.5 us  [factor(): pl.pallas_call(factor_kernel, out_shape=(jax.ShapeDtypeStruct((width, wid...]
  transfers between devices with their start and end apart: 5 -> 5, of which waited for: 2 -> 2; matrix products, arithmetic and copies ran while one was open for 2% -> 2% of each run, Pallas kernels for 28% -> 15%
where the time goes in v2:
time: 126 us
  blocking collectives  79.8 us (63%)
  Pallas kernels  29.9 us (24%)
  starting transfers between devices  5.94 us (5%)
  waiting for transfers between devices  3.87 us (3%)
  local copies, waits for them, and re-layouts  3.29 us (3%)
  other arithmetic  2.06 us (2%)
    all_to_all x1, blocking collectives, local(): lax.all_to_all(terms.reshape(chip_count, piece, -1), chips, 0, 0, tiled=T...  43.4 us
    all_to_all x1, blocking collectives, local(): sums = lax.all_to_all(copies, chips, 0, 0, tiled=True).reshape(width, -1)  36.4 us
    pallas_call x1, Pallas kernels, factor(): pl.pallas_call(factor_kernel, out_shape=(jax.ShapeDtypeStruct((width, wid...  18.5 us
    pallas_call x1, Pallas kernels, finish(): pl.pallas_call(finish_kernel, out_shape=(jax.ShapeDtypeStruct((own, trail...  7.44 us
    pallas_call x1, Pallas kernels, products(): pl.pallas_call(products_kernel, out_shape=jax.ShapeDtypeStruct((width, tr...  3.93 us
    ppermute x1, waiting for transfers between devices, local(): far_gram = lax.ppermute(near_gram, 'core', swap)  2.96 us
    ppermute x1, starting transfers between devices, local(): far_cross = lax.ppermute(near_cross, 'core', swap)  2.71 us
  transfers between devices with their start and end apart: 5, of which 2 were waited for; matrix products, arithmetic and copies ran while one was open for 2% of the time, Pallas kernels for 15%

profile of v2, /device:TPU:1, one launch (start us, length us, event | category | flops | bytes accessed | tf_op | source)
XLA Modules:
  0.0 125.6 jit_solution(15725330114651270660)
XLA Ops:
  0.6 1.2 constant_dynamic-slice_fusion.1
  1.9 1.5 %collective-permute-start.1 = (f32[128,896]{1,0:T(8,128)S(1)}, f32[128,896]{1,0:T(8,128)S(1)}, u32[]{:S(2)}, u32[]{:S(2)}) collective-permute-start(f32[128,896]{1,0:T(8,128)S(1)} %get-tuple-element.13), channel_id=1, source_target_pairs={{0,1},{1,0},{2,3},{3,2},{4,5},{5,4},{6,7},{7,6},{8,9},{9,8},{10,11... | collective-permute-start | bytes 1376264 | tf_op jit(solution)/shard_map/swap_inputs/ppermute | solution.py:211
  3.4 0.1 collective-permute-start
  3.5 0.7 multiply_bitcast_fusion
  4.1 0.1 copy.7.w_ref
  4.2 0.5 collective-permute-start.2
  4.7 0.9 collective-permute-done.2.wo_ref
  5.6 0.0 collective-permute-done.other_ref
  5.6 0.0 collective-permute-done.1.far_ref
  5.6 0.0 copy-start.1
  5.6 0.9 copy-done.1
  6.6 3.9 %local_products.1 = f32[512,1152]{1,0:T(8,128)S(1)} custom-call(s32[1]{0:T(128)} %bitcast.1.core_ref, f32[128,512]{1,0:T(8,128)S(1)} %copy-done.1, f32[128,512]{1,0:T(8,128)S(1)} %collective-permute-done.other_ref, f32[128,896]{1,0:T(8,128)S(1)} %get-tuple-element.14.trail_ref, f32[128,896]{1,0:T(8,128)S(1)} %collective-permute-done.1.far_ref, ...), custom_call_target="tpu_custom_call" | custom-call | tf_op jit(solution)/shard_map/local_products/pallas_call | solution.py:157
  10.5 43.4 %all_to_all.10 = f32[64,8,1152]{2,1,0:T(8,128)S(1)} all-to-all(f32[64,8,1152]{2,1,0:T(8,128)S(1)} %bitcast.6), channel_id=1, replica_groups=mesh['grp'=16,'z'=4,'core'=2] {'grp','z'}, dimensions={0} | all-to-all | bytes 4718592 | tf_op jit(solution)/shard_map/scatter_sum/all_to_all | solution.py:217
  53.9 0.1 reduce_sum.9
  54.1 0.2 broadcast_in_dim.18
  54.2 36.4 %all_to_all.11 = f32[64,8,1152]{2,1,0:T(8,128)S(1)} all-to-all(f32[64,8,1152]{2,1,0:T(8,128)S(1)} %broadcast_in_dim.18), channel_id=1, replica_groups=mesh['grp'=16,'z'=4,'core'=2] {'grp','z'}, dimensions={0} | all-to-all | bytes 4718592 | tf_op jit(solution)/shard_map/gather_sums/all_to_all | solution.py:221
  90.7 0.0 copy-start.3
  90.7 0.1 slice.9.near_ref
  90.8 2.7 %collective-permute-start.4 = (f32[512,896]{1,0:T(8,128)S(1)}, f32[512,896]{1,0:T(8,128)}, u32[]{:S(2)}, u32[]{:S(2)}) collective-permute-start(f32[512,896]{1,0:T(8,128)S(1)} %slice.9.near_ref), channel_id=1, source_target_pairs={{0,1},{1,0},{2,3},{3,2},{4,5},{5,4},{6,7},{7,6},{8,9},{9,8},{10,11... | collective-permute-start | bytes 5505032 | tf_op jit(solution)/shard_map/swap_cross/ppermute | solution.py:227
  93.5 0.0 copy-done.3
  93.6 0.0 copy-start.2
  93.6 1.1 collective-permute-start.3
  94.7 3.0 %collective-permute-done.3 = f32[512,256]{1,0:T(8,128)S(1)} collective-permute-done((f32[512,256]{1,0:T(8,128)S(1)}, f32[512,256]{1,0:T(8,128)S(1)}, u32[]{:S(2)}, u32[]{:S(2)}) %collective-permute-start.3) | collective-permute-done | bytes 524320 | tf_op jit(solution)/shard_map/swap_gram/ppermute | solution.py:225
  97.7 1.1 broadcast_select_fusion.1
  98.8 0.1 pad_maximum_fusion.gram_ref
  98.9 0.0 copy-start
  98.9 0.0 copy-done.2
  99.0 18.5 %factor_gram.1 = (f32[512,512]{1,0:T(8,128)S(1)}, f32[192,512]{1,0:T(8,128)S(1)}) custom-call(s32[1]{0:T(128)} %bitcast.start_ref, f32[512,512]{1,0:T(8,128)S(1)} %pad_maximum_fusion.gram_ref, f32[128,512]{1,0:T(8,128)S(1)} %copy-done.2), custom_call_target="tpu_custom_call" | custom-call | flops 1000000000 | bytes 4000000 | tf_op jit(solution)/shard_map/factor_gram/pallas_call | solution.py:118
  117.4 0.7 constant_dynamic-slice_fusion
  118.1 0.0 collective-permute-done.4.far_ref
  118.1 0.0 copy-done
  118.1 7.4 %apply_factor.1 = (f32[128,1792]{1,0:T(8,128)}, f32[64,1792]{1,0:T(8,128)}) custom-call(s32[1]{0:T(128)} %bitcast.1.core_ref, f32[192,512]{1,0:T(8,128)S(1)} %get-tuple-element.8.mixed_ref, f32[512,896]{1,0:T(8,128)S(1)} %slice.9.near_ref, f32[512,896]{1,0:T(8,128)} %collective-permute-done.4.far_ref, f32[128,1792]{1,0:T(8,128)S(1)} %copy-done), custom_call_target="tpu_custom_call" | custom-call | tf_op jit(solution)/shard_map/apply_factor/pallas_call | solution.py:185
  (1 shorter events, 0.0 us)
Async XLA Ops:
  1.9 3.8 %collective-permute-start.1 = (f32[128,896]{1,0:T(8,128)S(1)}, f32[128,896]{1,0:T(8,128)S(1)}, u32[]{:S(2)}, u32[]{:S(2)}) collective-permute-start(f32[128,896]{1,0:T(8,128)S(1)} %get-tuple-element.13), channel_id=1, source_target_pairs={{0,1},{1,0},{2,3},{3,2},{4,5},{5,4},{6,7},{7,6},{8,9},{9,8},{10,11... | collective-permute-start | bytes 1376264 | tf_op jit(solution)/shard_map/swap_inputs/ppermute | solution.py:211
  3.4 2.3 %collective-permute-start = (f32[128,512]{1,0:T(8,128)}, f32[128,512]{1,0:T(8,128)S(1)}, u32[]{:S(2)}, u32[]{:S(2)}) collective-permute-start(f32[128,512]{1,0:T(8,128)} %panel_ref.3), channel_id=1, source_target_pairs={{0,1},{1,0},{2,3},{3,2},{4,5},{5,4},{6,7},{7,6},{8,9},{9,8},{10,11... | collective-permute-start | bytes 786440 | tf_op jit(solution)/shard_map/swap_inputs/ppermute | solution.py:210
  4.2 1.4 %collective-permute-start.2 = (f32[128,1]{1,0:T(8,128)S(1)}, f32[128,1]{1,0:T(8,128)S(1)}, u32[]{:S(2)}, u32[]{:S(2)}) collective-permute-start(f32[128,1]{1,0:T(8,128)S(1)} %copy.7.w_ref), channel_id=1, source_target_pairs={{0,1},{1,0},{2,3},{3,2},{4,5},{5,4},{6,7},{7,6},{8,9},{9,8},{10,11... | collective-permute-start | bytes 1544 | tf_op jit(solution)/shard_map/swap_inputs/ppermute | solution.py:212
  5.6 1.0 copy-start.1
  90.7 2.9 %copy-start.3 = (f32[64,8,1152]{2,1,0:T(8,128)}, f32[64,8,1152]{2,1,0:T(8,128)S(1)}, u32[]{:S(2)}) copy-start(f32[64,8,1152]{2,1,0:T(8,128)S(1)} %all_to_all.11) | copy-start | bytes 7077892
  90.8 27.3 %collective-permute-start.4 = (f32[512,896]{1,0:T(8,128)S(1)}, f32[512,896]{1,0:T(8,128)}, u32[]{:S(2)}, u32[]{:S(2)}) collective-permute-start(f32[512,896]{1,0:T(8,128)S(1)} %slice.9.near_ref), channel_id=1, source_target_pairs={{0,1},{1,0},{2,3},{3,2},{4,5},{5,4},{6,7},{7,6},{8,9},{9,8},{10,11... | collective-permute-start | bytes 5505032 | tf_op jit(solution)/shard_map/swap_cross/ppermute | solution.py:227
  93.6 5.4 %copy-start.2 = (f32[128,512]{1,0:T(8,128)S(1)}, f32[128,512]{1,0:T(8,128)}, u32[]{:S(2)}) copy-start(f32[128,512]{1,0:T(8,128)} %panel_ref.3) | copy-start | bytes 786436
  93.6 4.1 %collective-permute-start.3 = (f32[512,256]{1,0:T(8,128)S(1)}, f32[512,256]{1,0:T(8,128)S(1)}, u32[]{:S(2)}, u32[]{:S(2)}) collective-permute-start(f32[512,256]{1,0:T(8,128)S(1)} %slice.8), channel_id=1, source_target_pairs={{0,1},{1,0},{2,3},{3,2},{4,5},{5,4},{6,7},{7,6},{8,9},{9,8},{10,11... | collective-permute-start | bytes 1572872 | tf_op jit(solution)/shard_map/swap_gram/ppermute | solution.py:225
  98.9 19.2 %copy-start = (f32[128,1792]{1,0:T(8,128)S(1)}, f32[128,1792]{1,0:T(8,128)}, u32[]{:S(2)}) copy-start(f32[128,1792]{1,0:T(8,128)} %trail_ref.1) | copy-start | bytes 2752516

commit v3 on v2

v3 whole, which is shorter than its diff:
```python
import functools

import jax
import jax.numpy as jnp
from jax import lax
from jax.experimental import pallas as pl
from jax.experimental.pallas import tpu as pltpu
from jax.sharding import Mesh, PartitionSpec as P

ridge_shift = 0.05
HIGHEST = lax.Precision.HIGHEST
tile = 128
strip = 32
chips = ("grp", "z")
classes = 4


def product(left, right, left_dim=1, right_dim=0):
    return lax.dot_general(
        left,
        right,
        (((left_dim,), (right_dim,)), ((), ())),
        precision=HIGHEST,
        preferred_element_type=jnp.float32,
    )


def factor_diagonal(work):
    sub = lax.broadcasted_iota(jnp.int32, (8, tile), 0)
    groups = strip // 8

    def spread_row(array, row):
        return jnp.broadcast_to(array[row : row + 1, :], (8, tile))

    for r in range(0, tile, strip):
        left = [work[r + 8 * g : r + 8 * g + 8, 0:tile] for g in range(groups)]
        right = [work[r + 8 * g : r + 8 * g + 8, tile : 2 * tile] for g in range(groups)]
        col = {}
        for c in range(strip):
            for g in range(c // 8, groups):
                col[c, g] = jnp.broadcast_to(left[g][:, r + c : r + c + 1], (8, tile))
        for k in range(strip):
            at, row = k // 8, k % 8
            inv = lax.rsqrt(spread_row(col[k, at], row))
            low = {g: col[k, g] * inv for g in range(at, groups)}
            for c in range(k + 1, strip):
                factor_c = spread_row(low[c // 8], c % 8)
                for g in range(c // 8, groups):
                    col[c, g] = col[c, g] - low[g] * factor_c
            below = jnp.where(sub > row, low[at], 0.0)
            for side in (left, right):
                pivot = spread_row(side[at], row) * inv
                side[at] = jnp.where(sub == row, pivot, side[at] - below * pivot)
                for g in range(at + 1, groups):
                    side[g] = side[g] - low[g] * pivot
        new_left = jnp.concatenate(left, 0)
        new_right = jnp.concatenate(right, 0)
        work[r : r + strip, 0:tile] = new_left
        work[r : r + strip, tile : 2 * tile] = new_right
        if r + strip < tile:
            update = product(new_left, jnp.concatenate([new_left, new_right], 1), 0, 0)
            work[r + strip : tile, :] = work[r + strip : tile, :] - update[r + strip : tile, :]


gram_blocks = (((0, 0), (1, 1), (0, 1), (0, 2), (0, 3)), ((2, 2), (3, 3), (2, 3), (1, 2), (1, 3)))


def products_kernel(core_ref, panel_ref, other_ref, trail_ref, far_ref, counts_ref, far_counts_ref, out_ref, pt, wp, wt, quarters, gram, *, chip_count, total_rows):
    core = core_ref[0]
    own, width = panel_ref.shape
    half = trail_ref.shape[1]
    for at, rows, trail, count in ((0, panel_ref, trail_ref, counts_ref), (own, other_ref, far_ref, far_counts_ref)):
        weight = jnp.transpose(jnp.broadcast_to(count[...].astype(jnp.float32) / total_rows, (own, own)))
        for c in range(0, width, tile):
            block = rows[:, c : c + tile]
            pt[c : c + tile, at : at + own] = jnp.transpose(block)
            wp[at : at + own, c : c + tile] = block * weight
        for c in range(0, half, tile):
            wt[at : at + own, c : c + tile] = trail[:, c : c + tile] * weight
    step = 2 * tile
    for c in range(0, half, step):
        n = min(step, half - c)
        part = product(pt[...], wt[:, c : c + n])
        for k in range(classes):
            for j in range(0, n, tile):
                quarters[k, c + j : c + j + tile, :] = part[k * tile : (k + 1) * tile, j : j + tile]
    near = pl.multiple_of(core * step, tile)
    first = product(pt[pl.ds(near, tile), :], wp[:, pl.ds(near, step)])
    gram[0:tile, :] = first[:, :tile]
    gram[2 * tile : 3 * tile, :] = first[:, tile:]
    near = pl.multiple_of(core * step + tile, tile)
    gram[tile : 2 * tile, :] = product(pt[pl.ds(near, tile), :], wp[:, pl.ds(near, tile)])
    near = pl.multiple_of(core * tile, tile)
    last = product(pt[pl.ds(near, tile), :], wp[:, step:])
    gram[3 * tile : 4 * tile, :] = last[:, :tile]
    gram[4 * tile :, :] = last[:, tile:]
    chunk = half // chip_count
    gram_chunk = gram.shape[0] // chip_count
    piece = classes * chunk + gram_chunk
    for q in range(chip_count):
        for k in range(classes):
            at = q * piece + k * chunk
            out_ref[at : at + chunk, :] = quarters[k, q * chunk : (q + 1) * chunk, :]
        at = q * piece + classes * chunk
        out_ref[at : at + gram_chunk, :] = gram[q * gram_chunk : (q + 1) * gram_chunk, :]


def products(core, panel, other, trailing, far, counts, far_counts, chip_count, total_rows):
    own, width = panel.shape
    half = far.shape[1]
    gram_rows = len(gram_blocks[0]) * tile
    whole = lambda shape: pl.BlockSpec(shape, lambda i, core: (0, 0))
    return pl.pallas_call(
        functools.partial(products_kernel, chip_count=chip_count, total_rows=total_rows),
        out_shape=jax.ShapeDtypeStruct((classes * half + gram_rows, tile), jnp.float32),
        grid_spec=pltpu.PrefetchScalarGridSpec(
            num_scalar_prefetch=1,
            grid=(1,),
            in_specs=[
                whole((own, width)),
                whole((own, width)),
                pl.BlockSpec((own, half), lambda i, core: (0, core[0])),
                whole((own, half)),
                whole((1, own)),
                whole((1, own)),
            ],
            out_specs=whole((classes * half + gram_rows, tile)),
            scratch_shapes=[
                pltpu.VMEM((width, 2 * own), jnp.float32),
                pltpu.VMEM((2 * own, width), jnp.float32),
                pltpu.VMEM((2 * own, half), jnp.float32),
                pltpu.VMEM((classes, half, tile), jnp.float32),
                pltpu.VMEM((gram_rows, tile), jnp.float32),
            ],
        ),
        compiler_params=pltpu.CompilerParams(vmem_limit_bytes=32 * 1024 * 1024),
    )(core, panel, other, trailing, far, counts, far_counts)


def sum_kernel(pieces_ref, copies_ref, four, *, chip_count, chunk, gram_chunk, kinds):
    piece = classes * chunk + gram_chunk
    size = 4 * piece
    total = pieces_ref[0:size, :]
    for at in range(size, chip_count * piece, size):
        total = total + pieces_ref[at : at + size, :]
    four[...] = total
    mine = four[0:piece, :]
    for at in range(piece, size, piece):
        mine = mine + four[at : at + piece, :]
    for k in range(classes):
        four[0:piece, :] = mine
        copy = jnp.concatenate(
            [four[k * chunk : (k + 1) * chunk, :], four[classes * chunk : piece, :]], 0
        )
        for chip, kind in enumerate(kinds):
            if kind == k:
                copies_ref[chip * (chunk + gram_chunk) : (chip + 1) * (chunk + gram_chunk), :] = copy


def sum_pieces(pieces, chip_count, chunk, gram_chunk, kinds):
    vmem = pl.BlockSpec(memory_space=pltpu.VMEM)
    return pl.pallas_call(
        functools.partial(
            sum_kernel, chip_count=chip_count, chunk=chunk, gram_chunk=gram_chunk, kinds=kinds
        ),
        out_shape=jax.ShapeDtypeStruct((chip_count * (chunk + gram_chunk), tile), jnp.float32),
        in_specs=[vmem],
        out_specs=vmem,
        scratch_shapes=[pltpu.VMEM((4 * (classes * chunk + gram_chunk), tile), jnp.float32)],
        compiler_params=pltpu.CompilerParams(vmem_limit_bytes=16 * 1024 * 1024),
    )(pieces)


def unpack_kernel(copies_ref, quarter_ref, gram_ref, *, chip_count, chunk, gram_chunk):
    both = chunk + gram_chunk
    for q in range(chip_count):
        quarter_ref[q * chunk : (q + 1) * chunk, :] = copies_ref[q * both : q * both + chunk, :]
        gram_ref[q * gram_chunk : (q + 1) * gram_chunk, :] = copies_ref[q * both + chunk : (q + 1) * both, :]


def unpack(copies, chip_count, chunk, gram_chunk):
    vmem = pl.BlockSpec(memory_space=pltpu.VMEM)
    return pl.pallas_call(
        functools.partial(unpack_kernel, chip_count=chip_count, chunk=chunk, gram_chunk=gram_chunk),
        out_shape=(
            jax.ShapeDtypeStruct((chip_count * chunk, tile), jnp.float32),
            jax.ShapeDtypeStruct((chip_count * gram_chunk, tile), jnp.float32),
        ),
        in_specs=[vmem],
        out_specs=(vmem, vmem),
        compiler_params=pltpu.CompilerParams(vmem_limit_bytes=16 * 1024 * 1024),
    )(copies)


def factor_kernel(core_ref, near_ref, far_ref, panel_ref, upper_ref, tinv, y_ref, a_ref, rows_ref, work):
    rows = lax.broadcasted_iota(jnp.int32, (tile, tile), 0)
    cols = lax.broadcasted_iota(jnp.int32, (tile, tile), 1)
    eye = jnp.where(rows == cols, 1.0, 0.0).astype(jnp.float32)
    width = upper_ref.shape[0]
    levels = width // tile
    for core, blocks in enumerate(gram_blocks):
        for at, (i, j) in enumerate(blocks):
            side = slice(at * tile, (at + 1) * tile)
            block = jnp.where(core_ref[0] == core, near_ref[side, :], far_ref[side, :])
            if i == j:
                block = block + ridge_shift * eye
            a_ref[i * tile : (i + 1) * tile, j * tile : (j + 1) * tile] = block
    upper_ref[...] = jnp.zeros_like(upper_ref)
    rows_ref[...] = panel_ref[...]

    def load(b):
        work[:, 0:tile] = a_ref[b : b + tile, b : b + tile]
        work[:, tile:] = eye

    def spread(b):
        e = b + tile
        inverse = work[:, tile:]
        tinv[b:e, :] = inverse
        upper_ref[b:e, b:e] = jnp.where(cols >= rows, work[:, 0:tile], 0.0)
        y = product(rows_ref[:, b:e], inverse, 1, 1)
        y_ref[:, b:e] = y
        if e < width:
            u = product(inverse, a_ref[b:e, e:])
            upper_ref[b:e, e:] = u
            for c in range(e, width, tile):
                a_ref[c : c + tile, c:] = a_ref[c : c + tile, c:] - product(
                    u[:, c - e : c - e + tile], u[:, c - e :], 0, 0
                )
            rows_ref[:, e:] = rows_ref[:, e:] - product(y, u)

    def level(step, carry):
        for i in range(levels):
            pl.when(step == i)(lambda i=i: load(i * tile))
        factor_diagonal(work)
        for i in range(levels):
            pl.when(step == i)(lambda i=i: spread(i * tile))
        return carry

    lax.fori_loop(0, levels, level, 0)


def factor(core, near, far, panel):
    own, width = panel.shape
    vmem = pl.BlockSpec(memory_space=pltpu.VMEM)
    return pl.pallas_call(
        factor_kernel,
        out_shape=(
            jax.ShapeDtypeStruct((width, width), jnp.float32),
            jax.ShapeDtypeStruct((width, tile), jnp.float32),
            jax.ShapeDtypeStruct((own, width), jnp.float32),
        ),
        in_specs=[pl.BlockSpec(memory_space=pltpu.SMEM), vmem, vmem, vmem],
        out_specs=(vmem, vmem, vmem),
        scratch_shapes=[
            pltpu.VMEM((width, width), jnp.float32),
            pltpu.VMEM((own, width), jnp.float32),
            pltpu.VMEM((tile, 2 * tile), jnp.float32),
        ],
        compiler_params=pltpu.CompilerParams(vmem_limit_bytes=16 * 1024 * 1024),
        cost_estimate=pl.CostEstimate(flops=16 * 10**9, bytes_accessed=4 * 10**6, transcendentals=0),
    )(core, near, far, panel)


def back_kernel(start_ref, upper_ref, tinv, y_ref, mixed_ref, r_ref, right):
    own, width = y_ref.shape
    picked = r_ref.shape[0]
    right[0:own, :] = y_ref[...]
    unit_row = lax.broadcasted_iota(jnp.int32, (picked, width), 0) + start_ref[0]
    unit_col = lax.broadcasted_iota(jnp.int32, (picked, width), 1)
    right[own:, :] = jnp.where(unit_row == unit_col, 1.0, 0.0).astype(jnp.float32)
    r_ref[...] = upper_ref[pl.ds(pl.multiple_of(start_ref[0], picked), picked), :]
    done = None
    for b in range(width - tile, -1, -tile):
        e = b + tile
        side = right[:, b:e]
        if done is not None:
            side = side - product(done, upper_ref[b:e, e:], 1, 1)
        part = product(side, tinv[b:e, :])
        mixed_ref[b // tile] = part
        done = part if done is None else jnp.concatenate([part, done], 1)


def back(start, upper, tinv, y, picked):
    own, width = y.shape
    vmem = pl.BlockSpec(memory_space=pltpu.VMEM)
    return pl.pallas_call(
        back_kernel,
        out_shape=(
            jax.ShapeDtypeStruct((width // tile, own + picked, tile), jnp.float32),
            jax.ShapeDtypeStruct((picked, width), jnp.float32),
        ),
        in_specs=[pl.BlockSpec(memory_space=pltpu.SMEM), vmem, vmem, vmem],
        out_specs=(vmem, vmem),
        scratch_shapes=[pltpu.VMEM((own + picked, width), jnp.float32)],
        compiler_params=pltpu.CompilerParams(vmem_limit_bytes=16 * 1024 * 1024),
        cost_estimate=pl.CostEstimate(flops=4 * 10**9, bytes_accessed=2 * 10**6, transcendentals=0),
    )(start, upper, tinv, y)


def finish_kernel(place_ref, mixed_ref, *refs):
    near, far = refs[:classes], refs[classes : 2 * classes]
    trail_ref, updated_ref, coupling_ref = refs[2 * classes :]
    own = trail_ref.shape[0]
    half = near[0].shape[0]
    core = place_ref[0]
    left = [mixed_ref[place_ref[1 + m]] for m in range(classes)]
    left = [jnp.concatenate(left[m : m + 2], 1) for m in range(0, classes, 2)]
    for c in range(0, half, tile):
        out = None
        for m in range(0, classes, 2):
            right = jnp.concatenate(
                [
                    jnp.concatenate([side[m][c : c + tile, :], side[m + 1][c : c + tile, :]], 0)
                    for side in (near, far)
                ],
                1,
            )
            term = product(left[m // 2], right)
            out = term if out is None else out + term
        for part, where in ((out[:, :tile], core), (out[:, tile:], 1 - core)):
            at = pl.ds(pl.multiple_of(where * half + c, tile), tile)
            updated_ref[:, at] = trail_ref[:, at] - part[:own]
            coupling_ref[:, at] = part[own:]


def finish(place, mixed, near, far, trailing):
    vmem = pl.BlockSpec(memory_space=pltpu.VMEM)
    own, trail = trailing.shape
    return pl.pallas_call(
        finish_kernel,
        out_shape=(
            jax.ShapeDtypeStruct((own, trail), jnp.float32),
            jax.ShapeDtypeStruct((mixed.shape[1] - own, trail), jnp.float32),
        ),
        in_specs=[pl.BlockSpec(memory_space=pltpu.SMEM)] + [vmem] * (2 + 2 * classes),
        out_specs=(vmem, vmem),
        compiler_params=pltpu.CompilerParams(vmem_limit_bytes=32 * 1024 * 1024),
    )(place, mixed, *near, *far, trailing)


def kind_of(x, y, z):
    return (x % 2) ^ (2 * (y % 2)) ^ (3 * (z % 2))


def local(panel, trailing, counts):
    own, width = panel.shape
    half = trailing.shape[1] // 2
    depth = lax.axis_size("z")
    groups = lax.axis_size("grp")
    side = 4
    members = 2 * depth
    chip_count = groups * depth
    chunk = half // chip_count
    gram_chunk = len(gram_blocks[0]) * tile // chip_count
    kinds = [kind_of(g % side, g // side, z) for g in range(groups) for z in range(depth)]
    group, z, core = lax.axis_index("grp"), lax.axis_index("z"), lax.axis_index("core")
    kind = kind_of(group % side, group // side, z)
    core_one = core.astype(jnp.int32)[None]
    place = jnp.stack([core] + [kind ^ m for m in range(classes)]).astype(jnp.int32)
    swap = [(0, 1), (1, 0)]
    count_row = counts[None, :]
    sent_trail = lax.dynamic_slice_in_dim(trailing, (1 - core) * half, half, 1)
    with jax.named_scope("swap_inputs"):
        far_counts = lax.ppermute(count_row, "core", swap)
        other_panel = lax.ppermute(panel, "core", swap)
        far_trail = lax.ppermute(sent_trail, "core", swap)
    with jax.named_scope("local_products"):
        terms = products(
            core_one, panel, other_panel, trailing, far_trail, count_row, far_counts, chip_count, own * groups * members
        )
    with jax.named_scope("scatter_sums"):
        pieces = lax.all_to_all(terms.reshape(chip_count, 1, -1), chips, 0, 0, tiled=True)
    with jax.named_scope("sum_pieces"):
        copies = sum_pieces(pieces.reshape(-1, tile), chip_count, chunk, gram_chunk, kinds)
    with jax.named_scope("gather_sums"):
        copies = lax.all_to_all(copies.reshape(chip_count, 1, -1), chips, 0, 0, tiled=True)
    with jax.named_scope("unpack_sums"):
        quarter, near_gram = unpack(copies.reshape(-1, tile), chip_count, chunk, gram_chunk)
    with jax.named_scope("swap_gram"):
        far_gram = lax.ppermute(near_gram, "core", swap)
    near = [quarter]
    with jax.named_scope("quarters_along_x"):
        near.append(lax.ppermute(quarter, "grp", [(i, i ^ 1) for i in range(groups)]))
    with jax.named_scope("quarters_along_y"):
        near.append(lax.ppermute(quarter, "grp", [(i, i ^ side) for i in range(groups)]))
    with jax.named_scope("quarters_along_z"):
        near.append(lax.ppermute(quarter, "z", [(i, i ^ 1) for i in range(depth)]))
    with jax.named_scope("factor_gram"):
        upper, tinv, y = factor(core_one, near_gram, far_gram, panel)
    upper, tinv, y, *near = lax.optimization_barrier((upper, tinv, y, *near))
    with jax.named_scope("swap_quarters"):
        far = [lax.ppermute(part, "core", swap) for part in near]
    picked = width // members
    start = (z * 2 + core) * picked
    with jax.named_scope("back_substitute"):
        mixed, r_rows = back(start.astype(jnp.int32)[None], upper, tinv, y, picked)
    with jax.named_scope("apply_factor"):
        updated, coupling = finish(place, mixed, near, far, trailing)
    return (r_rows, coupling, updated)


def solution(mesh):
    groups, members = mesh.devices.shape
    split = Mesh(mesh.devices.reshape(groups, members // 2, 2), ("grp", "z", "core"))
    rows = P(("grp", "z", "core"))
    return jax.shard_map(
        local,
        mesh=split,
        in_specs=(P(("grp", "z", "core"), None), P(("grp", "z", "core"), None), rows),
        out_specs=(P(("z", "core"), None), P(("z", "core"), None), P(("grp", "z", "core"), None)),
        check_vma=False,
    )
```

time: 126 us -> 105 us (0.83)
  blocking collectives: 79.8 us -> 60.8 us
  local copies, waits for them, and re-layouts: 3.29 us -> 7.79 us
  Pallas kernels: 29.9 us -> 26.7 us
  other arithmetic: 2.06 us -> 0 us
  waiting for transfers between devices: 3.87 us -> 2.18 us
    all_to_all x2, blocking collectives: 79.8 us -> 60.8 us  [the longest x1 41.4 us: local(): lax.all_to_all(terms.reshape(chip_count, 1, -1), chips, 0, 0, tiled=True)]
    unnamed x8 -> x16, local copies, waits for them, and re-layouts: 0.97 us -> 6.66 us
    pallas_call x1, Pallas kernels: 7.44 us -> 4.71 us  [finish(): pl.pallas_call(finish_kernel, out_shape=(jax.ShapeDtypeStruct((own, trail...]
    ppermute x1, waiting for transfers between devices: 2.96 us -> 0.64 us  [local(): far_gram = lax.ppermute(near_gram, 'core', swap)]
    pallas_call x1, Pallas kernels: 18.5 us -> 16.4 us  [factor(): pl.pallas_call(factor_kernel, out_shape=(jax.ShapeDtypeStruct((width, wid...]
    ppermute x1, starting transfers between devices: 1.14 us -> 2.86 us  [local(): far_gram = lax.ppermute(near_gram, 'core', swap)]
    pallas_call x1 -> x4, Pallas kernels: 3.93 us -> 5.54 us  [the longest x1 2.68 us: products(): pl.pallas_call(functools.partial(products_kernel, chip_count=chip_count,...]
    ppermute x2 -> x8, starting transfers between devices: 3.2 us -> 2.32 us  [the longest x4 1.28 us: local(): far = [lax.ppermute(part, 'core', swap) for part in near]]
  transfers between devices with their start and end apart: 5 -> 11, of which waited for: 2 -> 2; matrix products, arithmetic and copies ran while one was open for 2% -> 0% of each run, Pallas kernels for 15% -> 18%
where the time goes in v3:
time: 105 us
  blocking collectives  60.8 us (58%)
  Pallas kernels  26.7 us (25%)
  local copies, waits for them, and re-layouts  7.79 us (7%)
  starting transfers between devices  6.77 us (6%)
  waiting for transfers between devices  2.18 us (2%)
    all_to_all x1, blocking collectives, local(): lax.all_to_all(terms.reshape(chip_count, 1, -1), chips, 0, 0, tiled=True)  41.4 us
    all_to_all x1, blocking collectives, local(): lax.all_to_all(copies.reshape(chip_count, 1, -1), chips, 0, 0, tiled=True)  19.4 us
    pallas_call x1, Pallas kernels, factor(): pl.pallas_call(factor_kernel, out_shape=(jax.ShapeDtypeStruct((width, wid...  16.4 us
    unnamed x16, local copies, waits for them, and re-layouts  6.66 us
    pallas_call x1, Pallas kernels, finish(): pl.pallas_call(finish_kernel, out_shape=(jax.ShapeDtypeStruct((own, trail...  4.71 us
    ppermute x1, starting transfers between devices, local(): far_gram = lax.ppermute(near_gram, 'core', swap)  2.86 us
    pallas_call x1, Pallas kernels, products(): pl.pallas_call(functools.partial(products_kernel, chip_count=chip_count,...  2.68 us
    pallas_call x1, Pallas kernels, back(): pl.pallas_call(back_kernel, out_shape=(jax.ShapeDtypeStruct((width // til...  2.62 us
  transfers between devices with their start and end apart: 11, of which 2 were waited for; matrix products, arithmetic and copies ran while one was open for 0% of the time, Pallas kernels for 18%

profile of v3, /device:TPU:1, one launch (start us, length us, event | category | flops | bytes accessed | tf_op | source)
XLA Modules:
  0.0 105.0 jit_solution(14156949455840061729)
XLA Ops:
  0.6 1.1 %constant_dynamic-slice_fusion = f32[128,896]{1,0:T(8,128)S(1)} fusion(f32[128,1792]{1,0:T(8,128)} %refs_8_.1, s32[]{:T(128)S(6)} %select_n.26), kind=kLoop, calls=%fused_computation | loop fusion | bytes 917508 | tf_op jit(solution)/shard_map/dynamic_slice | solution.py:362
  1.7 1.5 %collective-permute-start.1 = (f32[128,896]{1,0:T(8,128)S(1)}, f32[128,896]{1,0:T(8,128)S(1)}, u32[]{:S(2)}, u32[]{:S(2)}) collective-permute-start(f32[128,896]{1,0:T(8,128)S(1)} %constant_dynamic-slice_fusion), channel_id=1, source_target_pairs={{0,1},{1,0},{2,3},{3,2},{4,5},{5,4},{6,7},{7,6},{8,9},{9,8},{10,11... | collective-permute-start | bytes 1376264 | tf_op jit(solution)/shard_map/swap_inputs/ppermute | solution.py:366
  3.2 0.1 collective-permute-start
  3.3 0.4 collective-permute-start.2
  3.7 1.5 %collective-permute-done.2.far_counts_ref = s32[1,128]{1,0:T(1,128)S(1)} collective-permute-done((s32[1,128]{1,0:T(1,128)}, s32[1,128]{1,0:T(1,128)S(1)}, u32[]{:S(2)}, u32[]{:S(2)}) %collective-permute-start.2) | collective-permute-done | bytes 544 | tf_op jit(solution)/shard_map/swap_inputs/ppermute | solution.py:364
  5.2 0.0 collective-permute-done.other_ref
  5.2 0.0 collective-permute-done.1.far_ref
  5.2 0.0 copy-start
  5.2 1.2 %copy-done = f32[128,1792]{1,0:T(8,128)S(1)} copy-done((f32[128,1792]{1,0:T(8,128)S(1)}, f32[128,1792]{1,0:T(8,128)}, u32[]{:S(2)}) %copy-start) | copy-done | bytes 917528
  6.4 0.0 copy-start.2
  6.4 0.9 copy-done.2
  7.4 0.0 copy-start.3
  7.4 0.7 copy-done.3
  8.0 2.7 %local_products.1 = f32[4224,128]{1,0:T(8,128)S(1)} custom-call(s32[1]{0:T(128)} %bitcast.1.core_ref, f32[128,512]{1,0:T(8,128)S(1)} %copy-done.2, f32[128,512]{1,0:T(8,128)S(1)} %collective-permute-done.other_ref, f32[128,1792]{1,0:T(8,128)S(1)} %copy-done, f32[128,896]{1,0:T(8,128)S(1)} %collective-permute-done.1.far_ref, s32[1,128]{1,0:T(1,128)S(1)} %bitcast.16, ...), custom_call_target="tpu_custom_call" | custom-call | tf_op jit(solution)/shard_map/local_products/pallas_call | solution.py:113
  10.7 41.4 %all_to_all.10 = f32[64,1,8448]{2,1,0:T(1,128)S(1)} all-to-all(f32[64,1,8448]{2,1,0:T(1,128)S(1)} %bitcast.11), channel_id=1, replica_groups=mesh['grp'=16,'z'=4,'core'=2] {'grp','z'}, dimensions={0} | all-to-all | bytes 4325376 | tf_op jit(solution)/shard_map/scatter_sums/all_to_all | solution.py:372
  52.1 0.2 sum_pieces.1
  52.3 19.4 %all_to_all.11 = f32[64,1,3072]{2,1,0:T(1,128)S(1)} all-to-all(f32[64,1,3072]{2,1,0:T(1,128)S(1)} %bitcast.14), channel_id=1, replica_groups=mesh['grp'=16,'z'=4,'core'=2] {'grp','z'}, dimensions={0} | all-to-all | bytes 1572864 | tf_op jit(solution)/shard_map/gather_sums/all_to_all | solution.py:376
  71.7 0.1 unpack_sums.1
  71.8 2.9 %collective-permute-start.3 = (f32[640,128]{1,0:T(8,128)S(1)}, f32[640,128]{1,0:T(8,128)S(1)}, u32[]{:S(2)}, u32[]{:S(2)}) collective-permute-start(f32[640,128]{1,0:T(8,128)S(1)} %get-tuple-element.19.near_ref), channel_id=1, source_target_pairs={{0,1},{1,0},{2,3},{3,2},{4,5},{5,4},{6,7},{7,6},{8,9},{9,8},{10,11... | collective-permute-start | bytes 983048 | tf_op jit(solution)/shard_map/swap_gram/ppermute | solution.py:380
  74.6 0.4 collective-permute-start.6
  75.1 0.0 collective-permute-start.5
  75.1 0.2 collective-permute-start.4
  75.2 0.6 collective-permute-done.3.far_ref
  75.9 16.4 %factor_gram.1 = (f32[512,512]{1,0:T(8,128)S(1)}, f32[512,128]{1,0:T(8,128)S(1)}, f32[128,512]{1,0:T(8,128)S(1)}) custom-call(s32[1]{0:T(128)} %bitcast.1.core_ref, f32[640,128]{1,0:T(8,128)S(1)} %get-tuple-element.19.near_ref, f32[640,128]{1,0:T(8,128)S(1)} %collective-permute-done.3.far_ref, f32[128,512]{1,0:T(8,128)S(1)} %copy-done.2), custom_call_target="tpu_custom_call" | custom-call | flops 16000000000 | bytes 4000000 | tf_op jit(solution)/shard_map/factor_gram/pallas_call | solution.py:245
  92.3 0.0 copy-start.4
  92.3 1.0 copy-done.4
  93.3 0.0 copy-start.6
  93.3 0.7 copy-done.6
  94.0 0.0 collective-permute-done.6.refs_3_
  94.0 0.0 collective-permute-done.5.refs_2_
  94.0 0.0 collective-permute-done.4.refs_1_
  94.0 0.6 collective-permute-start.7
  94.7 0.1 collective-permute-start.8
  94.8 0.4 collective-permute-start.9
  95.2 0.1 collective-permute-start.10
  95.3 0.1 stack.20.place_ref
  95.4 0.0 copy-start.5
  95.4 1.2 %copy-done.5 = f32[512,512]{1,0:T(8,128)S(1)} copy-done((f32[512,512]{1,0:T(8,128)S(1)}, f32[512,512]{1,0:T(8,128)}, u32[]{:S(2)}) %copy-start.5) | copy-done | bytes 1048600
  96.6 0.0 copy-start.7
  96.6 0.9 copy-done.7
  97.6 0.0 copy-start.1
  97.6 2.6 %back_substitute.1 = (f32[4,192,128]{2,1,0:T(8,128)S(1)}, f32[64,512]{1,0:T(8,128)}) custom-call(s32[1]{0:T(128)} %bitcast.start_ref, f32[512,512]{1,0:T(8,128)S(1)} %copy-done.5, f32[512,128]{1,0:T(8,128)S(1)} %get-tuple-element.25.tinv, f32[128,512]{1,0:T(8,128)S(1)} %copy-done.7), custom_call_target="tpu_custom_call" | custom-call | flops 4000000000 | bytes 2000000 | tf_op jit(solution)/shard_map/back_substitute/pallas_call | solution.py:286
  100.2 0.0 collective-permute-done.7.refs_4_
  100.2 0.0 collective-permute-done.8.refs_5_
  100.2 0.0 collective-permute-done.9.refs_6_
  100.2 0.0 collective-permute-done.10.refs_7_
  100.2 0.0 copy-done.1
  100.2 4.7 %apply_factor.1 = (f32[128,1792]{1,0:T(8,128)}, f32[64,1792]{1,0:T(8,128)}) custom-call(s32[5]{0:T(128)S(1)} %stack.20.place_ref, f32[4,192,128]{2,1,0:T(8,128)S(1)} %get-tuple-element.28.mixed_ref, f32[896,128]{1,0:T(8,128)S(1)} %get-tuple-element.29.refs_0_, f32[896,128]{1,0:T(8,128)S(1)} %collective-permute-done.4.refs_1_, ...), custom_call_target="tpu_custom_call" | custom-call | tf_op jit(solution)/shard_map/apply_factor/pallas_call | solution.py:329
Async XLA Ops:
  1.7 3.5 %collective-permute-start.1 = (f32[128,896]{1,0:T(8,128)S(1)}, f32[128,896]{1,0:T(8,128)S(1)}, u32[]{:S(2)}, u32[]{:S(2)}) collective-permute-start(f32[128,896]{1,0:T(8,128)S(1)} %constant_dynamic-slice_fusion), channel_id=1, source_target_pairs={{0,1},{1,0},{2,3},{3,2},{4,5},{5,4},{6,7},{7,6},{8,9},{9,8},{10,11... | collective-permute-start | bytes 1376264 | tf_op jit(solution)/shard_map/swap_inputs/ppermute | solution.py:366
  3.2 2.0 %collective-permute-start = (f32[128,512]{1,0:T(8,128)}, f32[128,512]{1,0:T(8,128)S(1)}, u32[]{:S(2)}, u32[]{:S(2)}) collective-permute-start(f32[128,512]{1,0:T(8,128)} %panel_ref.3), channel_id=1, source_target_pairs={{0,1},{1,0},{2,3},{3,2},{4,5},{5,4},{6,7},{7,6},{8,9},{9,8},{10,11... | collective-permute-start | bytes 786440 | tf_op jit(solution)/shard_map/swap_inputs/ppermute | solution.py:365
  3.3 1.9 %collective-permute-start.2 = (s32[1,128]{1,0:T(1,128)}, s32[1,128]{1,0:T(1,128)S(1)}, u32[]{:S(2)}, u32[]{:S(2)}) collective-permute-start(s32[1,128]{1,0:T(1,128)} %bitcast.15), channel_id=1, source_target_pairs={{0,1},{1,0},{2,3},{3,2},{4,5},{5,4},{6,7},{7,6},{8,9},{9,8},{10,11... | collective-permute-start | bytes 1544 | tf_op jit(solution)/shard_map/swap_inputs/ppermute | solution.py:364
  5.2 1.2 %copy-start = (f32[128,1792]{1,0:T(8,128)S(1)}, f32[128,1792]{1,0:T(8,128)}, u32[]{:S(2)}) copy-start(f32[128,1792]{1,0:T(8,128)} %refs_8_.1) | copy-start | bytes 2752516
  6.4 0.9 copy-start.2
  7.4 0.7 copy-start.3
  71.8 4.1 %collective-permute-start.3 = (f32[640,128]{1,0:T(8,128)S(1)}, f32[640,128]{1,0:T(8,128)S(1)}, u32[]{:S(2)}, u32[]{:S(2)}) collective-permute-start(f32[640,128]{1,0:T(8,128)S(1)} %get-tuple-element.19.near_ref), channel_id=1, source_target_pairs={{0,1},{1,0},{2,3},{3,2},{4,5},{5,4},{6,7},{7,6},{8,9},{9,8},{10,11... | collective-permute-start | bytes 983048 | tf_op jit(solution)/shard_map/swap_gram/ppermute | solution.py:380
  74.6 19.4 %collective-permute-start.6 = (f32[896,128]{1,0:T(8,128)S(1)}, f32[896,128]{1,0:T(8,128)S(1)}, u32[]{:S(2)}, u32[]{:S(2)}) collective-permute-start(f32[896,128]{1,0:T(8,128)S(1)} %get-tuple-element.29.refs_0_), channel_id=1, source_target_pairs={{0,2},{2,0},{4,6},{6,4},{1,3},{3,1},{5,7},{7,5},{8,10},{10,8},{12,... | collective-permute-start | bytes 1376264 | tf_op jit(solution)/shard_map/quarters_along_z/ppermute | solution.py:387
  75.1 19.0 %collective-permute-start.5 = (f32[896,128]{1,0:T(8,128)S(1)}, f32[896,128]{1,0:T(8,128)S(1)}, u32[]{:S(2)}, u32[]{:S(2)}) collective-permute-start(f32[896,128]{1,0:T(8,128)S(1)} %get-tuple-element.29.refs_0_), channel_id=1, source_target_pairs={{0,32},{8,40},{16,48},{24,56},{32,0},{40,8},{48,16},{56,24},{64,96... | collective-permute-start | bytes 1376264 | tf_op jit(solution)/shard_map/quarters_along_y/ppermute | solution.py:385
  75.1 19.0 %collective-permute-start.4 = (f32[896,128]{1,0:T(8,128)S(1)}, f32[896,128]{1,0:T(8,128)S(1)}, u32[]{:S(2)}, u32[]{:S(2)}) collective-permute-start(f32[896,128]{1,0:T(8,128)S(1)} %get-tuple-element.29.refs_0_), channel_id=1, source_target_pairs={{0,8},{8,0},{16,24},{24,16},{32,40},{40,32},{48,56},{56,48},{64,72... | collective-permute-start | bytes 1376264 | tf_op jit(solution)/shard_map/quarters_along_x/ppermute | solution.py:383
  92.3 1.0 copy-start.4
  93.3 0.7 copy-start.6
  94.0 6.2 %collective-permute-start.7 = (f32[896,128]{1,0:T(8,128)S(1)}, f32[896,128]{1,0:T(8,128)S(1)}, u32[]{:S(2)}, u32[]{:S(2)}) collective-permute-start(f32[896,128]{1,0:T(8,128)S(1)} %get-tuple-element.29.refs_0_), channel_id=1, source_target_pairs={{0,1},{1,0},{2,3},{3,2},{4,5},{5,4},{6,7},{7,6},{8,9},{9,8},{10,11... | collective-permute-start | bytes 1376264 | tf_op jit(solution)/shard_map/swap_quarters/ppermute | solution.py:392
  94.7 5.5 %collective-permute-start.8 = (f32[896,128]{1,0:T(8,128)S(1)}, f32[896,128]{1,0:T(8,128)S(1)}, u32[]{:S(2)}, u32[]{:S(2)}) collective-permute-start(f32[896,128]{1,0:T(8,128)S(1)} %collective-permute-done.4.refs_1_), channel_id=1, source_target_pairs={{0,1},{1,0},{2,3},{3,2},{4,5},{5,4},{6,7},{7,6},{8,9},{9,8},{10,11... | collective-permute-start | bytes 1376264 | tf_op jit(solution)/shard_map/swap_quarters/ppermute | solution.py:392
  94.8 5.4 %collective-permute-start.9 = (f32[896,128]{1,0:T(8,128)S(1)}, f32[896,128]{1,0:T(8,128)S(1)}, u32[]{:S(2)}, u32[]{:S(2)}) collective-permute-start(f32[896,128]{1,0:T(8,128)S(1)} %collective-permute-done.5.refs_2_), channel_id=1, source_target_pairs={{0,1},{1,0},{2,3},{3,2},{4,5},{5,4},{6,7},{7,6},{8,9},{9,8},{10,11... | collective-permute-start | bytes 1376264 | tf_op jit(solution)/shard_map/swap_quarters/ppermute | solution.py:392
  95.2 5.0 %collective-permute-start.10 = (f32[896,128]{1,0:T(8,128)S(1)}, f32[896,128]{1,0:T(8,128)}, u32[]{:S(2)}, u32[]{:S(2)}) collective-permute-start(f32[896,128]{1,0:T(8,128)S(1)} %collective-permute-done.6.refs_3_), channel_id=1, source_target_pairs={{0,1},{1,0},{2,3},{3,2},{4,5},{5,4},{6,7},{7,6},{8,9},{9,8},{10,11... | collective-permute-start | bytes 1376264 | tf_op jit(solution)/shard_map/swap_quarters/ppermute | solution.py:392
  95.4 1.2 %copy-start.5 = (f32[512,512]{1,0:T(8,128)S(1)}, f32[512,512]{1,0:T(8,128)}, u32[]{:S(2)}) copy-start(f32[512,512]{1,0:T(8,128)} %copy-done.4) | copy-start | bytes 3145732
  96.6 0.9 copy-start.7
  97.6 2.6 %copy-start.1 = (f32[128,1792]{1,0:T(8,128)S(1)}, f32[128,1792]{1,0:T(8,128)}, u32[]{:S(2)}) copy-start(f32[128,1792]{1,0:T(8,128)} %refs_8_.1) | copy-start | bytes 2752516

commit v4 on v3

v4 whole, which is shorter than its diff:
```python
import functools

import jax
import jax.numpy as jnp
from jax import lax
from jax.experimental import pallas as pl
from jax.experimental.pallas import tpu as pltpu
from jax.sharding import Mesh, PartitionSpec as P

ridge_shift = 0.05
HIGHEST = lax.Precision.HIGHEST
tile = 128
strip = 32
chips = ("grp", "z")
classes = 4


def product(left, right, left_dim=1, right_dim=0):
    return lax.dot_general(
        left,
        right,
        (((left_dim,), (right_dim,)), ((), ())),
        precision=HIGHEST,
        preferred_element_type=jnp.float32,
    )


def factor_diagonal(work):
    sub = lax.broadcasted_iota(jnp.int32, (8, tile), 0)
    groups = strip // 8

    def spread_row(array, row):
        return jnp.broadcast_to(array[row : row + 1, :], (8, tile))

    for r in range(0, tile, strip):
        left = [work[r + 8 * g : r + 8 * g + 8, 0:tile] for g in range(groups)]
        right = [work[r + 8 * g : r + 8 * g + 8, tile : 2 * tile] for g in range(groups)]
        col = {}
        for c in range(strip):
            for g in range(c // 8, groups):
                col[c, g] = jnp.broadcast_to(left[g][:, r + c : r + c + 1], (8, tile))
        for k in range(strip):
            at, row = k // 8, k % 8
            inv = lax.rsqrt(spread_row(col[k, at], row))
            low = {g: col[k, g] * inv for g in range(at, groups)}
            for c in range(k + 1, strip):
                factor_c = spread_row(low[c // 8], c % 8)
                for g in range(c // 8, groups):
                    col[c, g] = col[c, g] - low[g] * factor_c
            below = jnp.where(sub > row, low[at], 0.0)
            for side in (left, right):
                pivot = spread_row(side[at], row) * inv
                side[at] = jnp.where(sub == row, pivot, side[at] - below * pivot)
                for g in range(at + 1, groups):
                    side[g] = side[g] - low[g] * pivot
        new_left = jnp.concatenate(left, 0)
        new_right = jnp.concatenate(right, 0)
        work[r : r + strip, 0:tile] = new_left
        work[r : r + strip, tile : 2 * tile] = new_right
        if r + strip < tile:
            update = product(new_left, jnp.concatenate([new_left, new_right], 1), 0, 0)
            work[r + strip : tile, :] = work[r + strip : tile, :] - update[r + strip : tile, :]


gram_blocks = (((0, 0), (1, 1), (0, 1), (0, 2), (0, 3)), ((2, 2), (3, 3), (2, 3), (1, 2), (1, 3)))


def products_kernel(place_ref, panel_ref, other_ref, trail_ref, far_ref, counts_ref, far_counts_ref, *refs, total_rows):
    outs, gram, (pt, wp, wt, quarters) = refs[:classes], refs[classes], refs[classes + 1 :]
    core = place_ref[0]
    own, width = panel_ref.shape
    half = trail_ref.shape[1]
    for at, rows, trail, count in ((0, panel_ref, trail_ref, counts_ref), (own, other_ref, far_ref, far_counts_ref)):
        weight = jnp.transpose(jnp.broadcast_to(count[...].astype(jnp.float32) / total_rows, (own, own)))
        for c in range(0, width, tile):
            block = rows[:, c : c + tile]
            pt[c : c + tile, at : at + own] = jnp.transpose(block)
            wp[at : at + own, c : c + tile] = block * weight
        for c in range(0, half, tile):
            wt[at : at + own, c : c + tile] = trail[:, c : c + tile] * weight
    step = 2 * tile
    for c in range(0, half, step):
        n = min(step, half - c)
        part = product(pt[...], wt[:, c : c + n])
        for k in range(classes):
            for j in range(0, n, tile):
                quarters[k, c + j : c + j + tile, :] = part[k * tile : (k + 1) * tile, j : j + tile]
    for m in range(classes):
        outs[m][...] = quarters[place_ref[1 + m]]
    near = pl.multiple_of(core * step, tile)
    first = product(pt[pl.ds(near, tile), :], wp[:, pl.ds(near, step)])
    gram[0:tile, :] = first[:, :tile]
    gram[2 * tile : 3 * tile, :] = first[:, tile:]
    near = pl.multiple_of(core * step + tile, tile)
    gram[tile : 2 * tile, :] = product(pt[pl.ds(near, tile), :], wp[:, pl.ds(near, tile)])
    near = pl.multiple_of(core * tile, tile)
    last = product(pt[pl.ds(near, tile), :], wp[:, step:])
    gram[3 * tile : 4 * tile, :] = last[:, :tile]
    gram[4 * tile :, :] = last[:, tile:]


def products(place, panel, other, trailing, far, counts, far_counts, total_rows):
    own, width = panel.shape
    half = far.shape[1]
    gram_rows = len(gram_blocks[0]) * tile
    whole = lambda shape: pl.BlockSpec(shape, lambda i, place: (0, 0))
    return pl.pallas_call(
        functools.partial(products_kernel, total_rows=total_rows),
        out_shape=[jax.ShapeDtypeStruct((half, tile), jnp.float32)] * classes
        + [jax.ShapeDtypeStruct((gram_rows, tile), jnp.float32)],
        grid_spec=pltpu.PrefetchScalarGridSpec(
            num_scalar_prefetch=1,
            grid=(1,),
            in_specs=[
                whole((own, width)),
                whole((own, width)),
                pl.BlockSpec((own, half), lambda i, place: (0, place[0])),
                whole((own, half)),
                whole((1, own)),
                whole((1, own)),
            ],
            out_specs=[whole((half, tile))] * classes + [whole((gram_rows, tile))],
            scratch_shapes=[
                pltpu.VMEM((width, 2 * own), jnp.float32),
                pltpu.VMEM((2 * own, width), jnp.float32),
                pltpu.VMEM((2 * own, half), jnp.float32),
                pltpu.VMEM((classes, half, tile), jnp.float32),
            ],
        ),
        compiler_params=pltpu.CompilerParams(vmem_limit_bytes=32 * 1024 * 1024),
    )(place, panel, other, trailing, far, counts, far_counts)


def combine_kernel(gram_ref, *refs, chip_count):
    parts, out_ref, four = refs[:classes], refs[classes], refs[classes + 1]
    size = gram_ref.shape[0] // chip_count
    chunk = parts[0].shape[0] // chip_count
    total = gram_ref[0 : 4 * size, :]
    for at in range(4 * size, chip_count * size, 4 * size):
        total = total + gram_ref[at : at + 4 * size, :]
    four[...] = total
    gram = four[0:size, :]
    for at in range(size, 4 * size, size):
        gram = gram + four[at : at + size, :]
    for q in range(chip_count):
        side = slice(q * chunk, (q + 1) * chunk)
        cross = (parts[0][side, :] + parts[1][side, :]) + (parts[2][side, :] + parts[3][side, :])
        out_ref[q * (size + chunk) : (q + 1) * (size + chunk), :] = jnp.concatenate([gram, cross], 0)


def combine(gram_pieces, parts, chip_count):
    vmem = pl.BlockSpec(memory_space=pltpu.VMEM)
    gram_rows, rows = gram_pieces.shape[0], parts[0].shape[0]
    return pl.pallas_call(
        functools.partial(combine_kernel, chip_count=chip_count),
        out_shape=jax.ShapeDtypeStruct((gram_rows + rows, tile), jnp.float32),
        in_specs=[vmem] * (1 + classes),
        out_specs=vmem,
        scratch_shapes=[pltpu.VMEM((4 * gram_rows // chip_count, tile), jnp.float32)],
        compiler_params=pltpu.CompilerParams(vmem_limit_bytes=16 * 1024 * 1024),
    )(gram_pieces, *parts)


def unpack_kernel(mixed_ref, gram_ref, copies_ref, sums, *, size, chunk, kinds):
    both = size + chunk
    for k in range(classes):
        total = None
        for q, kind in enumerate(kinds):
            if kind == k:
                piece = mixed_ref[q * both : (q + 1) * both, :]
                total = piece if total is None else total + piece
        sums[...] = total
        cross = sums[size:, :]
        for q, kind in enumerate(kinds):
            if kind == k:
                copies_ref[q * chunk : (q + 1) * chunk, :] = cross
    for q in range(len(kinds)):
        gram_ref[q * size : (q + 1) * size, :] = mixed_ref[q * both : q * both + size, :]


def unpack(mixed, size, chunk, kinds):
    vmem = pl.BlockSpec(memory_space=pltpu.VMEM)
    return pl.pallas_call(
        functools.partial(unpack_kernel, size=size, chunk=chunk, kinds=kinds),
        out_shape=(
            jax.ShapeDtypeStruct((len(kinds) * size, tile), jnp.float32),
            jax.ShapeDtypeStruct((len(kinds) * chunk, tile), jnp.float32),
        ),
        in_specs=[vmem],
        out_specs=(vmem, vmem),
        scratch_shapes=[pltpu.VMEM((size + chunk, tile), jnp.float32)],
        compiler_params=pltpu.CompilerParams(vmem_limit_bytes=16 * 1024 * 1024),
    )(mixed)


def factor_levels(a_ref, rows_ref, work, upper_ref, tinv, y_ref):
    rows = lax.broadcasted_iota(jnp.int32, (tile, tile), 0)
    cols = lax.broadcasted_iota(jnp.int32, (tile, tile), 1)
    eye = jnp.where(rows == cols, 1.0, 0.0).astype(jnp.float32)
    width = a_ref.shape[0]
    levels = tinv.shape[0] // tile
    upper_ref[...] = jnp.zeros_like(upper_ref)

    def load(b):
        work[:, 0:tile] = a_ref[b : b + tile, b : b + tile]
        work[:, tile:] = eye

    def spread(b):
        e = b + tile
        inverse = work[:, tile:]
        tinv[b:e, :] = inverse
        upper_ref[b:e, b:e] = jnp.where(cols >= rows, work[:, 0:tile], 0.0)
        y = product(rows_ref[:, b:e], inverse, 1, 1)
        y_ref[:, b:e] = y
        if e < width:
            u = product(inverse, a_ref[b:e, e:])
            upper_ref[b:e, e:] = u
            for c in range(e, width, tile):
                a_ref[c : c + tile, c:] = a_ref[c : c + tile, c:] - product(
                    u[:, c - e : c - e + tile], u[:, c - e :], 0, 0
                )
            rows_ref[:, e:] = rows_ref[:, e:] - product(y, u)

    def level(step, carry):
        for i in range(levels):
            pl.when(step == i)(lambda i=i: load(i * tile))
        factor_diagonal(work)
        for i in range(levels):
            pl.when(step == i)(lambda i=i: spread(i * tile))
        return carry

    lax.fori_loop(0, levels, level, 0)


def factor_first_kernel(place_ref, near_ref, far_ref, panel_ref, upper_ref, tinv, y_ref, rest_a, rest_rows, a_ref, rows_ref, work):
    rows = lax.broadcasted_iota(jnp.int32, (tile, tile), 0)
    cols = lax.broadcasted_iota(jnp.int32, (tile, tile), 1)
    shift = jnp.where(rows == cols, ridge_shift, 0.0).astype(jnp.float32)
    for core, blocks in enumerate(gram_blocks):
        for at, (i, j) in enumerate(blocks):
            side = slice(at * tile, (at + 1) * tile)
            block = jnp.where(place_ref[0] == core, near_ref[side, :], far_ref[side, :])
            if i == j:
                block = block + shift
            a_ref[i * tile : (i + 1) * tile, j * tile : (j + 1) * tile] = block
    rows_ref[...] = panel_ref[...]
    factor_levels(a_ref, rows_ref, work, upper_ref, tinv, y_ref)
    done = tinv.shape[0]
    for c in range(done, a_ref.shape[0], tile):
        rest_a[c - done : c - done + tile, c - done :] = a_ref[c : c + tile, c:]
        if c > done:
            rest_a[c - done : c - done + tile, : c - done] = jnp.zeros((tile, c - done), jnp.float32)
    rest_rows[...] = rows_ref[:, done:]


def factor_rest_kernel(a_in, rows_in, upper_ref, tinv, y_ref, a_ref, rows_ref, work):
    a_ref[...] = a_in[...]
    rows_ref[...] = rows_in[...]
    factor_levels(a_ref, rows_ref, work, upper_ref, tinv, y_ref)


def factor_shapes(width, done, own):
    return [
        jax.ShapeDtypeStruct((done, width), jnp.float32),
        jax.ShapeDtypeStruct((done, tile), jnp.float32),
        jax.ShapeDtypeStruct((own, done), jnp.float32),
    ]


def factor_scratch(width, own):
    return [
        pltpu.VMEM((width, width), jnp.float32),
        pltpu.VMEM((own, width), jnp.float32),
        pltpu.VMEM((tile, 2 * tile), jnp.float32),
    ]


def factor_first(place, near, far, panel, done):
    own, width = panel.shape
    vmem = pl.BlockSpec(memory_space=pltpu.VMEM)
    return pl.pallas_call(
        factor_first_kernel,
        out_shape=factor_shapes(width, done, own)
        + [
            jax.ShapeDtypeStruct((width - done, width - done), jnp.float32),
            jax.ShapeDtypeStruct((own, width - done), jnp.float32),
        ],
        in_specs=[pl.BlockSpec(memory_space=pltpu.SMEM), vmem, vmem, vmem],
        out_specs=[vmem] * 5,
        scratch_shapes=factor_scratch(width, own),
        compiler_params=pltpu.CompilerParams(vmem_limit_bytes=16 * 1024 * 1024),
        cost_estimate=pl.CostEstimate(flops=10 * 10**9, bytes_accessed=4 * 10**6, transcendentals=0),
    )(place, near, far, panel)


def factor_rest(rest_a, rest_rows):
    own, width = rest_rows.shape
    vmem = pl.BlockSpec(memory_space=pltpu.VMEM)
    return pl.pallas_call(
        factor_rest_kernel,
        out_shape=factor_shapes(width, width, own),
        in_specs=[vmem, vmem],
        out_specs=[vmem] * 3,
        scratch_shapes=factor_scratch(width, own),
        compiler_params=pltpu.CompilerParams(vmem_limit_bytes=16 * 1024 * 1024),
        cost_estimate=pl.CostEstimate(flops=10 * 10**9, bytes_accessed=2 * 10**6, transcendentals=0),
    )(rest_a, rest_rows)


def back_kernel(place_ref, upper_a, tinv_a, y_a, upper_b, tinv_b, y_b, mixed_ref, r_ref, right):
    own, done = y_a.shape
    width = upper_a.shape[1]
    picked = r_ref.shape[0]
    start = pl.multiple_of(place_ref[1 + classes], picked)
    right[0:own, 0:done] = y_a[...]
    right[0:own, done:] = y_b[...]
    unit_row = lax.broadcasted_iota(jnp.int32, (picked, width), 0) + start
    unit_col = lax.broadcasted_iota(jnp.int32, (picked, width), 1)
    right[own:, :] = jnp.where(unit_row == unit_col, 1.0, 0.0).astype(jnp.float32)

    @pl.when(start < done)
    def _():
        r_ref[...] = upper_a[pl.ds(start, picked), :]

    @pl.when(start >= done)
    def _():
        r_ref[:, 0:done] = jnp.zeros((picked, done), jnp.float32)
        r_ref[:, done:] = upper_b[pl.ds(pl.multiple_of(start - done, picked), picked), :]

    solved = None
    for b in range(width - tile, -1, -tile):
        side = right[:, b : b + tile]
        low = b >= done
        if solved is not None:
            rest = upper_b[b - done : b - done + tile, b - done + tile :] if low else upper_a[b : b + tile, b + tile :]
            side = side - product(solved, rest, 1, 1)
        part = product(side, tinv_b[b - done : b - done + tile, :] if low else tinv_a[b : b + tile, :])
        mixed_ref[b // tile] = part
        solved = part if solved is None else jnp.concatenate([part, solved], 1)


def back(place, first, rest, picked):
    own, done = first[2].shape
    width = done + rest[2].shape[1]
    vmem = pl.BlockSpec(memory_space=pltpu.VMEM)
    return pl.pallas_call(
        back_kernel,
        out_shape=(
            jax.ShapeDtypeStruct((width // tile, own + picked, tile), jnp.float32),
            jax.ShapeDtypeStruct((picked, width), jnp.float32),
        ),
        in_specs=[pl.BlockSpec(memory_space=pltpu.SMEM)] + [vmem] * 6,
        out_specs=(vmem, vmem),
        scratch_shapes=[pltpu.VMEM((own + picked, width), jnp.float32)],
        compiler_params=pltpu.CompilerParams(vmem_limit_bytes=16 * 1024 * 1024),
        cost_estimate=pl.CostEstimate(flops=4 * 10**9, bytes_accessed=2 * 10**6, transcendentals=0),
    )(place, *first, *rest)


def finish_kernel(place_ref, mixed_ref, *refs):
    near, far = refs[:classes], refs[classes : 2 * classes]
    trail_ref, updated_ref, coupling_ref = refs[2 * classes :]
    own = trail_ref.shape[0]
    half = near[0].shape[0]
    core = place_ref[0]
    left = [mixed_ref[place_ref[1 + m]] for m in range(classes)]
    left = [jnp.concatenate(left[m : m + 2], 1) for m in range(0, classes, 2)]
    for c in range(0, half, tile):
        out = None
        for m in range(0, classes, 2):
            right = jnp.concatenate(
                [
                    jnp.concatenate([side[m][c : c + tile, :], side[m + 1][c : c + tile, :]], 0)
                    for side in (near, far)
                ],
                1,
            )
            term = product(left[m // 2], right)
            out = term if out is None else out + term
        for part, where in ((out[:, :tile], core), (out[:, tile:], 1 - core)):
            at = pl.ds(pl.multiple_of(where * half + c, tile), tile)
            updated_ref[:, at] = trail_ref[:, at] - part[:own]
            coupling_ref[:, at] = part[own:]


def finish(place, mixed, near, far, trailing):
    vmem = pl.BlockSpec(memory_space=pltpu.VMEM)
    own, trail = trailing.shape
    return pl.pallas_call(
        finish_kernel,
        out_shape=(
            jax.ShapeDtypeStruct((own, trail), jnp.float32),
            jax.ShapeDtypeStruct((mixed.shape[1] - own, trail), jnp.float32),
        ),
        in_specs=[pl.BlockSpec(memory_space=pltpu.SMEM)] + [vmem] * (2 + 2 * classes),
        out_specs=(vmem, vmem),
        compiler_params=pltpu.CompilerParams(vmem_limit_bytes=32 * 1024 * 1024),
    )(place, mixed, *near, *far, trailing)


def kind_of(x, y, z):
    return (x % 2) ^ (2 * (y % 2)) ^ (3 * (z % 2))


def local(panel, trailing, counts):
    own, width = panel.shape
    half = trailing.shape[1] // 2
    depth = lax.axis_size("z")
    groups = lax.axis_size("grp")
    side = 4
    members = 2 * depth
    chip_count = groups * depth
    chunk = half // chip_count
    gram_chunk = len(gram_blocks[0]) * tile // chip_count
    kinds = [kind_of(g % side, g // side, z) for g in range(groups) for z in range(depth)]
    group, z, core = lax.axis_index("grp"), lax.axis_index("z"), lax.axis_index("core")
    kind = kind_of(group % side, group // side, z)
    picked = width // members
    start = (z * 2 + core) * picked
    place = jnp.stack([core] + [kind ^ m for m in range(classes)] + [start]).astype(jnp.int32)
    swap = [(0, 1), (1, 0)]
    count_row = counts[None, :]
    sent_trail = lax.dynamic_slice_in_dim(trailing, (1 - core) * half, half, 1)
    with jax.named_scope("swap_inputs"):
        far_counts = lax.ppermute(count_row, "core", swap)
        other_panel = lax.ppermute(panel, "core", swap)
        far_trail = lax.ppermute(sent_trail, "core", swap)
    with jax.named_scope("local_products"):
        *terms, gram_terms = products(
            place, panel, other_panel, trailing, far_trail, count_row, far_counts, own * groups * members
        )
    along = (
        ("along_x", "grp", [(i, i ^ 1) for i in range(groups)]),
        ("along_y", "grp", [(i, i ^ side) for i in range(groups)]),
        ("along_z", "z", [(i, i ^ 1) for i in range(depth)]),
    )

    def exchange(rows):
        with jax.named_scope("exchange"):
            rows = lax.all_to_all(rows.reshape(chip_count, 1, -1), chips, 0, 0, tiled=True)
        return rows.reshape(-1, tile)

    parts = [terms[0]]
    for m, (name, axis, pairs) in enumerate(along):
        with jax.named_scope("terms_" + name):
            parts.append(lax.ppermute(terms[1 + m], axis, pairs))
    gram_pieces = exchange(gram_terms)
    with jax.named_scope("combine_terms"):
        both = combine(gram_pieces, parts, chip_count)
    both = exchange(both)
    with jax.named_scope("unpack_sums"):
        near_gram, copies = unpack(both, gram_chunk, chunk, kinds)
    with jax.named_scope("swap_gram"):
        far_gram = lax.ppermute(near_gram, "core", swap)
    quarter = exchange(copies)
    with jax.named_scope("factor_first"):
        *first, rest_a, rest_rows = factor_first(place, near_gram, far_gram, panel, width // 2)
    quarter, rest_a, rest_rows = lax.optimization_barrier((quarter, rest_a, rest_rows))
    near = []
    for name, axis, pairs in along:
        with jax.named_scope("quarters_" + name):
            near.append(lax.ppermute(quarter, axis, pairs))
    with jax.named_scope("swap_quarter"):
        far = [lax.ppermute(quarter, "core", swap)]
    with jax.named_scope("factor_rest"):
        rest = list(factor_rest(rest_a, rest_rows))
    *near, rest[1] = lax.optimization_barrier((*near, rest[1]))
    with jax.named_scope("swap_quarters"):
        far += [lax.ppermute(part, "core", swap) for part in near]
    near = [quarter, *near]
    with jax.named_scope("back_substitute"):
        mixed, r_rows = back(place, first, rest, picked)
    with jax.named_scope("apply_factor"):
        updated, coupling = finish(place, mixed, near, far, trailing)
    return (r_rows, coupling, updated)


def solution(mesh):
    groups, members = mesh.devices.shape
    split = Mesh(mesh.devices.reshape(groups, members // 2, 2), ("grp", "z", "core"))
    rows = P(("grp", "z", "core"))
    return jax.shard_map(
        local,
        mesh=split,
        in_specs=(P(("grp", "z", "core"), None), P(("grp", "z", "core"), None), rows),
        out_specs=(P(("z", "core"), None), P(("z", "core"), None), P(("grp", "z", "core"), None)),
        check_vma=False,
    )
```

time: 105 us -> 95.9 us (0.913)
  blocking collectives: 60.8 us -> 37.7 us
  starting transfers between devices: 6.77 us -> 18.1 us
  waiting for transfers between devices: 2.18 us -> 8.36 us
  local copies, waits for them, and re-layouts: 7.79 us -> 2.18 us
  Pallas kernels: 26.7 us -> 28.4 us
    all_to_all x2, blocking collectives: 60.8 us -> 37.7 us  [exchange(): lax.all_to_all(rows.reshape(chip_count, 1, -1), chips, 0, 0, tiled=True)]
    unnamed x16 -> x8, local copies, waits for them, and re-layouts: 6.66 us -> 0.97 us
    ppermute x7 -> x10, starting transfers between devices: 1.9 us -> 7.55 us  [the longest x3 4.31 us: local(): parts.append(lax.ppermute(terms[1 + m], axis, pairs))]
    all_to_all x0 -> x1, starting transfers between devices: none -> 4.94 us  [exchange(): lax.all_to_all(rows.reshape(chip_count, 1, -1), chips, 0, 0, tiled=True)]
    ppermute x7 -> x10, waiting for transfers between devices: 0.02 us -> 4.02 us  [the longest x3 4 us: local(): near.append(lax.ppermute(quarter, axis, pairs))]
    all_to_all x0 -> x1, waiting for transfers between devices: none -> 2.96 us  [exchange(): lax.all_to_all(rows.reshape(chip_count, 1, -1), chips, 0, 0, tiled=True)]
    pallas_call x4 -> x5, Pallas kernels: 19.4 us -> 21 us  [the longest x1 9.37 us: factor_first(): pl.pallas_call(factor_first_kernel, out_shape=factor_shapes(width, done,...]
  transfers between devices with their start and end apart: 11 -> 15, of which waited for: 2 -> 4; matrix products, arithmetic and copies ran while one was open for 0% -> 0% of each run, Pallas kernels for 18% -> 21%
where the time goes in v4:
time: 95.9 us; the launch traced here: 95.5 us
  blocking collectives  37.7 us (39%)
  Pallas kernels  28.4 us (30%)
  starting transfers between devices  18.1 us (19%)
  waiting for transfers between devices  8.36 us (9%)
  local copies, waits for them, and re-layouts  2.18 us (2%)
    all_to_all x2, blocking collectives, exchange(): lax.all_to_all(rows.reshape(chip_count, 1, -1), chips, 0, 0, tiled=True)  37.7 us
    pallas_call x1, Pallas kernels, factor_first(): pl.pallas_call(factor_first_kernel, out_shape=factor_shapes(width, done,...  9.37 us
    pallas_call x1, Pallas kernels, factor_rest(): pl.pallas_call(factor_rest_kernel, out_shape=factor_shapes(width, width,...  7.59 us
    all_to_all x1, starting transfers between devices, exchange(): lax.all_to_all(rows.reshape(chip_count, 1, -1), chips, 0, 0, tiled=True)  4.94 us
    ppermute x3, starting transfers between devices, local(): parts.append(lax.ppermute(terms[1 + m], axis, pairs))  4.31 us
    pallas_call x1, Pallas kernels, finish(): pl.pallas_call(finish_kernel, out_shape=(jax.ShapeDtypeStruct((own, trail...  4.29 us
    ppermute x3, waiting for transfers between devices, local(): near.append(lax.ppermute(quarter, axis, pairs))  4 us
    ppermute x1, starting transfers between devices, local(): far_gram = lax.ppermute(near_gram, 'core', swap)  3.57 us
  transfers between devices with their start and end apart: 15, of which 4 were waited for; matrix products, arithmetic and copies ran while one was open for 0% of the time, Pallas kernels for 21%

profile of v4, /device:TPU:1, one launch (start us, length us, event | category | flops | bytes accessed | tf_op | source)
XLA Modules:
  0.0 95.5 jit_solution(9002680186848441973)
XLA Ops:
  0.6 0.0 copy-start
  0.6 1.1 %constant_dynamic-slice_fusion = f32[128,896]{1,0:T(8,128)S(1)} fusion(f32[128,1792]{1,0:T(8,128)} %refs_8_.1, s32[]{:T(128)S(6)} %select_n.31), kind=kLoop, calls=%fused_computation | loop fusion | bytes 917508 | tf_op jit(solution)/shard_map/dynamic_slice | solution.py:423
  1.8 0.0 copy-start.3
  1.8 1.5 %collective-permute-start.1 = (f32[128,896]{1,0:T(8,128)S(1)}, f32[128,896]{1,0:T(8,128)S(1)}, u32[]{:S(2)}, u32[]{:S(2)}) collective-permute-start(f32[128,896]{1,0:T(8,128)S(1)} %constant_dynamic-slice_fusion), channel_id=1, source_target_pairs={{0,1},{1,0},{2,3},{3,2},{4,5},{5,4},{6,7},{7,6},{8,9},{9,8},{10,11... | collective-permute-start | bytes 1376264 | tf_op jit(solution)/shard_map/swap_inputs/ppermute | solution.py:427
  3.3 0.1 collective-permute-start
  3.4 0.0 copy-done.3
  3.4 0.5 collective-permute-start.2
  3.9 0.1 stack.27.place_ref
  3.9 0.8 collective-permute-done.2.far_counts_ref
  4.7 0.6 collective-permute-done.other_ref
  5.3 0.0 collective-permute-done.1.far_ref
  5.3 0.0 copy-done
  5.3 0.0 copy-start.1
  5.3 0.9 copy-done.1
  6.3 3.0 %local_products.1 = (f32[896,128]{1,0:T(8,128)S(1)}, f32[896,128]{1,0:T(8,128)S(1)}, f32[896,128]{1,0:T(8,128)S(1)}, f32[896,128]{1,0:T(8,128)S(1)}, f32[640,128]{1,0:T(8,128)S(1)}) custom-call(s32[6]{0:T(128)S(1)} %stack.27.place_ref, f32[128,512]{1,0:T(8,128)S(1)} %copy-done.1, f32[128,512]{1,0:T(8,128)S(1)} %collective-permute-done.other_ref, ...), custom_call_target="tpu_custom_call" | custom-call | tf_op jit(solution)/shard_map/local_products/pallas_call | solution.py:107
  9.3 1.4 %collective-permute-start.3 = (f32[896,128]{1,0:T(8,128)S(1)}, f32[896,128]{1,0:T(8,128)S(1)}, u32[]{:S(2)}, u32[]{:S(2)}) collective-permute-start(f32[896,128]{1,0:T(8,128)S(1)} %get-tuple-element.31), channel_id=1, source_target_pairs={{0,8},{8,0},{16,24},{24,16},{32,40},{40,32},{48,56},{56,48},{64,72... | collective-permute-start | bytes 1376264 | tf_op jit(solution)/shard_map/terms_along_x/ppermute | solution.py:446
  10.7 1.3 %collective-permute-start.4 = (f32[896,128]{1,0:T(8,128)S(1)}, f32[896,128]{1,0:T(8,128)S(1)}, u32[]{:S(2)}, u32[]{:S(2)}) collective-permute-start(f32[896,128]{1,0:T(8,128)S(1)} %get-tuple-element.32), channel_id=1, source_target_pairs={{0,32},{8,40},{16,48},{24,56},{32,0},{40,8},{48,16},{56,24},{64,96... | collective-permute-start | bytes 1376264 | tf_op jit(solution)/shard_map/terms_along_y/ppermute | solution.py:446
  12.0 1.6 %collective-permute-start.5 = (f32[896,128]{1,0:T(8,128)S(1)}, f32[896,128]{1,0:T(8,128)S(1)}, u32[]{:S(2)}, u32[]{:S(2)}) collective-permute-start(f32[896,128]{1,0:T(8,128)S(1)} %get-tuple-element.33), channel_id=1, source_target_pairs={{0,2},{2,0},{4,6},{6,4},{1,3},{3,1},{5,7},{7,5},{8,10},{10,8},{12,... | collective-permute-start | bytes 1376264 | tf_op jit(solution)/shard_map/terms_along_z/ppermute | solution.py:446
  13.6 19.6 %all_to_all.15 = f32[64,1,1280]{2,1,0:T(1,128)S(1)} all-to-all(f32[64,1,1280]{2,1,0:T(1,128)S(1)} %bitcast.21), channel_id=1, replica_groups=mesh['grp'=16,'z'=4,'core'=2] {'grp','z'}, dimensions={0} | all-to-all | bytes 655360 | tf_op jit(solution)/shard_map/exchange/all_to_all | solution.py:440
  33.2 0.0 collective-permute-done.3.refs_1_
  33.2 0.0 collective-permute-done.4.refs_2_
  33.2 0.0 collective-permute-done.5.refs_3_
  33.2 0.2 combine_terms.1
  33.4 18.1 %all_to_all.16 = f32[64,1,3072]{2,1,0:T(1,128)S(1)} all-to-all(f32[64,1,3072]{2,1,0:T(1,128)S(1)} %bitcast.14), channel_id=1, replica_groups=mesh['grp'=16,'z'=4,'core'=2] {'grp','z'}, dimensions={0} | all-to-all | bytes 1572864 | tf_op jit(solution)/shard_map/exchange/all_to_all | solution.py:440
  51.5 0.9 unpack_sums.1
  52.3 3.6 %collective-permute-start.6 = (f32[640,128]{1,0:T(8,128)S(1)}, f32[640,128]{1,0:T(8,128)S(1)}, u32[]{:S(2)}, u32[]{:S(2)}) collective-permute-start(f32[640,128]{1,0:T(8,128)S(1)} %get-tuple-element.34.near_ref), channel_id=1, source_target_pairs={{0,1},{1,0},{2,3},{3,2},{4,5},{5,4},{6,7},{7,6},{8,9},{9,8},{10,11... | collective-permute-start | bytes 983048 | tf_op jit(solution)/shard_map/swap_gram/ppermute | solution.py:454
  55.9 0.0 copy-start.2
  55.9 4.9 %all-to-all-start.2 = ((f32[64,1,1792]{2,1,0:T(1,128)}), f32[64,1,1792]{2,1,0:T(1,128)S(1)}, u32[]{:S(2)}, u32[]{:S(2)}) async-start(f32[64,1,1792]{2,1,0:T(1,128)} %bitcast.11), calls=%async_computation.2 | async-start | bytes 917504 | tf_op jit(solution)/shard_map/exchange/all_to_all | solution.py:440
  60.9 0.0 collective-permute-done.6.far_ref
  60.9 0.0 copy-done.2
  60.9 9.4 %factor_first.1 = (f32[256,512]{1,0:T(8,128)S(1)}, f32[256,128]{1,0:T(8,128)S(1)}, f32[128,256]{1,0:T(8,128)S(1)}, f32[256,256]{1,0:T(8,128)S(1)}, f32[128,256]{1,0:T(8,128)S(1)}) custom-call(s32[6]{0:T(128)S(1)} %stack.27.place_ref, f32[640,128]{1,0:T(8,128)S(1)} %get-tuple-element.34.near_ref, f32[640,128]{1,0:T(8,128)S(1)} %collective-permute-done.6.far_ref, ...), custom_call_target="tpu_custom_call" | custom-call | flops 10000000000 | bytes 4000000 | tf_op jit(solution)/shard_map/factor_first/pallas_call | solution.py:281
  70.3 3.0 %all-to-all-done.2 = f32[64,1,1792]{2,1,0:T(1,128)S(1)} async-done(((f32[64,1,1792]{2,1,0:T(1,128)}), f32[64,1,1792]{2,1,0:T(1,128)S(1)}, u32[]{:S(2)}, u32[]{:S(2)}) %all-to-all-start.2) | async-done | bytes 458784 | tf_op jit(solution)/shard_map/exchange/all_to_all | solution.py:440
  73.2 1.0 %collective-permute-start.10 = (f32[896,128]{1,0:T(8,128)S(1)}, f32[896,128]{1,0:T(8,128)S(1)}, u32[]{:S(2)}, u32[]{:S(2)}) collective-permute-start(f32[896,128]{1,0:T(8,128)S(1)} %bitcast.15), channel_id=1, source_target_pairs={{0,1},{1,0},{2,3},{3,2},{4,5},{5,4},{6,7},{7,6},{8,9},{9,8},{10,11... | collective-permute-start | bytes 1376264 | tf_op jit(solution)/shard_map/swap_quarter/ppermute | solution.py:464
  74.2 0.4 collective-permute-start.9
  74.6 0.0 collective-permute-start.8
  74.6 0.2 collective-permute-start.7
  74.9 7.6 %factor_rest.1 = (f32[256,256]{1,0:T(8,128)S(1)}, f32[256,128]{1,0:T(8,128)S(1)}, f32[128,256]{1,0:T(8,128)S(1)}) custom-call(f32[256,256]{1,0:T(8,128)S(1)} %get-tuple-element.41.a_in, f32[128,256]{1,0:T(8,128)S(1)} %get-tuple-element.42.rows_in), custom_call_target="tpu_custom_call" | custom-call | flops 10000000000 | bytes 2000000 | tf_op jit(solution)/shard_map/factor_rest/pallas_call | solution.py:299
  82.5 3.9 %collective-permute-done.9.refs_3_ = f32[896,128]{1,0:T(8,128)S(1)} collective-permute-done((f32[896,128]{1,0:T(8,128)S(1)}, f32[896,128]{1,0:T(8,128)S(1)}, u32[]{:S(2)}, u32[]{:S(2)}) %collective-permute-start.9) | collective-permute-done | bytes 458784 | tf_op jit(solution)/shard_map/quarters_along_z/ppermute | solution.py:462
  86.4 0.0 collective-permute-done.8.refs_2_
  86.4 0.0 collective-permute-done.7.refs_1_
  86.5 1.1 %collective-permute-start.11 = (f32[896,128]{1,0:T(8,128)S(1)}, f32[896,128]{1,0:T(8,128)S(1)}, u32[]{:S(2)}, u32[]{:S(2)}) collective-permute-start(f32[896,128]{1,0:T(8,128)S(1)} %collective-permute-done.7.refs_1_), channel_id=1, source_target_pairs={{0,1},{1,0},{2,3},{3,2},{4,5},{5,4},{6,7},{7,6},{8,9},{9,8},{10,11... | collective-permute-start | bytes 1376264 | tf_op jit(solution)/shard_map/swap_quarters/ppermute | solution.py:469
  87.6 0.0 collective-permute-start.12
  87.6 0.5 collective-permute-start.13
  88.1 3.2 %back_substitute.1 = (f32[4,192,128]{2,1,0:T(8,128)S(1)}, f32[64,512]{1,0:T(8,128)}) custom-call(s32[6]{0:T(128)S(1)} %stack.27.place_ref, f32[256,512]{1,0:T(8,128)S(1)} %get-tuple-element.35.upper_a, f32[256,128]{1,0:T(8,128)S(1)} %get-tuple-element.36.tinv_a, f32[128,256]{1,0:T(8,128)S(1)} %get-tuple-element.37.y_a, ...), custom_call_target="tpu_custom_call" | custom-call | flops 4000000000 | bytes 2000000 | tf_op jit(solution)/shard_map/back_substitute/pallas_call | solution.py:346
  91.2 0.0 collective-permute-done.10.refs_4_
  91.2 0.0 collective-permute-done.11.refs_5_
  91.2 0.0 collective-permute-done.12.refs_6_
  91.2 0.0 collective-permute-done.13.refs_7_
  91.2 4.3 %apply_factor.1 = (f32[128,1792]{1,0:T(8,128)}, f32[64,1792]{1,0:T(8,128)}) custom-call(s32[6]{0:T(128)S(1)} %stack.27.place_ref, f32[4,192,128]{2,1,0:T(8,128)S(1)} %get-tuple-element.49.mixed_ref, f32[896,128]{1,0:T(8,128)S(1)} %bitcast.19, f32[896,128]{1,0:T(8,128)S(1)} %collective-permute-done.7.refs_1_, f32[896,128]{1,0:T(8,128)S(1)} %collective-permute-done.8.refs_2_, ...), custom_call_target="tpu_custom_call" | custom-call | tf_op jit(solution)/shard_map/apply_factor/pallas_call | solution.py:389
Async XLA Ops:
  0.6 4.7 %copy-start = (f32[128,1792]{1,0:T(8,128)S(1)}, f32[128,1792]{1,0:T(8,128)}, u32[]{:S(2)}) copy-start(f32[128,1792]{1,0:T(8,128)} %refs_8_.1) | copy-start | bytes 2752516
  1.8 1.6 %copy-start.3 = (s32[128]{0:T(128)S(1)}, s32[128]{0:T(128)}, u32[]{:S(2)}) copy-start(s32[128]{0:T(128)} %param.5) | copy-start | bytes 1540
  1.8 3.5 %collective-permute-start.1 = (f32[128,896]{1,0:T(8,128)S(1)}, f32[128,896]{1,0:T(8,128)S(1)}, u32[]{:S(2)}, u32[]{:S(2)}) collective-permute-start(f32[128,896]{1,0:T(8,128)S(1)} %constant_dynamic-slice_fusion), channel_id=1, source_target_pairs={{0,1},{1,0},{2,3},{3,2},{4,5},{5,4},{6,7},{7,6},{8,9},{9,8},{10,11... | collective-permute-start | bytes 1376264 | tf_op jit(solution)/shard_map/swap_inputs/ppermute | solution.py:427
  3.3 2.0 %collective-permute-start = (f32[128,512]{1,0:T(8,128)}, f32[128,512]{1,0:T(8,128)S(1)}, u32[]{:S(2)}, u32[]{:S(2)}) collective-permute-start(f32[128,512]{1,0:T(8,128)} %panel_ref.3), channel_id=1, source_target_pairs={{0,1},{1,0},{2,3},{3,2},{4,5},{5,4},{6,7},{7,6},{8,9},{9,8},{10,11... | collective-permute-start | bytes 786440 | tf_op jit(solution)/shard_map/swap_inputs/ppermute | solution.py:426
  3.4 1.3 %collective-permute-start.2 = (s32[1,128]{1,0:T(1,128)S(1)}, s32[1,128]{1,0:T(1,128)S(1)}, u32[]{:S(2)}, u32[]{:S(2)}) collective-permute-start(s32[1,128]{1,0:T(1,128)S(1)} %bitcast.22), channel_id=1, source_target_pairs={{0,1},{1,0},{2,3},{3,2},{4,5},{5,4},{6,7},{7,6},{8,9},{9,8},{10,11... | collective-permute-start | bytes 1544 | tf_op jit(solution)/shard_map/swap_inputs/ppermute | solution.py:425
  5.3 1.0 copy-start.1
  9.3 23.9 %collective-permute-start.3 = (f32[896,128]{1,0:T(8,128)S(1)}, f32[896,128]{1,0:T(8,128)S(1)}, u32[]{:S(2)}, u32[]{:S(2)}) collective-permute-start(f32[896,128]{1,0:T(8,128)S(1)} %get-tuple-element.31), channel_id=1, source_target_pairs={{0,8},{8,0},{16,24},{24,16},{32,40},{40,32},{48,56},{56,48},{64,72... | collective-permute-start | bytes 1376264 | tf_op jit(solution)/shard_map/terms_along_x/ppermute | solution.py:446
  10.7 22.6 %collective-permute-start.4 = (f32[896,128]{1,0:T(8,128)S(1)}, f32[896,128]{1,0:T(8,128)S(1)}, u32[]{:S(2)}, u32[]{:S(2)}) collective-permute-start(f32[896,128]{1,0:T(8,128)S(1)} %get-tuple-element.32), channel_id=1, source_target_pairs={{0,32},{8,40},{16,48},{24,56},{32,0},{40,8},{48,16},{56,24},{64,96... | collective-permute-start | bytes 1376264 | tf_op jit(solution)/shard_map/terms_along_y/ppermute | solution.py:446
  12.0 21.3 %collective-permute-start.5 = (f32[896,128]{1,0:T(8,128)S(1)}, f32[896,128]{1,0:T(8,128)S(1)}, u32[]{:S(2)}, u32[]{:S(2)}) collective-permute-start(f32[896,128]{1,0:T(8,128)S(1)} %get-tuple-element.33), channel_id=1, source_target_pairs={{0,2},{2,0},{4,6},{6,4},{1,3},{3,1},{5,7},{7,5},{8,10},{10,8},{12,... | collective-permute-start | bytes 1376264 | tf_op jit(solution)/shard_map/terms_along_z/ppermute | solution.py:446
  52.3 8.5 %collective-permute-start.6 = (f32[640,128]{1,0:T(8,128)S(1)}, f32[640,128]{1,0:T(8,128)S(1)}, u32[]{:S(2)}, u32[]{:S(2)}) collective-permute-start(f32[640,128]{1,0:T(8,128)S(1)} %get-tuple-element.34.near_ref), channel_id=1, source_target_pairs={{0,1},{1,0},{2,3},{3,2},{4,5},{5,4},{6,7},{7,6},{8,9},{9,8},{10,11... | collective-permute-start | bytes 983048 | tf_op jit(solution)/shard_map/swap_gram/ppermute | solution.py:454
  55.9 5.0 %copy-start.2 = (f32[128,512]{1,0:T(8,128)S(1)}, f32[128,512]{1,0:T(8,128)}, u32[]{:S(2)}) copy-start(f32[128,512]{1,0:T(8,128)} %panel_ref.3) | copy-start | bytes 786436
  55.9 17.3 %all-to-all-start.2 = ((f32[64,1,1792]{2,1,0:T(1,128)}), f32[64,1,1792]{2,1,0:T(1,128)S(1)}, u32[]{:S(2)}, u32[]{:S(2)}) async-start(f32[64,1,1792]{2,1,0:T(1,128)} %bitcast.11), calls=%async_computation.2 | async-start | bytes 917504 | tf_op jit(solution)/shard_map/exchange/all_to_all | solution.py:440
  73.2 18.0 %collective-permute-start.10 = (f32[896,128]{1,0:T(8,128)S(1)}, f32[896,128]{1,0:T(8,128)S(1)}, u32[]{:S(2)}, u32[]{:S(2)}) collective-permute-start(f32[896,128]{1,0:T(8,128)S(1)} %bitcast.15), channel_id=1, source_target_pairs={{0,1},{1,0},{2,3},{3,2},{4,5},{5,4},{6,7},{7,6},{8,9},{9,8},{10,11... | collective-permute-start | bytes 1376264 | tf_op jit(solution)/shard_map/swap_quarter/ppermute | solution.py:464
  74.2 12.2 %collective-permute-start.9 = (f32[896,128]{1,0:T(8,128)S(1)}, f32[896,128]{1,0:T(8,128)S(1)}, u32[]{:S(2)}, u32[]{:S(2)}) collective-permute-start(f32[896,128]{1,0:T(8,128)S(1)} %bitcast.16), channel_id=1, source_target_pairs={{0,2},{2,0},{4,6},{6,4},{1,3},{3,1},{5,7},{7,5},{8,10},{10,8},{12,... | collective-permute-start | bytes 1376264 | tf_op jit(solution)/shard_map/quarters_along_z/ppermute | solution.py:462
  74.6 11.8 %collective-permute-start.8 = (f32[896,128]{1,0:T(8,128)S(1)}, f32[896,128]{1,0:T(8,128)S(1)}, u32[]{:S(2)}, u32[]{:S(2)}) collective-permute-start(f32[896,128]{1,0:T(8,128)S(1)} %bitcast.17), channel_id=1, source_target_pairs={{0,32},{8,40},{16,48},{24,56},{32,0},{40,8},{48,16},{56,24},{64,96... | collective-permute-start | bytes 1376264 | tf_op jit(solution)/shard_map/quarters_along_y/ppermute | solution.py:462
  74.6 11.8 %collective-permute-start.7 = (f32[896,128]{1,0:T(8,128)S(1)}, f32[896,128]{1,0:T(8,128)S(1)}, u32[]{:S(2)}, u32[]{:S(2)}) collective-permute-start(f32[896,128]{1,0:T(8,128)S(1)} %bitcast.18), channel_id=1, source_target_pairs={{0,8},{8,0},{16,24},{24,16},{32,40},{40,32},{48,56},{56,48},{64,72... | collective-permute-start | bytes 1376264 | tf_op jit(solution)/shard_map/quarters_along_x/ppermute | solution.py:462
  86.5 4.8 %collective-permute-start.11 = (f32[896,128]{1,0:T(8,128)S(1)}, f32[896,128]{1,0:T(8,128)S(1)}, u32[]{:S(2)}, u32[]{:S(2)}) collective-permute-start(f32[896,128]{1,0:T(8,128)S(1)} %collective-permute-done.7.refs_1_), channel_id=1, source_target_pairs={{0,1},{1,0},{2,3},{3,2},{4,5},{5,4},{6,7},{7,6},{8,9},{9,8},{10,11... | collective-permute-start | bytes 1376264 | tf_op jit(solution)/shard_map/swap_quarters/ppermute | solution.py:469
  87.6 3.7 %collective-permute-start.12 = (f32[896,128]{1,0:T(8,128)S(1)}, f32[896,128]{1,0:T(8,128)S(1)}, u32[]{:S(2)}, u32[]{:S(2)}) collective-permute-start(f32[896,128]{1,0:T(8,128)S(1)} %collective-permute-done.8.refs_2_), channel_id=1, source_target_pairs={{0,1},{1,0},{2,3},{3,2},{4,5},{5,4},{6,7},{7,6},{8,9},{9,8},{10,11... | collective-permute-start | bytes 1376264 | tf_op jit(solution)/shard_map/swap_quarters/ppermute | solution.py:469
  87.6 3.7 %collective-permute-start.13 = (f32[896,128]{1,0:T(8,128)S(1)}, f32[896,128]{1,0:T(8,128)S(1)}, u32[]{:S(2)}, u32[]{:S(2)}) collective-permute-start(f32[896,128]{1,0:T(8,128)S(1)} %collective-permute-done.9.refs_3_), channel_id=1, source_target_pairs={{0,1},{1,0},{2,3},{3,2},{4,5},{5,4},{6,7},{7,6},{8,9},{9,8},{10,11... | collective-permute-start | bytes 1376264 | tf_op jit(solution)/shard_map/swap_quarters/ppermute | solution.py:469

commit v5 on v4

--- a/solution.py
+++ b/solution.py
@@ -132,65 +132,78 @@
 
 
 def combine_kernel(gram_ref, *refs, chip_count):
-    parts, out_ref, four = refs[:classes], refs[classes], refs[classes + 1]
+    parts, out_ref = refs[:classes], refs[classes]
     size = gram_ref.shape[0] // chip_count
     chunk = parts[0].shape[0] // chip_count
-    total = gram_ref[0 : 4 * size, :]
-    for at in range(4 * size, chip_count * size, 4 * size):
-        total = total + gram_ref[at : at + 4 * size, :]
-    four[...] = total
-    gram = four[0:size, :]
-    for at in range(size, 4 * size, size):
-        gram = gram + four[at : at + size, :]
     for q in range(chip_count):
         side = slice(q * chunk, (q + 1) * chunk)
         cross = (parts[0][side, :] + parts[1][side, :]) + (parts[2][side, :] + parts[3][side, :])
+        gram = gram_ref[q * size : (q + 1) * size, :]
         out_ref[q * (size + chunk) : (q + 1) * (size + chunk), :] = jnp.concatenate([gram, cross], 0)
 
 
-def combine(gram_pieces, parts, chip_count):
-    vmem = pl.BlockSpec(memory_space=pltpu.VMEM)
-    gram_rows, rows = gram_pieces.shape[0], parts[0].shape[0]
+def combine(gram, parts, chip_count):
+    vmem = pl.BlockSpec(memory_space=pltpu.VMEM)
     return pl.pallas_call(
         functools.partial(combine_kernel, chip_count=chip_count),
-        out_shape=jax.ShapeDtypeStruct((gram_rows + rows, tile), jnp.float32),
+        out_shape=jax.ShapeDtypeStruct((gram.shape[0] + parts[0].shape[0], tile), jnp.float32),
         in_specs=[vmem] * (1 + classes),
         out_specs=vmem,
-        scratch_shapes=[pltpu.VMEM((4 * gram_rows // chip_count, tile), jnp.float32)],
         compiler_params=pltpu.CompilerParams(vmem_limit_bytes=16 * 1024 * 1024),
-    )(gram_pieces, *parts)
-
-
-def unpack_kernel(mixed_ref, gram_ref, copies_ref, sums, *, size, chunk, kinds):
-    both = size + chunk
+    )(gram, *parts)
+
+
+def sum_kernel(pieces_ref, copies_ref, *, size, kinds):
+    both = pieces_ref.shape[0] // len(kinds)
+    totals = []
     for k in range(classes):
         total = None
         for q, kind in enumerate(kinds):
             if kind == k:
-                piece = mixed_ref[q * both : (q + 1) * both, :]
+                piece = pieces_ref[q * both : (q + 1) * both, :]
                 total = piece if total is None else total + piece
-        sums[...] = total
-        cross = sums[size:, :]
+        totals.append(total)
+    gram = (totals[0] + totals[1]) + (totals[2] + totals[3])
+    is_gram = lax.broadcasted_iota(jnp.int32, (both, tile), 0) < size
+    for k in range(classes):
+        copy = jnp.where(is_gram, gram, totals[k])
         for q, kind in enumerate(kinds):
             if kind == k:
-                copies_ref[q * chunk : (q + 1) * chunk, :] = cross
-    for q in range(len(kinds)):
-        gram_ref[q * size : (q + 1) * size, :] = mixed_ref[q * both : q * both + size, :]
-
-
-def unpack(mixed, size, chunk, kinds):
-    vmem = pl.BlockSpec(memory_space=pltpu.VMEM)
-    return pl.pallas_call(
-        functools.partial(unpack_kernel, size=size, chunk=chunk, kinds=kinds),
+                copies_ref[q * both : (q + 1) * both, :] = copy
+
+
+def sum_pieces(pieces, size, kinds):
+    vmem = pl.BlockSpec(memory_space=pltpu.VMEM)
+    return pl.pallas_call(
+        functools.partial(sum_kernel, size=size, kinds=kinds),
+        out_shape=jax.ShapeDtypeStruct(pieces.shape, jnp.float32),
+        in_specs=[vmem],
+        out_specs=vmem,
+        compiler_params=pltpu.CompilerParams(vmem_limit_bytes=16 * 1024 * 1024),
+    )(pieces)
+
+
+def unpack_kernel(copies_ref, gram_ref, quarter_ref, *, chip_count):
+    size = gram_ref.shape[0] // chip_count
+    chunk = quarter_ref.shape[0] // chip_count
+    both = size + chunk
+    for q in range(chip_count):
+        gram_ref[q * size : (q + 1) * size, :] = copies_ref[q * both : q * both + size, :]
+        quarter_ref[q * chunk : (q + 1) * chunk, :] = copies_ref[q * both + size : (q + 1) * both, :]
+
+
+def unpack(copies, chip_count, size, chunk):
+    vmem = pl.BlockSpec(memory_space=pltpu.VMEM)
+    return pl.pallas_call(
+        functools.partial(unpack_kernel, chip_count=chip_count),
         out_shape=(
-            jax.ShapeDtypeStruct((len(kinds) * size, tile), jnp.float32),
-            jax.ShapeDtypeStruct((len(kinds) * chunk, tile), jnp.float32),
+            jax.ShapeDtypeStruct((chip_count * size, tile), jnp.float32),
+            jax.ShapeDtypeStruct((chip_count * chunk, tile), jnp.float32),
         ),
         in_specs=[vmem],
         out_specs=(vmem, vmem),
-        scratch_shapes=[pltpu.VMEM((size + chunk, tile), jnp.float32)],
         compiler_params=pltpu.CompilerParams(vmem_limit_bytes=16 * 1024 * 1024),
-    )(mixed)
+    )(copies)
 
 
 def factor_levels(a_ref, rows_ref, work, upper_ref, tinv, y_ref):
@@ -429,10 +442,23 @@
         *terms, gram_terms = products(
             place, panel, other_panel, trailing, far_trail, count_row, far_counts, own * groups * members
         )
+    line = [(i * 2 + c, (i ^ (3 if c else 1)) * 2 + c) for i in range(side) for c in range(2)]
+    across = [
+        ((i * side + j) * 2 + c, ((i ^ (3 if c else 1)) * side + j) * 2 + c)
+        for i in range(groups // side)
+        for j in range(side)
+        for c in range(2)
+    ]
+    inner = [
+        ((j * side + i) * 2 + c, (j * side + (i ^ (3 if c else 1))) * 2 + c)
+        for i in range(side)
+        for j in range(groups // side)
+        for c in range(2)
+    ]
     along = (
-        ("along_x", "grp", [(i, i ^ 1) for i in range(groups)]),
-        ("along_y", "grp", [(i, i ^ side) for i in range(groups)]),
-        ("along_z", "z", [(i, i ^ 1) for i in range(depth)]),
+        ("along_x", ("grp", "core"), inner),
+        ("along_y", ("grp", "core"), across),
+        ("along_z", ("z", "core"), line),
     )
 
     def exchange(rows):
@@ -444,30 +470,30 @@
     for m, (name, axis, pairs) in enumerate(along):
         with jax.named_scope("terms_" + name):
             parts.append(lax.ppermute(terms[1 + m], axis, pairs))
-    gram_pieces = exchange(gram_terms)
     with jax.named_scope("combine_terms"):
-        both = combine(gram_pieces, parts, chip_count)
-    both = exchange(both)
+        pieces = combine(gram_terms, parts, chip_count)
+    pieces = exchange(pieces)
+    with jax.named_scope("sum_pieces"):
+        copies = sum_pieces(pieces, gram_chunk, kinds)
+    copies = exchange(copies)
     with jax.named_scope("unpack_sums"):
-        near_gram, copies = unpack(both, gram_chunk, chunk, kinds)
+        near_gram, quarter = unpack(copies, chip_count, gram_chunk, chunk)
     with jax.named_scope("swap_gram"):
         far_gram = lax.ppermute(near_gram, "core", swap)
-    quarter = exchange(copies)
-    with jax.named_scope("factor_first"):
-        *first, rest_a, rest_rows = factor_first(place, near_gram, far_gram, panel, width // 2)
-    quarter, rest_a, rest_rows = lax.optimization_barrier((quarter, rest_a, rest_rows))
     near = []
     for name, axis, pairs in along:
         with jax.named_scope("quarters_" + name):
             near.append(lax.ppermute(quarter, axis, pairs))
     with jax.named_scope("swap_quarter"):
         far = [lax.ppermute(quarter, "core", swap)]
-    with jax.named_scope("factor_rest"):
-        rest = list(factor_rest(rest_a, rest_rows))
-    *near, rest[1] = lax.optimization_barrier((*near, rest[1]))
+    with jax.named_scope("factor_first"):
+        *first, rest_a, rest_rows = factor_first(place, near_gram, far_gram, panel, width // 2)
+    *near, rest_a, rest_rows = lax.optimization_barrier((*near, rest_a, rest_rows))
     with jax.named_scope("swap_quarters"):
         far += [lax.ppermute(part, "core", swap) for part in near]
     near = [quarter, *near]
+    with jax.named_scope("factor_rest"):
+        rest = factor_rest(rest_a, rest_rows)
     with jax.named_scope("back_substitute"):
         mixed, r_rows = back(place, first, rest, picked)
     with jax.named_scope("apply_factor"):

time: 95.9 us -> 92.6 us (0.966)
  blocking collectives: 37.7 us -> 35.6 us
  waiting for transfers between devices: 8.36 us -> 7.27 us
    ppermute x3, waiting for transfers between devices: 0.01 us -> 5.86 us  [local(): parts.append(lax.ppermute(terms[1 + m], axis, pairs))]
    all_to_all x1 -> x0, starting transfers between devices: 4.94 us -> none  [exchange(): lax.all_to_all(rows.reshape(chip_count, 1, -1), chips, 0, 0, tiled=True)]
    ppermute x3, starting transfers between devices: 4.31 us -> 9.13 us  [local(): parts.append(lax.ppermute(terms[1 + m], axis, pairs))]
    ppermute x3, waiting for transfers between devices: 4 us -> 0.01 us  [local(): near.append(lax.ppermute(quarter, axis, pairs))]
    all_to_all x1 -> x0, waiting for transfers between devices: 2.96 us -> none  [exchange(): lax.all_to_all(rows.reshape(chip_count, 1, -1), chips, 0, 0, tiled=True)]
    all_to_all x2, blocking collectives: 37.7 us -> 35.6 us  [exchange(): lax.all_to_all(rows.reshape(chip_count, 1, -1), chips, 0, 0, tiled=True)]
    ppermute x3, starting transfers between devices: 0.6 us -> 2.33 us  [local(): near.append(lax.ppermute(quarter, axis, pairs))]
    ppermute x1, starting transfers between devices: 3.57 us -> 4.56 us  [local(): far_gram = lax.ppermute(near_gram, 'core', swap)]
  transfers between devices with their start and end apart: 15 -> 14, of which waited for: 4 -> 4; matrix products, arithmetic and copies ran while one was open for 0% -> 0% of each run, Pallas kernels for 21% -> 22%
where the time goes in v5:
time: 92.6 us; the launch traced here: 92.4 us
  blocking collectives  35.6 us (38%)
  Pallas kernels  27.8 us (30%)
  starting transfers between devices  18.9 us (20%)
  waiting for transfers between devices  7.27 us (8%)
  local copies, waits for them, and re-layouts  2.18 us (2%)
    all_to_all x2, blocking collectives, exchange(): lax.all_to_all(rows.reshape(chip_count, 1, -1), chips, 0, 0, tiled=True)  35.6 us
    pallas_call x1, Pallas kernels, factor_first(): pl.pallas_call(factor_first_kernel, out_shape=factor_shapes(width, done,...  9.37 us
    ppermute x3, starting transfers between devices, local(): parts.append(lax.ppermute(terms[1 + m], axis, pairs))  9.13 us
    pallas_call x1, Pallas kernels, factor_rest(): pl.pallas_call(factor_rest_kernel, out_shape=factor_shapes(width, width,...  7.59 us
    ppermute x3, waiting for transfers between devices, local(): parts.append(lax.ppermute(terms[1 + m], axis, pairs))  5.86 us
    ppermute x1, starting transfers between devices, local(): far_gram = lax.ppermute(near_gram, 'core', swap)  4.56 us
    pallas_call x1, Pallas kernels, finish(): pl.pallas_call(finish_kernel, out_shape=(jax.ShapeDtypeStruct((own, trail...  4.28 us
    pallas_call x1, Pallas kernels, back(): pl.pallas_call(back_kernel, out_shape=(jax.ShapeDtypeStruct((width // til...  3.16 us
  transfers between devices with their start and end apart: 14, of which 4 were waited for; matrix products, arithmetic and copies ran while one was open for 0% of the time, Pallas kernels for 22%

profile of v5, /device:TPU:1, one launch (start us, length us, event | category | flops | bytes accessed | tf_op | source)
XLA Modules:
  0.0 92.4 jit_solution(5372405263923413221)
XLA Ops:
  0.6 0.0 copy-start
  0.6 1.1 %constant_dynamic-slice_fusion = f32[128,896]{1,0:T(8,128)S(1)} fusion(f32[128,1792]{1,0:T(8,128)} %refs_8_.1, s32[]{:T(128)S(6)} %select_n.31), kind=kLoop, calls=%fused_computation | loop fusion | bytes 917508 | tf_op jit(solution)/shard_map/dynamic_slice | solution.py:436
  1.8 0.0 copy-start.3
  1.8 1.5 %collective-permute-start.1 = (f32[128,896]{1,0:T(8,128)S(1)}, f32[128,896]{1,0:T(8,128)S(1)}, u32[]{:S(2)}, u32[]{:S(2)}) collective-permute-start(f32[128,896]{1,0:T(8,128)S(1)} %constant_dynamic-slice_fusion), channel_id=1, source_target_pairs={{0,1},{1,0},{2,3},{3,2},{4,5},{5,4},{6,7},{7,6},{8,9},{9,8},{10,11... | collective-permute-start | bytes 1376264 | tf_op jit(solution)/shard_map/swap_inputs/ppermute | solution.py:440
  3.3 0.1 collective-permute-start
  3.4 0.0 copy-done.3
  3.4 0.5 collective-permute-start.2
  3.9 0.1 stack.27.place_ref
  3.9 0.8 collective-permute-done.2.far_counts_ref
  4.7 0.6 collective-permute-done.other_ref
  5.3 0.0 collective-permute-done.1.far_ref
  5.3 0.0 copy-done
  5.3 0.0 copy-start.1
  5.3 0.9 %copy-done.1 = f32[128,512]{1,0:T(8,128)S(1)} copy-done((f32[128,512]{1,0:T(8,128)S(1)}, f32[128,512]{1,0:T(8,128)}, u32[]{:S(2)}) %copy-start.1) | copy-done | bytes 262168
  6.3 3.0 %local_products.1 = (f32[896,128]{1,0:T(8,128)S(1)}, f32[896,128]{1,0:T(8,128)S(1)}, f32[896,128]{1,0:T(8,128)S(1)}, f32[896,128]{1,0:T(8,128)S(1)}, f32[640,128]{1,0:T(8,128)S(1)}) custom-call(s32[6]{0:T(128)S(1)} %stack.27.place_ref, f32[128,512]{1,0:T(8,128)S(1)} %copy-done.1, f32[128,512]{1,0:T(8,128)S(1)} %collective-permute-done.other_ref, ...), custom_call_target="tpu_custom_call" | custom-call | tf_op jit(solution)/shard_map/local_products/pallas_call | solution.py:107
  9.3 2.6 %collective-permute-start.3 = (f32[896,128]{1,0:T(8,128)S(1)}, f32[896,128]{1,0:T(8,128)S(1)}, u32[]{:S(2)}, u32[]{:S(2)}) collective-permute-start(f32[896,128]{1,0:T(8,128)S(1)} %get-tuple-element.29), channel_id=1, source_target_pairs={{0,8},{1,25},{32,40},{33,57},{64,72},{65,89},{96,104},{97,121},{8,... | collective-permute-start | bytes 1376264 | tf_op jit(solution)/shard_map/terms_along_x/ppermute | solution.py:472
  11.9 2.7 %collective-permute-start.4 = (f32[896,128]{1,0:T(8,128)S(1)}, f32[896,128]{1,0:T(8,128)S(1)}, u32[]{:S(2)}, u32[]{:S(2)}) collective-permute-start(f32[896,128]{1,0:T(8,128)S(1)} %get-tuple-element.30), channel_id=1, source_target_pairs={{0,32},{1,97},{8,40},{9,105},{16,48},{17,113},{24,56},{25,121},{32... | collective-permute-start | bytes 1376264 | tf_op jit(solution)/shard_map/terms_along_y/ppermute | solution.py:472
  14.7 3.8 %collective-permute-start.5 = (f32[896,128]{1,0:T(8,128)S(1)}, f32[896,128]{1,0:T(8,128)S(1)}, u32[]{:S(2)}, u32[]{:S(2)}) collective-permute-start(f32[896,128]{1,0:T(8,128)S(1)} %get-tuple-element.31), channel_id=1, source_target_pairs={{0,2},{1,7},{2,0},{3,5},{4,6},{5,3},{6,4},{7,1},{8,10},{9,15},{10,... | collective-permute-start | bytes 1376264 | tf_op jit(solution)/shard_map/terms_along_z/ppermute | solution.py:472
  18.4 0.0 collective-permute-done.3.refs_1_
  18.4 2.1 %collective-permute-done.4.refs_2_ = f32[896,128]{1,0:T(8,128)S(1)} collective-permute-done((f32[896,128]{1,0:T(8,128)S(1)}, f32[896,128]{1,0:T(8,128)S(1)}, u32[]{:S(2)}, u32[]{:S(2)}) %collective-permute-start.4) | collective-permute-done | bytes 458784 | tf_op jit(solution)/shard_map/terms_along_y/ppermute | solution.py:472
  20.5 3.8 %collective-permute-done.5.refs_3_ = f32[896,128]{1,0:T(8,128)S(1)} collective-permute-done((f32[896,128]{1,0:T(8,128)S(1)}, f32[896,128]{1,0:T(8,128)S(1)}, u32[]{:S(2)}, u32[]{:S(2)}) %collective-permute-start.5) | collective-permute-done | bytes 458784 | tf_op jit(solution)/shard_map/terms_along_z/ppermute | solution.py:472
  24.3 0.2 combine_terms.1
  24.5 18.4 %all_to_all.10 = f32[64,1,3072]{2,1,0:T(1,128)S(1)} all-to-all(f32[64,1,3072]{2,1,0:T(1,128)S(1)} %bitcast.14), channel_id=1, replica_groups=mesh['grp'=16,'z'=4,'core'=2] {'grp','z'}, dimensions={0} | all-to-all | bytes 1572864 | tf_op jit(solution)/shard_map/exchange/all_to_all | solution.py:466
  42.9 0.1 sum_pieces.1
  43.0 17.2 %all_to_all.11 = f32[64,1,3072]{2,1,0:T(1,128)S(1)} all-to-all(f32[64,1,3072]{2,1,0:T(1,128)S(1)} %bitcast.13), channel_id=1, replica_groups=mesh['grp'=16,'z'=4,'core'=2] {'grp','z'}, dimensions={0} | all-to-all | bytes 1572864 | tf_op jit(solution)/shard_map/exchange/all_to_all | solution.py:466
  60.2 0.0 copy-start.2
  60.2 0.1 unpack_sums.1
  60.2 4.6 %collective-permute-start.6 = (f32[640,128]{1,0:T(8,128)S(1)}, f32[640,128]{1,0:T(8,128)S(1)}, u32[]{:S(2)}, u32[]{:S(2)}) collective-permute-start(f32[640,128]{1,0:T(8,128)S(1)} %get-tuple-element.32.near_ref), channel_id=1, source_target_pairs={{0,1},{1,0},{2,3},{3,2},{4,5},{5,4},{6,7},{7,6},{8,9},{9,8},{10,11... | collective-permute-start | bytes 983048 | tf_op jit(solution)/shard_map/swap_gram/ppermute | solution.py:482
  64.8 0.1 collective-permute-start.10
  64.9 0.2 collective-permute-start.9
  65.1 0.8 collective-permute-start.8
  65.9 1.3 %collective-permute-start.7 = (f32[896,128]{1,0:T(8,128)S(1)}, f32[896,128]{1,0:T(8,128)S(1)}, u32[]{:S(2)}, u32[]{:S(2)}) collective-permute-start(f32[896,128]{1,0:T(8,128)S(1)} %get-tuple-element.36.refs_0_), channel_id=1, source_target_pairs={{0,8},{1,25},{32,40},{33,57},{64,72},{65,89},{96,104},{97,121},{8,... | collective-permute-start | bytes 1376264 | tf_op jit(solution)/shard_map/quarters_along_x/ppermute | solution.py:486
  67.2 0.0 collective-permute-done.6.far_ref
  67.2 0.0 copy-done.2
  67.2 9.4 %factor_first.1 = (f32[256,512]{1,0:T(8,128)S(1)}, f32[256,128]{1,0:T(8,128)S(1)}, f32[128,256]{1,0:T(8,128)S(1)}, f32[256,256]{1,0:T(8,128)S(1)}, f32[128,256]{1,0:T(8,128)S(1)}) custom-call(s32[6]{0:T(128)S(1)} %stack.27.place_ref, f32[640,128]{1,0:T(8,128)S(1)} %get-tuple-element.32.near_ref, f32[640,128]{1,0:T(8,128)S(1)} %collective-permute-done.6.far_ref, ...), custom_call_target="tpu_custom_call" | custom-call | flops 10000000000 | bytes 4000000 | tf_op jit(solution)/shard_map/factor_first/pallas_call | solution.py:294
  76.6 0.0 collective-permute-done.9.refs_3_
  76.6 0.0 collective-permute-done.8.refs_2_
  76.6 0.0 collective-permute-done.7.refs_1_
  76.6 0.1 collective-permute-start.11
  76.7 0.5 collective-permute-start.12
  77.2 0.1 collective-permute-start.13
  77.3 7.6 %factor_rest.1 = (f32[256,256]{1,0:T(8,128)S(1)}, f32[256,128]{1,0:T(8,128)S(1)}, f32[128,256]{1,0:T(8,128)S(1)}) custom-call(f32[256,256]{1,0:T(8,128)S(1)} %get-tuple-element.39.a_in, f32[128,256]{1,0:T(8,128)S(1)} %get-tuple-element.40.rows_in), custom_call_target="tpu_custom_call" | custom-call | flops 10000000000 | bytes 2000000 | tf_op jit(solution)/shard_map/factor_rest/pallas_call | solution.py:312
  84.9 3.2 %back_substitute.1 = (f32[4,192,128]{2,1,0:T(8,128)S(1)}, f32[64,512]{1,0:T(8,128)}) custom-call(s32[6]{0:T(128)S(1)} %stack.27.place_ref, f32[256,512]{1,0:T(8,128)S(1)} %get-tuple-element.33.upper_a, f32[256,128]{1,0:T(8,128)S(1)} %get-tuple-element.34.tinv_a, f32[128,256]{1,0:T(8,128)S(1)} %get-tuple-element.35.y_a, ...), custom_call_target="tpu_custom_call" | custom-call | flops 4000000000 | bytes 2000000 | tf_op jit(solution)/shard_map/back_substitute/pallas_call | solution.py:359
  88.1 0.0 collective-permute-done.10.refs_4_
  88.1 0.0 collective-permute-done.11.refs_5_
  88.1 0.0 collective-permute-done.12.refs_6_
  88.1 0.0 collective-permute-done.13.refs_7_
  88.1 4.3 %apply_factor.1 = (f32[128,1792]{1,0:T(8,128)}, f32[64,1792]{1,0:T(8,128)}) custom-call(s32[6]{0:T(128)S(1)} %stack.27.place_ref, f32[4,192,128]{2,1,0:T(8,128)S(1)} %get-tuple-element.45.mixed_ref, f32[896,128]{1,0:T(8,128)S(1)} %get-tuple-element.36.refs_0_, f32[896,128]{1,0:T(8,128)S(1)} %collective-permute-done.7.refs_1_, ...), custom_call_target="tpu_custom_call" | custom-call | tf_op jit(solution)/shard_map/apply_factor/pallas_call | solution.py:402
Async XLA Ops:
  0.6 4.7 %copy-start = (f32[128,1792]{1,0:T(8,128)S(1)}, f32[128,1792]{1,0:T(8,128)}, u32[]{:S(2)}) copy-start(f32[128,1792]{1,0:T(8,128)} %refs_8_.1) | copy-start | bytes 2752516
  1.8 1.6 %copy-start.3 = (s32[128]{0:T(128)S(1)}, s32[128]{0:T(128)}, u32[]{:S(2)}) copy-start(s32[128]{0:T(128)} %param.5) | copy-start | bytes 1540
  1.8 3.5 %collective-permute-start.1 = (f32[128,896]{1,0:T(8,128)S(1)}, f32[128,896]{1,0:T(8,128)S(1)}, u32[]{:S(2)}, u32[]{:S(2)}) collective-permute-start(f32[128,896]{1,0:T(8,128)S(1)} %constant_dynamic-slice_fusion), channel_id=1, source_target_pairs={{0,1},{1,0},{2,3},{3,2},{4,5},{5,4},{6,7},{7,6},{8,9},{9,8},{10,11... | collective-permute-start | bytes 1376264 | tf_op jit(solution)/shard_map/swap_inputs/ppermute | solution.py:440
  3.3 2.0 %collective-permute-start = (f32[128,512]{1,0:T(8,128)}, f32[128,512]{1,0:T(8,128)S(1)}, u32[]{:S(2)}, u32[]{:S(2)}) collective-permute-start(f32[128,512]{1,0:T(8,128)} %panel_ref.3), channel_id=1, source_target_pairs={{0,1},{1,0},{2,3},{3,2},{4,5},{5,4},{6,7},{7,6},{8,9},{9,8},{10,11... | collective-permute-start | bytes 786440 | tf_op jit(solution)/shard_map/swap_inputs/ppermute | solution.py:439
  3.4 1.3 %collective-permute-start.2 = (s32[1,128]{1,0:T(1,128)S(1)}, s32[1,128]{1,0:T(1,128)S(1)}, u32[]{:S(2)}, u32[]{:S(2)}) collective-permute-start(s32[1,128]{1,0:T(1,128)S(1)} %bitcast.15), channel_id=1, source_target_pairs={{0,1},{1,0},{2,3},{3,2},{4,5},{5,4},{6,7},{7,6},{8,9},{9,8},{10,11... | collective-permute-start | bytes 1544 | tf_op jit(solution)/shard_map/swap_inputs/ppermute | solution.py:438
  5.3 1.0 %copy-start.1 = (f32[128,512]{1,0:T(8,128)S(1)}, f32[128,512]{1,0:T(8,128)}, u32[]{:S(2)}) copy-start(f32[128,512]{1,0:T(8,128)} %panel_ref.3) | copy-start | bytes 786436
  9.3 9.1 %collective-permute-start.3 = (f32[896,128]{1,0:T(8,128)S(1)}, f32[896,128]{1,0:T(8,128)S(1)}, u32[]{:S(2)}, u32[]{:S(2)}) collective-permute-start(f32[896,128]{1,0:T(8,128)S(1)} %get-tuple-element.29), channel_id=1, source_target_pairs={{0,8},{1,25},{32,40},{33,57},{64,72},{65,89},{96,104},{97,121},{8,... | collective-permute-start | bytes 1376264 | tf_op jit(solution)/shard_map/terms_along_x/ppermute | solution.py:472
  11.9 8.6 %collective-permute-start.4 = (f32[896,128]{1,0:T(8,128)S(1)}, f32[896,128]{1,0:T(8,128)S(1)}, u32[]{:S(2)}, u32[]{:S(2)}) collective-permute-start(f32[896,128]{1,0:T(8,128)S(1)} %get-tuple-element.30), channel_id=1, source_target_pairs={{0,32},{1,97},{8,40},{9,105},{16,48},{17,113},{24,56},{25,121},{32... | collective-permute-start | bytes 1376264 | tf_op jit(solution)/shard_map/terms_along_y/ppermute | solution.py:472
  14.7 9.6 %collective-permute-start.5 = (f32[896,128]{1,0:T(8,128)S(1)}, f32[896,128]{1,0:T(8,128)S(1)}, u32[]{:S(2)}, u32[]{:S(2)}) collective-permute-start(f32[896,128]{1,0:T(8,128)S(1)} %get-tuple-element.31), channel_id=1, source_target_pairs={{0,2},{1,7},{2,0},{3,5},{4,6},{5,3},{6,4},{7,1},{8,10},{9,15},{10,... | collective-permute-start | bytes 1376264 | tf_op jit(solution)/shard_map/terms_along_z/ppermute | solution.py:472
  60.2 7.1 %copy-start.2 = (f32[128,512]{1,0:T(8,128)S(1)}, f32[128,512]{1,0:T(8,128)}, u32[]{:S(2)}) copy-start(f32[128,512]{1,0:T(8,128)} %panel_ref.3) | copy-start | bytes 786436
  60.2 7.0 %collective-permute-start.6 = (f32[640,128]{1,0:T(8,128)S(1)}, f32[640,128]{1,0:T(8,128)S(1)}, u32[]{:S(2)}, u32[]{:S(2)}) collective-permute-start(f32[640,128]{1,0:T(8,128)S(1)} %get-tuple-element.32.near_ref), channel_id=1, source_target_pairs={{0,1},{1,0},{2,3},{3,2},{4,5},{5,4},{6,7},{7,6},{8,9},{9,8},{10,11... | collective-permute-start | bytes 983048 | tf_op jit(solution)/shard_map/swap_gram/ppermute | solution.py:482
  64.8 23.3 %collective-permute-start.10 = (f32[896,128]{1,0:T(8,128)S(1)}, f32[896,128]{1,0:T(8,128)S(1)}, u32[]{:S(2)}, u32[]{:S(2)}) collective-permute-start(f32[896,128]{1,0:T(8,128)S(1)} %get-tuple-element.36.refs_0_), channel_id=1, source_target_pairs={{0,1},{1,0},{2,3},{3,2},{4,5},{5,4},{6,7},{7,6},{8,9},{9,8},{10,11... | collective-permute-start | bytes 1376264 | tf_op jit(solution)/shard_map/swap_quarter/ppermute | solution.py:488
  64.9 11.7 %collective-permute-start.9 = (f32[896,128]{1,0:T(8,128)S(1)}, f32[896,128]{1,0:T(8,128)S(1)}, u32[]{:S(2)}, u32[]{:S(2)}) collective-permute-start(f32[896,128]{1,0:T(8,128)S(1)} %get-tuple-element.36.refs_0_), channel_id=1, source_target_pairs={{0,2},{1,7},{2,0},{3,5},{4,6},{5,3},{6,4},{7,1},{8,10},{9,15},{10,... | collective-permute-start | bytes 1376264 | tf_op jit(solution)/shard_map/quarters_along_z/ppermute | solution.py:486
  65.1 11.5 %collective-permute-start.8 = (f32[896,128]{1,0:T(8,128)S(1)}, f32[896,128]{1,0:T(8,128)S(1)}, u32[]{:S(2)}, u32[]{:S(2)}) collective-permute-start(f32[896,128]{1,0:T(8,128)S(1)} %get-tuple-element.36.refs_0_), channel_id=1, source_target_pairs={{0,32},{1,97},{8,40},{9,105},{16,48},{17,113},{24,56},{25,121},{32... | collective-permute-start | bytes 1376264 | tf_op jit(solution)/shard_map/quarters_along_y/ppermute | solution.py:486
  65.9 10.7 %collective-permute-start.7 = (f32[896,128]{1,0:T(8,128)S(1)}, f32[896,128]{1,0:T(8,128)S(1)}, u32[]{:S(2)}, u32[]{:S(2)}) collective-permute-start(f32[896,128]{1,0:T(8,128)S(1)} %get-tuple-element.36.refs_0_), channel_id=1, source_target_pairs={{0,8},{1,25},{32,40},{33,57},{64,72},{65,89},{96,104},{97,121},{8,... | collective-permute-start | bytes 1376264 | tf_op jit(solution)/shard_map/quarters_along_x/ppermute | solution.py:486
  76.6 11.4 %collective-permute-start.11 = (f32[896,128]{1,0:T(8,128)S(1)}, f32[896,128]{1,0:T(8,128)S(1)}, u32[]{:S(2)}, u32[]{:S(2)}) collective-permute-start(f32[896,128]{1,0:T(8,128)S(1)} %collective-permute-done.7.refs_1_), channel_id=1, source_target_pairs={{0,1},{1,0},{2,3},{3,2},{4,5},{5,4},{6,7},{7,6},{8,9},{9,8},{10,11... | collective-permute-start | bytes 1376264 | tf_op jit(solution)/shard_map/swap_quarters/ppermute | solution.py:493
  76.7 11.3 %collective-permute-start.12 = (f32[896,128]{1,0:T(8,128)S(1)}, f32[896,128]{1,0:T(8,128)S(1)}, u32[]{:S(2)}, u32[]{:S(2)}) collective-permute-start(f32[896,128]{1,0:T(8,128)S(1)} %collective-permute-done.8.refs_2_), channel_id=1, source_target_pairs={{0,1},{1,0},{2,3},{3,2},{4,5},{5,4},{6,7},{7,6},{8,9},{9,8},{10,11... | collective-permute-start | bytes 1376264 | tf_op jit(solution)/shard_map/swap_quarters/ppermute | solution.py:493
  77.2 10.9 %collective-permute-start.13 = (f32[896,128]{1,0:T(8,128)S(1)}, f32[896,128]{1,0:T(8,128)S(1)}, u32[]{:S(2)}, u32[]{:S(2)}) collective-permute-start(f32[896,128]{1,0:T(8,128)S(1)} %collective-permute-done.9.refs_3_), channel_id=1, source_target_pairs={{0,1},{1,0},{2,3},{3,2},{4,5},{5,4},{6,7},{7,6},{8,9},{9,8},{10,11... | collective-permute-start | bytes 1376264 | tf_op jit(solution)/shard_map/swap_quarters/ppermute | solution.py:493

commit v6 on v5

v6 whole, which is shorter than its diff:
```python
import functools

import jax
import jax.numpy as jnp
from jax import lax
from jax.experimental import pallas as pl
from jax.experimental.pallas import tpu as pltpu
from jax.sharding import Mesh, PartitionSpec as P

ridge_shift = 0.05
HIGHEST = lax.Precision.HIGHEST
tile = 128
strip = 32
chips = ("grp", "z")
classes = 4


def product(left, right, left_dim=1, right_dim=0):
    return lax.dot_general(
        left,
        right,
        (((left_dim,), (right_dim,)), ((), ())),
        precision=HIGHEST,
        preferred_element_type=jnp.float32,
    )


def three_parts(x):
    high = x.astype(jnp.bfloat16)
    rest = x - high.astype(jnp.float32)
    middle = rest.astype(jnp.bfloat16)
    return high, middle, (rest - middle.astype(jnp.float32)).astype(jnp.bfloat16)


def stacked(left, right, left_dim=1, right_dim=0):
    lh, lm, ll = three_parts(left)
    rh, rm, rl = three_parts(right)
    return lax.dot_general(
        jnp.concatenate([lh, lh, lm, lh, ll, lm], left_dim),
        jnp.concatenate([rh, rm, rh, rl, rh, rm], right_dim),
        (((left_dim,), (right_dim,)), ((), ())),
        preferred_element_type=jnp.float32,
    )


def factor_diagonal(work, later):
    sub = lax.broadcasted_iota(jnp.int32, (8, tile), 0)
    groups = strip // 8

    def spread_row(array, row):
        return jnp.broadcast_to(array[row : row + 1, :], (8, tile))

    for r in range(0, tile, strip):
        left = [work[r + 8 * g : r + 8 * g + 8, 0:tile] for g in range(groups)]
        right = [work[r + 8 * g : r + 8 * g + 8, tile : 2 * tile] for g in range(groups)]
        if later:
            later.pop(0)()
        col = {}
        for c in range(strip):
            for g in range(c // 8, groups):
                col[c, g] = jnp.broadcast_to(left[g][:, r + c : r + c + 1], (8, tile))
        for k in range(strip):
            at, row = k // 8, k % 8
            inv = lax.rsqrt(spread_row(col[k, at], row))
            low = {g: col[k, g] * inv for g in range(at, groups)}
            for c in range(k + 1, strip):
                factor_c = spread_row(low[c // 8], c % 8)
                for g in range(c // 8, groups):
                    col[c, g] = col[c, g] - low[g] * factor_c
            below = jnp.where(sub > row, low[at], 0.0)
            for side in (left, right):
                pivot = spread_row(side[at], row) * inv
                side[at] = jnp.where(sub == row, pivot, side[at] - below * pivot)
                for g in range(at + 1, groups):
                    side[g] = side[g] - low[g] * pivot
        new_left = jnp.concatenate(left, 0)
        new_right = jnp.concatenate(right, 0)
        work[r : r + strip, 0:tile] = new_left
        work[r : r + strip, tile : 2 * tile] = new_right
        if r + strip < tile:
            update = stacked(new_left, jnp.concatenate([new_left, new_right], 1), 0, 0)
            work[r + strip : tile, :] = work[r + strip : tile, :] - update[r + strip : tile, :]


gram_blocks = (((0, 0), (1, 1), (0, 1), (0, 2), (0, 3)), ((2, 2), (3, 3), (2, 3), (1, 2), (1, 3)))


def products_kernel(place_ref, panel_ref, other_ref, trail_ref, far_ref, counts_ref, far_counts_ref, *refs, total_rows):
    outs, gram, (pt, wp, wt, quarters) = refs[:classes], refs[classes], refs[classes + 1 :]
    core = place_ref[0]
    own, width = panel_ref.shape
    half = trail_ref.shape[1]
    for at, rows, trail, count in ((0, panel_ref, trail_ref, counts_ref), (own, other_ref, far_ref, far_counts_ref)):
        weight = jnp.transpose(jnp.broadcast_to(count[...].astype(jnp.float32) / total_rows, (own, own)))
        for c in range(0, width, tile):
            block = rows[:, c : c + tile]
            pt[c : c + tile, at : at + own] = jnp.transpose(block)
            wp[at : at + own, c : c + tile] = block * weight
        for c in range(0, half, tile):
            wt[at : at + own, c : c + tile] = trail[:, c : c + tile] * weight
    step = 2 * tile
    for c in range(0, half, step):
        n = min(step, half - c)
        part = product(pt[...], wt[:, c : c + n])
        for k in range(classes):
            for j in range(0, n, tile):
                quarters[k, c + j : c + j + tile, :] = part[k * tile : (k + 1) * tile, j : j + tile]
    for m in range(classes):
        outs[m][...] = quarters[place_ref[1 + m]]
    near = pl.multiple_of(core * step, tile)
    first = product(pt[pl.ds(near, tile), :], wp[:, pl.ds(near, step)])
    gram[0:tile, :] = first[:, :tile]
    gram[2 * tile : 3 * tile, :] = first[:, tile:]
    near = pl.multiple_of(core * step + tile, tile)
    gram[tile : 2 * tile, :] = product(pt[pl.ds(near, tile), :], wp[:, pl.ds(near, tile)])
    near = pl.multiple_of(core * tile, tile)
    last = product(pt[pl.ds(near, tile), :], wp[:, step:])
    gram[3 * tile : 4 * tile, :] = last[:, :tile]
    gram[4 * tile :, :] = last[:, tile:]


def products(place, panel, other, trailing, far, counts, far_counts, total_rows):
    own, width = panel.shape
    half = far.shape[1]
    gram_rows = len(gram_blocks[0]) * tile
    whole = lambda shape: pl.BlockSpec(shape, lambda i, place: (0, 0))
    return pl.pallas_call(
        functools.partial(products_kernel, total_rows=total_rows),
        out_shape=[jax.ShapeDtypeStruct((half, tile), jnp.float32)] * classes
        + [jax.ShapeDtypeStruct((gram_rows, tile), jnp.float32)],
        grid_spec=pltpu.PrefetchScalarGridSpec(
            num_scalar_prefetch=1,
            grid=(1,),
            in_specs=[
                whole((own, width)),
                whole((own, width)),
                pl.BlockSpec((own, half), lambda i, place: (0, place[0])),
                whole((own, half)),
                whole((1, own)),
                whole((1, own)),
            ],
            out_specs=[whole((half, tile))] * classes + [whole((gram_rows, tile))],
            scratch_shapes=[
                pltpu.VMEM((width, 2 * own), jnp.float32),
                pltpu.VMEM((2 * own, width), jnp.float32),
                pltpu.VMEM((2 * own, half), jnp.float32),
                pltpu.VMEM((classes, half, tile), jnp.float32),
            ],
        ),
        compiler_params=pltpu.CompilerParams(vmem_limit_bytes=32 * 1024 * 1024),
    )(place, panel, other, trailing, far, counts, far_counts)


def combine_kernel(gram_ref, *refs, chip_count):
    parts, out_ref = refs[:classes], refs[classes]
    size = gram_ref.shape[0] // chip_count
    chunk = parts[0].shape[0] // chip_count
    for q in range(chip_count):
        side = slice(q * chunk, (q + 1) * chunk)
        cross = (parts[0][side, :] + parts[1][side, :]) + (parts[2][side, :] + parts[3][side, :])
        gram = gram_ref[q * size : (q + 1) * size, :]
        out_ref[q * (size + chunk) : (q + 1) * (size + chunk), :] = jnp.concatenate([gram, cross], 0)


def combine(gram, parts, chip_count):
    vmem = pl.BlockSpec(memory_space=pltpu.VMEM)
    return pl.pallas_call(
        functools.partial(combine_kernel, chip_count=chip_count),
        out_shape=jax.ShapeDtypeStruct((gram.shape[0] + parts[0].shape[0], tile), jnp.float32),
        in_specs=[vmem] * (1 + classes),
        out_specs=vmem,
        compiler_params=pltpu.CompilerParams(vmem_limit_bytes=16 * 1024 * 1024),
    )(gram, *parts)


def sum_kernel(pieces_ref, copies_ref, *, size, kinds):
    both = pieces_ref.shape[0] // len(kinds)
    totals = []
    for k in range(classes):
        total = None
        for q, kind in enumerate(kinds):
            if kind == k:
                piece = pieces_ref[q * both : (q + 1) * both, :]
                total = piece if total is None else total + piece
        totals.append(total)
    gram = (totals[0] + totals[1]) + (totals[2] + totals[3])
    is_gram = lax.broadcasted_iota(jnp.int32, (both, tile), 0) < size
    for k in range(classes):
        copy = jnp.where(is_gram, gram, totals[k])
        for q, kind in enumerate(kinds):
            if kind == k:
                copies_ref[q * both : (q + 1) * both, :] = copy


def sum_pieces(pieces, size, kinds):
    vmem = pl.BlockSpec(memory_space=pltpu.VMEM)
    return pl.pallas_call(
        functools.partial(sum_kernel, size=size, kinds=kinds),
        out_shape=jax.ShapeDtypeStruct(pieces.shape, jnp.float32),
        in_specs=[vmem],
        out_specs=vmem,
        compiler_params=pltpu.CompilerParams(vmem_limit_bytes=16 * 1024 * 1024),
    )(pieces)


def unpack_kernel(near_ref, far_ref, near_gram, far_gram, quarters_ref, *, chip_count):
    size = near_gram.shape[0] // chip_count
    chunk = quarters_ref.shape[1] // chip_count
    both = size + chunk
    for at, (copies_ref, gram_ref) in enumerate(((near_ref, near_gram), (far_ref, far_gram))):
        for q in range(chip_count):
            gram_ref[q * size : (q + 1) * size, :] = copies_ref[q * both : q * both + size, :]
            quarters_ref[at, q * chunk : (q + 1) * chunk, :] = copies_ref[q * both + size : (q + 1) * both, :]


def unpack(near, far, chip_count, size, chunk):
    vmem = pl.BlockSpec(memory_space=pltpu.VMEM)
    gram = jax.ShapeDtypeStruct((chip_count * size, tile), jnp.float32)
    return pl.pallas_call(
        functools.partial(unpack_kernel, chip_count=chip_count),
        out_shape=(gram, gram, jax.ShapeDtypeStruct((2, chip_count * chunk, tile), jnp.float32)),
        in_specs=[vmem] * 2,
        out_specs=[vmem] * 3,
        compiler_params=pltpu.CompilerParams(vmem_limit_bytes=16 * 1024 * 1024),
    )(near, far)


def factor_kernel(place_ref, near_ref, far_ref, panel_ref, mixed_ref, r_ref, a_ref, upper, linv, rows_ref, y_ref, w_ref, z_ref, work):
    rows = lax.broadcasted_iota(jnp.int32, (tile, tile), 0)
    cols = lax.broadcasted_iota(jnp.int32, (tile, tile), 1)
    eye = jnp.where(rows == cols, 1.0, 0.0).astype(jnp.float32)
    own, width = panel_ref.shape
    picked = r_ref.shape[0]
    for core, blocks in enumerate(gram_blocks):
        for at, (i, j) in enumerate(blocks):
            side = slice(at * tile, (at + 1) * tile)
            block = jnp.where(place_ref[0] == core, near_ref[side, :], far_ref[side, :])
            if i == j:
                block = block + ridge_shift * eye
            a_ref[i * tile : (i + 1) * tile, j * tile : (j + 1) * tile] = block
    upper[...] = jnp.zeros_like(upper)
    linv[...] = jnp.zeros_like(linv)
    z_ref[...] = jnp.zeros_like(z_ref)
    rows_ref[...] = panel_ref[...]
    work[:, 0:tile] = a_ref[0:tile, 0:tile]
    work[:, tile:] = eye
    later = []
    for b in range(0, width, tile):
        e = b + tile
        n = e + tile
        factor_diagonal(work, later)
        while later:
            later.pop(0)()
        inverse = work[:, tile:]
        diagonal = work[:, 0:tile]
        if e == width:
            upper[b:e, b:e] = jnp.where(cols >= rows, diagonal, 0.0)
            y = stacked(rows_ref[:, b:e], inverse, 1, 1)
            last = jnp.concatenate([-stacked(inverse, w_ref[:, 0:b]), inverse], 1)
            linv[b:e, :] = last
            z_ref[...] = z_ref[...] + stacked(y, last)
            break
        beside = stacked(inverse, a_ref[b:e, e:n])
        work[:, 0:tile] = a_ref[e:n, e:n] - stacked(beside, beside, 0, 0)
        work[:, tile:] = eye

        def rows_of_tiles(b=b, e=e, n=n, inverse=inverse, diagonal=diagonal, beside=beside):
            upper[b:e, b:e] = jnp.where(cols >= rows, diagonal, 0.0)
            upper[b:e, e:n] = beside
            linv[b:e, b:e] = inverse
            if b:
                linv[b:e, 0:b] = -stacked(inverse, w_ref[:, 0:b])
            y_ref[:, b:e] = stacked(rows_ref[:, b:e], inverse, 1, 1)
            if n < width:
                upper[b:e, n:] = stacked(inverse, a_ref[b:e, n:])

        def remainder(b=b, e=e, n=n, beside=beside):
            right = upper[b:e, e:]
            if n < width:
                a_ref[e:n, n:] = a_ref[e:n, n:] - stacked(beside, right[:, tile:], 0, 0)
            for c in range(n, width, tile):
                a_ref[c : c + tile, c:] = a_ref[c : c + tile, c:] - stacked(
                    right[:, c - e : c - e + tile], right[:, c - e :], 0, 0
                )
            rows_ref[:, e:] = rows_ref[:, e:] - stacked(y_ref[:, b:e], right)

        def inverses(b=b, e=e, n=n):
            w_ref[:, 0:e] = stacked(upper[0:e, e:n], linv[0:e, 0:e], 0, 0)
            z_ref[:, 0:e] = z_ref[:, 0:e] + stacked(y_ref[:, b:e], linv[b:e, 0:e])

        later = [rows_of_tiles, remainder, inverses]
    at = pl.ds(pl.multiple_of(place_ref[1 + classes], picked), picked)
    r_ref[...] = upper[at, :]
    for b in range(0, width, tile):
        mixed_ref[b // tile, 0:own, :] = z_ref[:, b : b + tile]
        mixed_ref[b // tile, own:, :] = linv[at, b : b + tile]


def factor(place, near, far, panel, picked):
    own, width = panel.shape
    vmem = pl.BlockSpec(memory_space=pltpu.VMEM)
    square = pltpu.VMEM((width, width), jnp.float32)
    flat = pltpu.VMEM((own, width), jnp.float32)
    return pl.pallas_call(
        factor_kernel,
        out_shape=(
            jax.ShapeDtypeStruct((width // tile, own + picked, tile), jnp.float32),
            jax.ShapeDtypeStruct((picked, width), jnp.float32),
        ),
        in_specs=[pl.BlockSpec(memory_space=pltpu.SMEM), vmem, vmem, vmem],
        out_specs=(vmem, vmem),
        scratch_shapes=[
            square,
            square,
            square,
            flat,
            flat,
            pltpu.VMEM((tile, width - tile), jnp.float32),
            flat,
            pltpu.VMEM((tile, 2 * tile), jnp.float32),
        ],
        compiler_params=pltpu.CompilerParams(vmem_limit_bytes=20 * 1024 * 1024),
        cost_estimate=pl.CostEstimate(flops=20 * 10**9, bytes_accessed=4 * 10**6, transcendentals=0),
    )(place, near, far, panel)


def finish_kernel(place_ref, mixed_ref, *refs):
    quarters = refs[:classes]
    trail_ref, updated_ref, coupling_ref = refs[classes:]
    own = trail_ref.shape[0]
    half = quarters[0].shape[1]
    core = place_ref[0]
    left = [mixed_ref[place_ref[1 + m]] for m in range(classes)]
    left = [jnp.concatenate(left[m : m + 2], 1) for m in range(0, classes, 2)]
    for c in range(0, half, tile):
        out = None
        for m in range(0, classes, 2):
            right = jnp.concatenate(
                [
                    jnp.concatenate([quarters[m][side, c : c + tile, :], quarters[m + 1][side, c : c + tile, :]], 0)
                    for side in range(2)
                ],
                1,
            )
            term = product(left[m // 2], right)
            out = term if out is None else out + term
        for part, where in ((out[:, :tile], core), (out[:, tile:], 1 - core)):
            at = pl.ds(pl.multiple_of(where * half + c, tile), tile)
            updated_ref[:, at] = trail_ref[:, at] - part[:own]
            coupling_ref[:, at] = part[own:]


def finish(place, mixed, quarters, trailing):
    vmem = pl.BlockSpec(memory_space=pltpu.VMEM)
    own, trail = trailing.shape
    return pl.pallas_call(
        finish_kernel,
        out_shape=(
            jax.ShapeDtypeStruct((own, trail), jnp.float32),
            jax.ShapeDtypeStruct((mixed.shape[1] - own, trail), jnp.float32),
        ),
        in_specs=[pl.BlockSpec(memory_space=pltpu.SMEM)] + [vmem] * (2 + classes),
        out_specs=(vmem, vmem),
        compiler_params=pltpu.CompilerParams(vmem_limit_bytes=32 * 1024 * 1024),
    )(place, mixed, *quarters, trailing)


def kind_of(x, y, z):
    return (x % 2) ^ (2 * (y % 2)) ^ (3 * (z % 2))


def local(panel, trailing, counts):
    own, width = panel.shape
    half = trailing.shape[1] // 2
    depth = lax.axis_size("z")
    groups = lax.axis_size("grp")
    side = 4
    members = 2 * depth
    chip_count = groups * depth
    chunk = half // chip_count
    gram_chunk = len(gram_blocks[0]) * tile // chip_count
    kinds = [kind_of(g % side, g // side, z) for g in range(groups) for z in range(depth)]
    group, z, core = lax.axis_index("grp"), lax.axis_index("z"), lax.axis_index("core")
    kind = kind_of(group % side, group // side, z)
    picked = width // members
    start = (z * 2 + core) * picked
    place = jnp.stack([core] + [kind ^ m for m in range(classes)] + [start]).astype(jnp.int32)
    swap = [(0, 1), (1, 0)]
    count_row = counts[None, :]
    sent_trail = lax.dynamic_slice_in_dim(trailing, (1 - core) * half, half, 1)
    with jax.named_scope("swap_inputs"):
        far_counts = lax.ppermute(count_row, "core", swap)
        other_panel = lax.ppermute(panel, "core", swap)
        far_trail = lax.ppermute(sent_trail, "core", swap)
    with jax.named_scope("local_products"):
        *terms, gram_terms = products(
            place, panel, other_panel, trailing, far_trail, count_row, far_counts, own * groups * members
        )
    def pairs(before, after):
        out = []
        for a in range(before):
            for i in range(side):
                for b in range(after):
                    for c in range(2):
                        to = i ^ (3 if c else 1)
                        out.append((((a * side + i) * after + b) * 2 + c, ((a * side + to) * after + b) * 2 + c))
        return out

    along = (
        ("along_x", ("grp", "core"), groups // side, 1),
        ("along_y", ("grp", "core"), 1, side),
        ("along_z", ("z", "core"), 1, 1),
    )

    def exchange(rows):
        with jax.named_scope("exchange"):
            rows = lax.all_to_all(rows.reshape(chip_count, 1, -1), chips, 0, 0, tiled=True)
        return rows.reshape(-1, tile)

    parts = [terms[0]]
    for m, (name, axis, before, after) in enumerate(along):
        with jax.named_scope("terms_" + name):
            parts.append(lax.ppermute(terms[1 + m], axis, pairs(before, after)))
    with jax.named_scope("combine_terms"):
        pieces = combine(gram_terms, parts, chip_count)
    pieces = exchange(pieces)
    with jax.named_scope("sum_pieces"):
        copies = sum_pieces(pieces, gram_chunk, kinds)
    copies = exchange(copies)
    with jax.named_scope("swap_copies"):
        far_copies = lax.ppermute(copies, "core", swap)
    with jax.named_scope("unpack_sums"):
        near_gram, far_gram, quarter = unpack(copies, far_copies, chip_count, gram_chunk, chunk)
    quarters = [quarter]
    for name, axis, before, after in along:
        with jax.named_scope("quarters_" + name):
            quarters.append(lax.ppermute(quarter, axis, pairs(before, after)))
    with jax.named_scope("factor_gram"):
        mixed, r_rows = factor(place, near_gram, far_gram, panel, picked)
    with jax.named_scope("apply_factor"):
        updated, coupling = finish(place, mixed, quarters, trailing)
    return (r_rows, coupling, updated)


def solution(mesh):
    groups, members = mesh.devices.shape
    split = Mesh(mesh.devices.reshape(groups, members // 2, 2), ("grp", "z", "core"))
    rows = P(("grp", "z", "core"))
    return jax.shard_map(
        local,
        mesh=split,
        in_specs=(P(("grp", "z", "core"), None), P(("grp", "z", "core"), None), rows),
        out_specs=(P(("z", "core"), None), P(("z", "core"), None), P(("grp", "z", "core"), None)),
        check_vma=False,
    )
```

time: 92.6 us -> 89.5 us (0.967)
  Pallas kernels: 27.8 us -> 23.6 us
  waiting for transfers between devices: 7.27 us -> 9.17 us
    pallas_call x3 -> x1, Pallas kernels: 20.1 us -> 15.9 us  [factor(): pl.pallas_call(factor_kernel, out_shape=(jax.ShapeDtypeStruct((width // t...]
    ppermute x11 -> x7, waiting for transfers between devices: 5.89 us -> 7.78 us  [the longest x3 5.86 us: local(): parts.append(lax.ppermute(terms[1 + m], axis, pairs(before, after)))]
    ppermute x11 -> x7, starting transfers between devices: 16.8 us -> 16 us  [the longest x3 9.13 us: local(): parts.append(lax.ppermute(terms[1 + m], axis, pairs(before, after)))]
  transfers between devices with their start and end apart: 14 -> 10, of which waited for: 4 -> 5; matrix products, arithmetic and copies ran while one was open for 0% -> 0% of each run, Pallas kernels for 22% -> 18%
where the time goes in v6:
time: 89.5 us; the launch traced here: 89.3 us
  blocking collectives  35.6 us (40%)
  Pallas kernels  23.6 us (26%)
  starting transfers between devices  18.1 us (20%)
  waiting for transfers between devices  9.17 us (10%)
  local copies, waits for them, and re-layouts  2.18 us (2%)
    all_to_all x2, blocking collectives, exchange(): lax.all_to_all(rows.reshape(chip_count, 1, -1), chips, 0, 0, tiled=True)  35.6 us
    pallas_call x1, Pallas kernels, factor(): pl.pallas_call(factor_kernel, out_shape=(jax.ShapeDtypeStruct((width // t...  15.9 us
    ppermute x3, starting transfers between devices, local(): parts.append(lax.ppermute(terms[1 + m], axis, pairs(before, after)))  9.13 us
    ppermute x3, waiting for transfers between devices, local(): parts.append(lax.ppermute(terms[1 + m], axis, pairs(before, after)))  5.86 us
    ppermute x1, starting transfers between devices, local(): far_copies = lax.ppermute(copies, 'core', swap)  4.48 us
    pallas_call x1, Pallas kernels, finish(): pl.pallas_call(finish_kernel, out_shape=(jax.ShapeDtypeStruct((own, trail...  4.28 us
    pallas_call x1, Pallas kernels, products(): pl.pallas_call(functools.partial(products_kernel, total_rows=total_rows),...  2.99 us
    ppermute x3, starting transfers between devices, local(): quarters.append(lax.ppermute(quarter, axis, pairs(before, after)))  2.41 us
  transfers between devices with their start and end apart: 10, of which 5 were waited for; matrix products, arithmetic and copies ran while one was open for 0% of the time, Pallas kernels for 18%

profile of v6, /device:TPU:1, one launch (start us, length us, event | category | flops | bytes accessed | tf_op | source)
XLA Modules:
  0.0 89.3 jit_solution(13860938165429594832)
XLA Ops:
  0.6 0.0 copy-start
  0.6 1.1 %constant_dynamic-slice_fusion = f32[128,896]{1,0:T(8,128)S(1)} fusion(f32[128,1792]{1,0:T(8,128)} %refs_4_.1, s32[]{:T(128)S(6)} %select_n.31), kind=kLoop, calls=%fused_computation | loop fusion | bytes 917508 | tf_op jit(solution)/shard_map/dynamic_slice | solution.py:390
  1.8 0.0 copy-start.3
  1.8 1.5 %collective-permute-start.1 = (f32[128,896]{1,0:T(8,128)S(1)}, f32[128,896]{1,0:T(8,128)S(1)}, u32[]{:S(2)}, u32[]{:S(2)}) collective-permute-start(f32[128,896]{1,0:T(8,128)S(1)} %constant_dynamic-slice_fusion), channel_id=1, source_target_pairs={{0,1},{1,0},{2,3},{3,2},{4,5},{5,4},{6,7},{7,6},{8,9},{9,8},{10,11... | collective-permute-start | bytes 1376264 | tf_op jit(solution)/shard_map/swap_inputs/ppermute | solution.py:394
  3.3 0.1 collective-permute-start
  3.4 0.0 copy-done.3
  3.4 0.5 collective-permute-start.2
  3.9 0.1 stack.27.place_ref
  3.9 0.8 collective-permute-done.2.far_counts_ref
  4.7 0.6 collective-permute-done.other_ref
  5.3 0.0 collective-permute-done.1.far_ref
  5.3 0.0 copy-done
  5.3 0.0 copy-start.1
  5.3 0.9 %copy-done.1 = f32[128,512]{1,0:T(8,128)S(1)} copy-done((f32[128,512]{1,0:T(8,128)S(1)}, f32[128,512]{1,0:T(8,128)}, u32[]{:S(2)}) %copy-start.1) | copy-done | bytes 262168
  6.3 3.0 %local_products.1 = (f32[896,128]{1,0:T(8,128)S(1)}, f32[896,128]{1,0:T(8,128)S(1)}, f32[896,128]{1,0:T(8,128)S(1)}, f32[896,128]{1,0:T(8,128)S(1)}, f32[640,128]{1,0:T(8,128)S(1)}) custom-call(s32[6]{0:T(128)S(1)} %stack.27.place_ref, f32[128,512]{1,0:T(8,128)S(1)} %copy-done.1, f32[128,512]{1,0:T(8,128)S(1)} %collective-permute-done.other_ref, ...), custom_call_target="tpu_custom_call" | custom-call | tf_op jit(solution)/shard_map/local_products/pallas_call | solution.py:127
  9.3 2.6 %collective-permute-start.3 = (f32[896,128]{1,0:T(8,128)S(1)}, f32[896,128]{1,0:T(8,128)S(1)}, u32[]{:S(2)}, u32[]{:S(2)}) collective-permute-start(f32[896,128]{1,0:T(8,128)S(1)} %get-tuple-element.17), channel_id=1, source_target_pairs={{0,8},{1,25},{8,0},{9,17},{16,24},{17,9},{24,16},{25,1},{32,40},{3... | collective-permute-start | bytes 1376264 | tf_op jit(solution)/shard_map/terms_along_x/ppermute | solution.py:423
  11.9 2.7 %collective-permute-start.4 = (f32[896,128]{1,0:T(8,128)S(1)}, f32[896,128]{1,0:T(8,128)S(1)}, u32[]{:S(2)}, u32[]{:S(2)}) collective-permute-start(f32[896,128]{1,0:T(8,128)S(1)} %get-tuple-element.18), channel_id=1, source_target_pairs={{0,32},{1,97},{8,40},{9,105},{16,48},{17,113},{24,56},{25,121},{32... | collective-permute-start | bytes 1376264 | tf_op jit(solution)/shard_map/terms_along_y/ppermute | solution.py:423
  14.7 3.8 %collective-permute-start.5 = (f32[896,128]{1,0:T(8,128)S(1)}, f32[896,128]{1,0:T(8,128)S(1)}, u32[]{:S(2)}, u32[]{:S(2)}) collective-permute-start(f32[896,128]{1,0:T(8,128)S(1)} %get-tuple-element.19), channel_id=1, source_target_pairs={{0,2},{1,7},{2,0},{3,5},{4,6},{5,3},{6,4},{7,1},{8,10},{9,15},{10,... | collective-permute-start | bytes 1376264 | tf_op jit(solution)/shard_map/terms_along_z/ppermute | solution.py:423
  18.4 0.0 collective-permute-done.3.refs_1_
  18.4 2.1 %collective-permute-done.4.refs_2_ = f32[896,128]{1,0:T(8,128)S(1)} collective-permute-done((f32[896,128]{1,0:T(8,128)S(1)}, f32[896,128]{1,0:T(8,128)S(1)}, u32[]{:S(2)}, u32[]{:S(2)}) %collective-permute-start.4) | collective-permute-done | bytes 458784 | tf_op jit(solution)/shard_map/terms_along_y/ppermute | solution.py:423
  20.5 3.8 %collective-permute-done.5.refs_3_ = f32[896,128]{1,0:T(8,128)S(1)} collective-permute-done((f32[896,128]{1,0:T(8,128)S(1)}, f32[896,128]{1,0:T(8,128)S(1)}, u32[]{:S(2)}, u32[]{:S(2)}) %collective-permute-start.5) | collective-permute-done | bytes 458784 | tf_op jit(solution)/shard_map/terms_along_z/ppermute | solution.py:423
  24.3 0.2 combine_terms.1
  24.5 18.4 %all_to_all.10 = f32[64,1,3072]{2,1,0:T(1,128)S(1)} all-to-all(f32[64,1,3072]{2,1,0:T(1,128)S(1)} %bitcast.15), channel_id=1, replica_groups=mesh['grp'=16,'z'=4,'core'=2] {'grp','z'}, dimensions={0} | all-to-all | bytes 1572864 | tf_op jit(solution)/shard_map/exchange/all_to_all | solution.py:417
  42.9 0.1 sum_pieces.1
  43.0 17.2 %all_to_all.11 = f32[64,1,3072]{2,1,0:T(1,128)S(1)} all-to-all(f32[64,1,3072]{2,1,0:T(1,128)S(1)} %bitcast.14), channel_id=1, replica_groups=mesh['grp'=16,'z'=4,'core'=2] {'grp','z'}, dimensions={0} | all-to-all | bytes 1572864 | tf_op jit(solution)/shard_map/exchange/all_to_all | solution.py:417
  60.2 0.0 copy-start.2
  60.2 4.5 %collective-permute-start.6 = (f32[1536,128]{1,0:T(8,128)S(1)}, f32[1536,128]{1,0:T(8,128)S(1)}, u32[]{:S(2)}, u32[]{:S(2)}) collective-permute-start(f32[1536,128]{1,0:T(8,128)S(1)} %bitcast.11), channel_id=1, source_target_pairs={{0,1},{1,0},{2,3},{3,2},{4,5},{5,4},{6,7},{7,6},{8,9},{9,8},{10,11... | collective-permute-start | bytes 2359304 | tf_op jit(solution)/shard_map/swap_copies/ppermute | solution.py:431
  64.6 1.9 %collective-permute-done.6.far_ref = f32[1536,128]{1,0:T(8,128)S(1)} collective-permute-done((f32[1536,128]{1,0:T(8,128)S(1)}, f32[1536,128]{1,0:T(8,128)S(1)}, u32[]{:S(2)}, u32[]{:S(2)}) %collective-permute-start.6) | collective-permute-done | bytes 786464 | tf_op jit(solution)/shard_map/swap_copies/ppermute | solution.py:431
  66.5 0.1 unpack_sums.1
  66.7 0.3 collective-permute-start.9
  67.0 0.8 collective-permute-start.8
  67.8 1.3 %collective-permute-start.7 = (f32[2,896,128]{2,1,0:T(8,128)S(1)}, f32[2,896,128]{2,1,0:T(8,128)S(1)}, u32[]{:S(2)}, u32[]{:S(2)}) collective-permute-start(f32[2,896,128]{2,1,0:T(8,128)S(1)} %get-tuple-element.24.refs_0_), channel_id=1, source_target_pairs={{0,8},{1,25},{8,0},{9,17},{16,24},{17,9},{24,16},{25,1},{32,40},{3... | collective-permute-start | bytes 2752520 | tf_op jit(solution)/shard_map/quarters_along_x/ppermute | solution.py:437
  69.1 0.0 copy-done.2
  69.1 15.9 %factor_gram.1 = (f32[4,192,128]{2,1,0:T(8,128)S(1)}, f32[64,512]{1,0:T(8,128)}) custom-call(s32[6]{0:T(128)S(1)} %stack.27.place_ref, f32[640,128]{1,0:T(8,128)S(1)} %get-tuple-element.20.near_ref, f32[640,128]{1,0:T(8,128)S(1)} %get-tuple-element.21.far_ref, f32[128,512]{1,0:T(8,128)S(1)} %copy-done.2), custom_call_target="tpu_custom_call" | custom-call | flops 20000000000 | bytes 4000000 | tf_op jit(solution)/shard_map/factor_gram/pallas_call | solution.py:304
  85.0 0.0 collective-permute-done.9.refs_3_
  85.0 0.0 collective-permute-done.8.refs_2_
  85.0 0.0 collective-permute-done.7.refs_1_
  85.0 4.3 %apply_factor.1 = (f32[128,1792]{1,0:T(8,128)}, f32[64,1792]{1,0:T(8,128)}) custom-call(s32[6]{0:T(128)S(1)} %stack.27.place_ref, f32[4,192,128]{2,1,0:T(8,128)S(1)} %get-tuple-element.23.mixed_ref, f32[2,896,128]{2,1,0:T(8,128)S(1)} %get-tuple-element.24.refs_0_, f32[2,896,128]{2,1,0:T(8,128)S(1)} %collective-permute-done.7.refs_1_, ...), custom_call_target="tpu_custom_call" | custom-call | tf_op jit(solution)/shard_map/apply_factor/pallas_call | solution.py:356
Async XLA Ops:
  0.6 4.7 %copy-start = (f32[128,1792]{1,0:T(8,128)S(1)}, f32[128,1792]{1,0:T(8,128)}, u32[]{:S(2)}) copy-start(f32[128,1792]{1,0:T(8,128)} %refs_4_.1) | copy-start | bytes 2752516
  1.8 1.6 %copy-start.3 = (s32[128]{0:T(128)S(1)}, s32[128]{0:T(128)}, u32[]{:S(2)}) copy-start(s32[128]{0:T(128)} %param.5) | copy-start | bytes 1540
  1.8 3.5 %collective-permute-start.1 = (f32[128,896]{1,0:T(8,128)S(1)}, f32[128,896]{1,0:T(8,128)S(1)}, u32[]{:S(2)}, u32[]{:S(2)}) collective-permute-start(f32[128,896]{1,0:T(8,128)S(1)} %constant_dynamic-slice_fusion), channel_id=1, source_target_pairs={{0,1},{1,0},{2,3},{3,2},{4,5},{5,4},{6,7},{7,6},{8,9},{9,8},{10,11... | collective-permute-start | bytes 1376264 | tf_op jit(solution)/shard_map/swap_inputs/ppermute | solution.py:394
  3.3 2.0 %collective-permute-start = (f32[128,512]{1,0:T(8,128)}, f32[128,512]{1,0:T(8,128)S(1)}, u32[]{:S(2)}, u32[]{:S(2)}) collective-permute-start(f32[128,512]{1,0:T(8,128)} %panel_ref.3), channel_id=1, source_target_pairs={{0,1},{1,0},{2,3},{3,2},{4,5},{5,4},{6,7},{7,6},{8,9},{9,8},{10,11... | collective-permute-start | bytes 786440 | tf_op jit(solution)/shard_map/swap_inputs/ppermute | solution.py:393
  3.4 1.3 %collective-permute-start.2 = (s32[1,128]{1,0:T(1,128)S(1)}, s32[1,128]{1,0:T(1,128)S(1)}, u32[]{:S(2)}, u32[]{:S(2)}) collective-permute-start(s32[1,128]{1,0:T(1,128)S(1)} %bitcast.16), channel_id=1, source_target_pairs={{0,1},{1,0},{2,3},{3,2},{4,5},{5,4},{6,7},{7,6},{8,9},{9,8},{10,11... | collective-permute-start | bytes 1544 | tf_op jit(solution)/shard_map/swap_inputs/ppermute | solution.py:392
  5.3 1.0 %copy-start.1 = (f32[128,512]{1,0:T(8,128)S(1)}, f32[128,512]{1,0:T(8,128)}, u32[]{:S(2)}) copy-start(f32[128,512]{1,0:T(8,128)} %panel_ref.3) | copy-start | bytes 786436
  9.3 9.1 %collective-permute-start.3 = (f32[896,128]{1,0:T(8,128)S(1)}, f32[896,128]{1,0:T(8,128)S(1)}, u32[]{:S(2)}, u32[]{:S(2)}) collective-permute-start(f32[896,128]{1,0:T(8,128)S(1)} %get-tuple-element.17), channel_id=1, source_target_pairs={{0,8},{1,25},{8,0},{9,17},{16,24},{17,9},{24,16},{25,1},{32,40},{3... | collective-permute-start | bytes 1376264 | tf_op jit(solution)/shard_map/terms_along_x/ppermute | solution.py:423
  11.9 8.6 %collective-permute-start.4 = (f32[896,128]{1,0:T(8,128)S(1)}, f32[896,128]{1,0:T(8,128)S(1)}, u32[]{:S(2)}, u32[]{:S(2)}) collective-permute-start(f32[896,128]{1,0:T(8,128)S(1)} %get-tuple-element.18), channel_id=1, source_target_pairs={{0,32},{1,97},{8,40},{9,105},{16,48},{17,113},{24,56},{25,121},{32... | collective-permute-start | bytes 1376264 | tf_op jit(solution)/shard_map/terms_along_y/ppermute | solution.py:423
  14.7 9.6 %collective-permute-start.5 = (f32[896,128]{1,0:T(8,128)S(1)}, f32[896,128]{1,0:T(8,128)S(1)}, u32[]{:S(2)}, u32[]{:S(2)}) collective-permute-start(f32[896,128]{1,0:T(8,128)S(1)} %get-tuple-element.19), channel_id=1, source_target_pairs={{0,2},{1,7},{2,0},{3,5},{4,6},{5,3},{6,4},{7,1},{8,10},{9,15},{10,... | collective-permute-start | bytes 1376264 | tf_op jit(solution)/shard_map/terms_along_z/ppermute | solution.py:423
  60.2 8.9 %copy-start.2 = (f32[128,512]{1,0:T(8,128)S(1)}, f32[128,512]{1,0:T(8,128)}, u32[]{:S(2)}) copy-start(f32[128,512]{1,0:T(8,128)} %panel_ref.3) | copy-start | bytes 786436
  60.2 6.4 %collective-permute-start.6 = (f32[1536,128]{1,0:T(8,128)S(1)}, f32[1536,128]{1,0:T(8,128)S(1)}, u32[]{:S(2)}, u32[]{:S(2)}) collective-permute-start(f32[1536,128]{1,0:T(8,128)S(1)} %bitcast.11), channel_id=1, source_target_pairs={{0,1},{1,0},{2,3},{3,2},{4,5},{5,4},{6,7},{7,6},{8,9},{9,8},{10,11... | collective-permute-start | bytes 2359304 | tf_op jit(solution)/shard_map/swap_copies/ppermute | solution.py:431
  66.7 18.3 %collective-permute-start.9 = (f32[2,896,128]{2,1,0:T(8,128)S(1)}, f32[2,896,128]{2,1,0:T(8,128)S(1)}, u32[]{:S(2)}, u32[]{:S(2)}) collective-permute-start(f32[2,896,128]{2,1,0:T(8,128)S(1)} %get-tuple-element.24.refs_0_), channel_id=1, source_target_pairs={{0,2},{1,7},{2,0},{3,5},{4,6},{5,3},{6,4},{7,1},{8,10},{9,15},{10,... | collective-permute-start | bytes 2752520 | tf_op jit(solution)/shard_map/quarters_along_z/ppermute | solution.py:437
  67.0 18.0 %collective-permute-start.8 = (f32[2,896,128]{2,1,0:T(8,128)S(1)}, f32[2,896,128]{2,1,0:T(8,128)S(1)}, u32[]{:S(2)}, u32[]{:S(2)}) collective-permute-start(f32[2,896,128]{2,1,0:T(8,128)S(1)} %get-tuple-element.24.refs_0_), channel_id=1, source_target_pairs={{0,32},{1,97},{8,40},{9,105},{16,48},{17,113},{24,56},{25,121},{32... | collective-permute-start | bytes 2752520 | tf_op jit(solution)/shard_map/quarters_along_y/ppermute | solution.py:437
  67.8 17.2 %collective-permute-start.7 = (f32[2,896,128]{2,1,0:T(8,128)S(1)}, f32[2,896,128]{2,1,0:T(8,128)S(1)}, u32[]{:S(2)}, u32[]{:S(2)}) collective-permute-start(f32[2,896,128]{2,1,0:T(8,128)S(1)} %get-tuple-element.24.refs_0_), channel_id=1, source_target_pairs={{0,8},{1,25},{8,0},{9,17},{16,24},{17,9},{24,16},{25,1},{32,40},{3... | collective-permute-start | bytes 2752520 | tf_op jit(solution)/shard_map/quarters_along_x/ppermute | solution.py:437

commit v7 on v6

--- a/solution.py
+++ b/solution.py
@@ -13,6 +13,7 @@
 strip = 32
 chips = ("grp", "z")
 classes = 4
+shares = (3, 3, 2, 2)
 
 
 def product(left, right, left_dim=1, right_dim=0):
@@ -38,6 +39,17 @@
     return lax.dot_general(
         jnp.concatenate([lh, lh, lm, lh, ll, lm], left_dim),
         jnp.concatenate([rh, rm, rh, rl, rh, rm], right_dim),
+        (((left_dim,), (right_dim,)), ((), ())),
+        preferred_element_type=jnp.float32,
+    )
+
+
+def stacked_two(left, right, left_dim=1, right_dim=0):
+    lh, ll, _ = three_parts(left)
+    rh, rl, _ = three_parts(right)
+    return lax.dot_general(
+        jnp.concatenate([lh, lh, ll], left_dim),
+        jnp.concatenate([rh, rl, rh], right_dim),
         (((left_dim,), (right_dim,)), ((), ())),
         preferred_element_type=jnp.float32,
     )
@@ -86,7 +98,7 @@
 
 
 def products_kernel(place_ref, panel_ref, other_ref, trail_ref, far_ref, counts_ref, far_counts_ref, *refs, total_rows):
-    outs, gram, (pt, wp, wt, quarters) = refs[:classes], refs[classes], refs[classes + 1 :]
+    outs, (pt, wp, wt, quarters, gram, shared) = refs[:classes], refs[classes:]
     core = place_ref[0]
     own, width = panel_ref.shape
     half = trail_ref.shape[1]
@@ -101,12 +113,10 @@
     step = 2 * tile
     for c in range(0, half, step):
         n = min(step, half - c)
-        part = product(pt[...], wt[:, c : c + n])
+        part = stacked_two(pt[...], wt[:, c : c + n])
         for k in range(classes):
             for j in range(0, n, tile):
                 quarters[k, c + j : c + j + tile, :] = part[k * tile : (k + 1) * tile, j : j + tile]
-    for m in range(classes):
-        outs[m][...] = quarters[place_ref[1 + m]]
     near = pl.multiple_of(core * step, tile)
     first = product(pt[pl.ds(near, tile), :], wp[:, pl.ds(near, step)])
     gram[0:tile, :] = first[:, :tile]
@@ -117,17 +127,31 @@
     last = product(pt[pl.ds(near, tile), :], wp[:, step:])
     gram[3 * tile : 4 * tile, :] = last[:, :tile]
     gram[4 * tile :, :] = last[:, tile:]
-
-
-def products(place, panel, other, trailing, far, counts, far_counts, total_rows):
+    most = max(shares)
+    chip_count = shared.shape[1] // most
+    first = 0
+    for k, share in enumerate(shares):
+        if share == most:
+            shared[k] = gram[first : first + chip_count * share, :]
+        else:
+            shared[k] = jnp.zeros_like(shared[k])
+            for q in range(chip_count):
+                shared[k, q * most : q * most + share, :] = gram[first + q * share : first + (q + 1) * share, :]
+        first += chip_count * share
+    for m in range(classes):
+        outs[m][0:half, :] = quarters[place_ref[1 + m]]
+        outs[m][half:, :] = shared[place_ref[1 + m]]
+
+
+def products(place, panel, other, trailing, far, counts, far_counts, chip_count, total_rows):
     own, width = panel.shape
     half = far.shape[1]
     gram_rows = len(gram_blocks[0]) * tile
+    sent_rows = half + max(shares) * chip_count
     whole = lambda shape: pl.BlockSpec(shape, lambda i, place: (0, 0))
     return pl.pallas_call(
         functools.partial(products_kernel, total_rows=total_rows),
-        out_shape=[jax.ShapeDtypeStruct((half, tile), jnp.float32)] * classes
-        + [jax.ShapeDtypeStruct((gram_rows, tile), jnp.float32)],
+        out_shape=[jax.ShapeDtypeStruct((sent_rows, tile), jnp.float32)] * classes,
         grid_spec=pltpu.PrefetchScalarGridSpec(
             num_scalar_prefetch=1,
             grid=(1,),
@@ -139,66 +163,72 @@
                 whole((1, own)),
                 whole((1, own)),
             ],
-            out_specs=[whole((half, tile))] * classes + [whole((gram_rows, tile))],
+            out_specs=[whole((sent_rows, tile))] * classes,
             scratch_shapes=[
                 pltpu.VMEM((width, 2 * own), jnp.float32),
                 pltpu.VMEM((2 * own, width), jnp.float32),
                 pltpu.VMEM((2 * own, half), jnp.float32),
                 pltpu.VMEM((classes, half, tile), jnp.float32),
+                pltpu.VMEM((gram_rows, tile), jnp.float32),
+                pltpu.VMEM((classes, max(shares) * chip_count, tile), jnp.float32),
             ],
         ),
         compiler_params=pltpu.CompilerParams(vmem_limit_bytes=32 * 1024 * 1024),
     )(place, panel, other, trailing, far, counts, far_counts)
 
 
-def combine_kernel(gram_ref, *refs, chip_count):
+def combine_kernel(*refs, chip_count, chunk):
     parts, out_ref = refs[:classes], refs[classes]
-    size = gram_ref.shape[0] // chip_count
-    chunk = parts[0].shape[0] // chip_count
+    most = max(shares)
+    piece = chunk + most
+
+    def added(at, rows):
+        side = slice(at, at + rows)
+        return (parts[0][side, :] + parts[1][side, :]) + (parts[2][side, :] + parts[3][side, :])
+
     for q in range(chip_count):
-        side = slice(q * chunk, (q + 1) * chunk)
-        cross = (parts[0][side, :] + parts[1][side, :]) + (parts[2][side, :] + parts[3][side, :])
-        gram = gram_ref[q * size : (q + 1) * size, :]
-        out_ref[q * (size + chunk) : (q + 1) * (size + chunk), :] = jnp.concatenate([gram, cross], 0)
-
-
-def combine(gram, parts, chip_count):
+        gram = added(chip_count * chunk + q * most, most)
+        out_ref[q * piece : (q + 1) * piece, :] = jnp.concatenate([gram, added(q * chunk, chunk)], 0)
+
+
+def combine(parts, chip_count, chunk):
     vmem = pl.BlockSpec(memory_space=pltpu.VMEM)
     return pl.pallas_call(
-        functools.partial(combine_kernel, chip_count=chip_count),
-        out_shape=jax.ShapeDtypeStruct((gram.shape[0] + parts[0].shape[0], tile), jnp.float32),
-        in_specs=[vmem] * (1 + classes),
+        functools.partial(combine_kernel, chip_count=chip_count, chunk=chunk),
+        out_shape=jax.ShapeDtypeStruct(parts[0].shape, jnp.float32),
+        in_specs=[vmem] * classes,
         out_specs=vmem,
         compiler_params=pltpu.CompilerParams(vmem_limit_bytes=16 * 1024 * 1024),
-    )(gram, *parts)
-
-
-def sum_kernel(pieces_ref, copies_ref, *, size, kinds):
-    both = pieces_ref.shape[0] // len(kinds)
-    totals = []
+    )(*parts)
+
+
+def sum_kernel(pieces_ref, copies_ref, total_ref, *, chunk, kinds):
+    most = max(shares)
+    piece = chunk + most
+    both = chunk + sum(shares)
     for k in range(classes):
         total = None
         for q, kind in enumerate(kinds):
             if kind == k:
-                piece = pieces_ref[q * both : (q + 1) * both, :]
-                total = piece if total is None else total + piece
-        totals.append(total)
-    gram = (totals[0] + totals[1]) + (totals[2] + totals[3])
-    is_gram = lax.broadcasted_iota(jnp.int32, (both, tile), 0) < size
+                part = pieces_ref[q * piece : (q + 1) * piece, :]
+                total = part if total is None else total + part
+        total_ref[k, 0:piece, :] = total
+    gram = [total_ref[k, 0:share, :] for k, share in enumerate(shares)]
     for k in range(classes):
-        copy = jnp.where(is_gram, gram, totals[k])
+        copy = jnp.concatenate(gram + [total_ref[k, most:piece, :]], 0)
         for q, kind in enumerate(kinds):
             if kind == k:
                 copies_ref[q * both : (q + 1) * both, :] = copy
 
 
-def sum_pieces(pieces, size, kinds):
+def sum_pieces(pieces, chunk, kinds):
     vmem = pl.BlockSpec(memory_space=pltpu.VMEM)
     return pl.pallas_call(
-        functools.partial(sum_kernel, size=size, kinds=kinds),
-        out_shape=jax.ShapeDtypeStruct(pieces.shape, jnp.float32),
+        functools.partial(sum_kernel, chunk=chunk, kinds=kinds),
+        out_shape=jax.ShapeDtypeStruct((len(kinds) * (chunk + sum(shares)), tile), jnp.float32),
         in_specs=[vmem],
         out_specs=vmem,
+        scratch_shapes=[pltpu.VMEM((classes, chunk + max(shares) + 7, tile), jnp.float32)],
         compiler_params=pltpu.CompilerParams(vmem_limit_bytes=16 * 1024 * 1024),
     )(pieces)
 
@@ -209,7 +239,11 @@
     both = size + chunk
     for at, (copies_ref, gram_ref) in enumerate(((near_ref, near_gram), (far_ref, far_gram))):
         for q in range(chip_count):
-            gram_ref[q * size : (q + 1) * size, :] = copies_ref[q * both : q * both + size, :]
+            at_row, first = q * both, 0
+            for share in shares:
+                gram_ref[first + q * share : first + (q + 1) * share, :] = copies_ref[at_row : at_row + share, :]
+                at_row += share
+                first += chip_count * share
             quarters_ref[at, q * chunk : (q + 1) * chunk, :] = copies_ref[q * both + size : (q + 1) * both, :]
 
 
@@ -342,7 +376,7 @@
                 ],
                 1,
             )
-            term = product(left[m // 2], right)
+            term = stacked_two(left[m // 2], right)
             out = term if out is None else out + term
         for part, where in ((out[:, :tile], core), (out[:, tile:], 1 - core)):
             at = pl.ds(pl.multiple_of(where * half + c, tile), tile)
@@ -378,7 +412,7 @@
     members = 2 * depth
     chip_count = groups * depth
     chunk = half // chip_count
-    gram_chunk = len(gram_blocks[0]) * tile // chip_count
+    gram_chunk = sum(shares)
     kinds = [kind_of(g % side, g // side, z) for g in range(groups) for z in range(depth)]
     group, z, core = lax.axis_index("grp"), lax.axis_index("z"), lax.axis_index("core")
     kind = kind_of(group % side, group // side, z)
@@ -393,8 +427,8 @@
         other_panel = lax.ppermute(panel, "core", swap)
         far_trail = lax.ppermute(sent_trail, "core", swap)
     with jax.named_scope("local_products"):
-        *terms, gram_terms = products(
-            place, panel, other_panel, trailing, far_trail, count_row, far_counts, own * groups * members
+        terms = products(
+            place, panel, other_panel, trailing, far_trail, count_row, far_counts, chip_count, own * groups * members
         )
     def pairs(before, after):
         out = []
@@ -422,10 +456,10 @@
         with jax.named_scope("terms_" + name):
             parts.append(lax.ppermute(terms[1 + m], axis, pairs(before, after)))
     with jax.named_scope("combine_terms"):
-        pieces = combine(gram_terms, parts, chip_count)
+        pieces = combine(parts, chip_count, chunk)
     pieces = exchange(pieces)
     with jax.named_scope("sum_pieces"):
-        copies = sum_pieces(pieces, gram_chunk, kinds)
+        copies = sum_pieces(pieces, chunk, kinds)
     copies = exchange(copies)
     with jax.named_scope("swap_copies"):
         far_copies = lax.ppermute(copies, "core", swap)

time: 89.5 us -> 86.2 us (0.963)
  blocking collectives: 35.6 us -> 33.1 us
  Pallas kernels: 23.6 us -> 21.6 us
  waiting for transfers between devices: 9.17 us -> 10.2 us
    all_to_all x2, blocking collectives: 35.6 us -> 33.1 us  [exchange(): lax.all_to_all(rows.reshape(chip_count, 1, -1), chips, 0, 0, tiled=True)]
    pallas_call x1, Pallas kernels: 4.28 us -> 3.01 us  [finish(): pl.pallas_call(finish_kernel, out_shape=(jax.ShapeDtypeStruct((own, trail...]
    ppermute x3, waiting for transfers between devices: 5.86 us -> 6.92 us  [local(): parts.append(lax.ppermute(terms[1 + m], axis, pairs(before, after)))]
  transfers between devices with their start and end apart: 10 -> 10, of which waited for: 5 -> 6; matrix products, arithmetic and copies ran while one was open for 0% -> 0% of each run, Pallas kernels for 18% -> 18%
where the time goes in v7:
time: 86.2 us; the launch traced here: 86 us
  blocking collectives  33.1 us (38%)
  Pallas kernels  21.6 us (25%)
  starting transfers between devices  18.2 us (21%)
  waiting for transfers between devices  10.2 us (12%)
  local copies, waits for them, and re-layouts  2.18 us (3%)
    all_to_all x2, blocking collectives, exchange(): lax.all_to_all(rows.reshape(chip_count, 1, -1), chips, 0, 0, tiled=True)  33.1 us
    pallas_call x1, Pallas kernels, factor(): pl.pallas_call(factor_kernel, out_shape=(jax.ShapeDtypeStruct((width // t...  15.9 us
    ppermute x3, starting transfers between devices, local(): parts.append(lax.ppermute(terms[1 + m], axis, pairs(before, after)))  9.13 us
    ppermute x3, waiting for transfers between devices, local(): parts.append(lax.ppermute(terms[1 + m], axis, pairs(before, after)))  6.92 us
    ppermute x1, starting transfers between devices, local(): far_copies = lax.ppermute(copies, 'core', swap)  4.53 us
    pallas_call x1, Pallas kernels, finish(): pl.pallas_call(finish_kernel, out_shape=(jax.ShapeDtypeStruct((own, trail...  3.01 us
    ppermute x3, starting transfers between devices, local(): quarters.append(lax.ppermute(quarter, axis, pairs(before, after)))  2.48 us
    pallas_call x1, Pallas kernels, products(): pl.pallas_call(functools.partial(products_kernel, total_rows=total_rows),...  2.15 us
  transfers between devices with their start and end apart: 10, of which 6 were waited for; matrix products, arithmetic and copies ran while one was open for 0% of the time, Pallas kernels for 18%

profile of v7, /device:TPU:1, one launch (start us, length us, event | category | flops | bytes accessed | tf_op | source)
XLA Modules:
  0.0 86.0 jit_solution(11911927407127347595)
XLA Ops:
  0.6 0.0 copy-start
  0.6 1.1 %constant_dynamic-slice_fusion = f32[128,896]{1,0:T(8,128)S(1)} fusion(f32[128,1792]{1,0:T(8,128)} %refs_4_.1, s32[]{:T(128)S(6)} %select_n.31), kind=kLoop, calls=%fused_computation | loop fusion | bytes 917508 | tf_op jit(solution)/shard_map/dynamic_slice | solution.py:424
  1.8 0.0 copy-start.3
  1.8 1.5 %collective-permute-start.1 = (f32[128,896]{1,0:T(8,128)S(1)}, f32[128,896]{1,0:T(8,128)S(1)}, u32[]{:S(2)}, u32[]{:S(2)}) collective-permute-start(f32[128,896]{1,0:T(8,128)S(1)} %constant_dynamic-slice_fusion), channel_id=1, source_target_pairs={{0,1},{1,0},{2,3},{3,2},{4,5},{5,4},{6,7},{7,6},{8,9},{9,8},{10,11... | collective-permute-start | bytes 1376264 | tf_op jit(solution)/shard_map/swap_inputs/ppermute | solution.py:428
  3.3 0.1 collective-permute-start
  3.4 0.0 copy-done.3
  3.4 0.5 collective-permute-start.2
  3.9 0.1 stack.27.place_ref
  3.9 0.8 collective-permute-done.2.far_counts_ref
  4.7 0.6 collective-permute-done.other_ref
  5.3 0.0 collective-permute-done.1.far_ref
  5.3 0.0 copy-done
  5.3 0.0 copy-start.1
  5.3 0.9 %copy-done.1 = f32[128,512]{1,0:T(8,128)S(1)} copy-done((f32[128,512]{1,0:T(8,128)S(1)}, f32[128,512]{1,0:T(8,128)}, u32[]{:S(2)}) %copy-start.1) | copy-done | bytes 262168
  6.3 2.2 %local_products.1 = (f32[1088,128]{1,0:T(8,128)S(1)}, f32[1088,128]{1,0:T(8,128)S(1)}, f32[1088,128]{1,0:T(8,128)S(1)}, f32[1088,128]{1,0:T(8,128)S(1)}) custom-call(s32[6]{0:T(128)S(1)} %stack.27.place_ref, f32[128,512]{1,0:T(8,128)S(1)} %copy-done.1, f32[128,512]{1,0:T(8,128)S(1)} %collective-permute-done.other_ref, f32[128,1792]{1,0:T(8,128)S(1)} %copy-done, ...), custom_call_target="tpu_custom_call" | custom-call | tf_op jit(solution)/shard_map/local_products/pallas_call | solution.py:152
  8.4 2.6 %collective-permute-start.3 = (f32[1088,128]{1,0:T(8,128)S(1)}, f32[1088,128]{1,0:T(8,128)S(1)}, u32[]{:S(2)}, u32[]{:S(2)}) collective-permute-start(f32[1088,128]{1,0:T(8,128)S(1)} %get-tuple-element.15), channel_id=1, source_target_pairs={{0,8},{1,25},{8,0},{9,17},{16,24},{17,9},{24,16},{25,1},{32,40},{3... | collective-permute-start | bytes 1671176 | tf_op jit(solution)/shard_map/terms_along_x/ppermute | solution.py:457
  11.1 2.7 %collective-permute-start.4 = (f32[1088,128]{1,0:T(8,128)S(1)}, f32[1088,128]{1,0:T(8,128)S(1)}, u32[]{:S(2)}, u32[]{:S(2)}) collective-permute-start(f32[1088,128]{1,0:T(8,128)S(1)} %get-tuple-element.16), channel_id=1, source_target_pairs={{0,32},{1,97},{8,40},{9,105},{16,48},{17,113},{24,56},{25,121},{32... | collective-permute-start | bytes 1671176 | tf_op jit(solution)/shard_map/terms_along_y/ppermute | solution.py:457
  13.8 3.8 %collective-permute-start.5 = (f32[1088,128]{1,0:T(8,128)S(1)}, f32[1088,128]{1,0:T(8,128)S(1)}, u32[]{:S(2)}, u32[]{:S(2)}) collective-permute-start(f32[1088,128]{1,0:T(8,128)S(1)} %get-tuple-element.17), channel_id=1, source_target_pairs={{0,2},{1,7},{2,0},{3,5},{4,6},{5,3},{6,4},{7,1},{8,10},{9,15},{10,... | collective-permute-start | bytes 1671176 | tf_op jit(solution)/shard_map/terms_along_z/ppermute | solution.py:457
  17.6 0.5 collective-permute-done.3.refs_1_
  18.1 2.6 %collective-permute-done.4.refs_2_ = f32[1088,128]{1,0:T(8,128)S(1)} collective-permute-done((f32[1088,128]{1,0:T(8,128)S(1)}, f32[1088,128]{1,0:T(8,128)S(1)}, u32[]{:S(2)}, u32[]{:S(2)}) %collective-permute-start.4) | collective-permute-done | bytes 557088 | tf_op jit(solution)/shard_map/terms_along_y/ppermute | solution.py:457
  20.7 3.8 %collective-permute-done.5.refs_3_ = f32[1088,128]{1,0:T(8,128)S(1)} collective-permute-done((f32[1088,128]{1,0:T(8,128)S(1)}, f32[1088,128]{1,0:T(8,128)S(1)}, u32[]{:S(2)}, u32[]{:S(2)}) %collective-permute-start.5) | collective-permute-done | bytes 557088 | tf_op jit(solution)/shard_map/terms_along_z/ppermute | solution.py:457
  24.5 0.2 combine_terms.1
  24.7 16.1 %all_to_all.10 = f32[64,1,2176]{2,1,0:T(1,128)S(1)} all-to-all(f32[64,1,2176]{2,1,0:T(1,128)S(1)} %bitcast.14), channel_id=1, replica_groups=mesh['grp'=16,'z'=4,'core'=2] {'grp','z'}, dimensions={0} | all-to-all | bytes 1114112 | tf_op jit(solution)/shard_map/exchange/all_to_all | solution.py:451
  40.8 0.1 sum_pieces.1
  40.9 17.0 %all_to_all.11 = f32[64,1,3072]{2,1,0:T(1,128)S(1)} all-to-all(f32[64,1,3072]{2,1,0:T(1,128)S(1)} %bitcast.13), channel_id=1, replica_groups=mesh['grp'=16,'z'=4,'core'=2] {'grp','z'}, dimensions={0} | all-to-all | bytes 1572864 | tf_op jit(solution)/shard_map/exchange/all_to_all | solution.py:451
  57.9 0.0 copy-start.2
  57.9 4.5 %collective-permute-start.6 = (f32[1536,128]{1,0:T(8,128)S(1)}, f32[1536,128]{1,0:T(8,128)S(1)}, u32[]{:S(2)}, u32[]{:S(2)}) collective-permute-start(f32[1536,128]{1,0:T(8,128)S(1)} %bitcast.11), channel_id=1, source_target_pairs={{0,1},{1,0},{2,3},{3,2},{4,5},{5,4},{6,7},{7,6},{8,9},{9,8},{10,11... | collective-permute-start | bytes 2359304 | tf_op jit(solution)/shard_map/swap_copies/ppermute | solution.py:465
  62.4 1.9 %collective-permute-done.6.far_ref = f32[1536,128]{1,0:T(8,128)S(1)} collective-permute-done((f32[1536,128]{1,0:T(8,128)S(1)}, f32[1536,128]{1,0:T(8,128)S(1)}, u32[]{:S(2)}, u32[]{:S(2)}) %collective-permute-start.6) | collective-permute-done | bytes 786464 | tf_op jit(solution)/shard_map/swap_copies/ppermute | solution.py:465
  64.3 0.2 unpack_sums.1
  64.6 0.6 collective-permute-start.9
  65.2 0.5 collective-permute-start.8
  65.7 1.3 %collective-permute-start.7 = (f32[2,896,128]{2,1,0:T(8,128)S(1)}, f32[2,896,128]{2,1,0:T(8,128)S(1)}, u32[]{:S(2)}, u32[]{:S(2)}) collective-permute-start(f32[2,896,128]{2,1,0:T(8,128)S(1)} %get-tuple-element.22.refs_0_), channel_id=1, source_target_pairs={{0,8},{1,25},{8,0},{9,17},{16,24},{17,9},{24,16},{25,1},{32,40},{3... | collective-permute-start | bytes 2752520 | tf_op jit(solution)/shard_map/quarters_along_x/ppermute | solution.py:471
  67.0 0.0 copy-done.2
  67.0 15.9 %factor_gram.1 = (f32[4,192,128]{2,1,0:T(8,128)S(1)}, f32[64,512]{1,0:T(8,128)}) custom-call(s32[6]{0:T(128)S(1)} %stack.27.place_ref, f32[640,128]{1,0:T(8,128)S(1)} %get-tuple-element.18.near_ref, f32[640,128]{1,0:T(8,128)S(1)} %get-tuple-element.19.far_ref, f32[128,512]{1,0:T(8,128)S(1)} %copy-done.2), custom_call_target="tpu_custom_call" | custom-call | flops 20000000000 | bytes 4000000 | tf_op jit(solution)/shard_map/factor_gram/pallas_call | solution.py:338
  82.9 0.0 collective-permute-done.9.refs_3_
  82.9 0.0 collective-permute-done.8.refs_2_
  82.9 0.0 collective-permute-done.7.refs_1_
  83.0 3.0 %apply_factor.1 = (f32[128,1792]{1,0:T(8,128)}, f32[64,1792]{1,0:T(8,128)}) custom-call(s32[6]{0:T(128)S(1)} %stack.27.place_ref, f32[4,192,128]{2,1,0:T(8,128)S(1)} %get-tuple-element.21.mixed_ref, f32[2,896,128]{2,1,0:T(8,128)S(1)} %get-tuple-element.22.refs_0_, f32[2,896,128]{2,1,0:T(8,128)S(1)} %collective-permute-done.7.refs_1_, ...), custom_call_target="tpu_custom_call" | custom-call | tf_op jit(solution)/shard_map/apply_factor/pallas_call | solution.py:390
Async XLA Ops:
  0.6 4.7 %copy-start = (f32[128,1792]{1,0:T(8,128)S(1)}, f32[128,1792]{1,0:T(8,128)}, u32[]{:S(2)}) copy-start(f32[128,1792]{1,0:T(8,128)} %refs_4_.1) | copy-start | bytes 2752516
  1.8 1.6 %copy-start.3 = (s32[128]{0:T(128)S(1)}, s32[128]{0:T(128)}, u32[]{:S(2)}) copy-start(s32[128]{0:T(128)} %param.5) | copy-start | bytes 1540
  1.8 3.5 %collective-permute-start.1 = (f32[128,896]{1,0:T(8,128)S(1)}, f32[128,896]{1,0:T(8,128)S(1)}, u32[]{:S(2)}, u32[]{:S(2)}) collective-permute-start(f32[128,896]{1,0:T(8,128)S(1)} %constant_dynamic-slice_fusion), channel_id=1, source_target_pairs={{0,1},{1,0},{2,3},{3,2},{4,5},{5,4},{6,7},{7,6},{8,9},{9,8},{10,11... | collective-permute-start | bytes 1376264 | tf_op jit(solution)/shard_map/swap_inputs/ppermute | solution.py:428
  3.3 2.0 %collective-permute-start = (f32[128,512]{1,0:T(8,128)}, f32[128,512]{1,0:T(8,128)S(1)}, u32[]{:S(2)}, u32[]{:S(2)}) collective-permute-start(f32[128,512]{1,0:T(8,128)} %panel_ref.3), channel_id=1, source_target_pairs={{0,1},{1,0},{2,3},{3,2},{4,5},{5,4},{6,7},{7,6},{8,9},{9,8},{10,11... | collective-permute-start | bytes 786440 | tf_op jit(solution)/shard_map/swap_inputs/ppermute | solution.py:427
  3.4 1.3 %collective-permute-start.2 = (s32[1,128]{1,0:T(1,128)S(1)}, s32[1,128]{1,0:T(1,128)S(1)}, u32[]{:S(2)}, u32[]{:S(2)}) collective-permute-start(s32[1,128]{1,0:T(1,128)S(1)} %bitcast.16), channel_id=1, source_target_pairs={{0,1},{1,0},{2,3},{3,2},{4,5},{5,4},{6,7},{7,6},{8,9},{9,8},{10,11... | collective-permute-start | bytes 1544 | tf_op jit(solution)/shard_map/swap_inputs/ppermute | solution.py:426
  5.3 1.0 %copy-start.1 = (f32[128,512]{1,0:T(8,128)S(1)}, f32[128,512]{1,0:T(8,128)}, u32[]{:S(2)}) copy-start(f32[128,512]{1,0:T(8,128)} %panel_ref.3) | copy-start | bytes 786436
  8.4 9.7 %collective-permute-start.3 = (f32[1088,128]{1,0:T(8,128)S(1)}, f32[1088,128]{1,0:T(8,128)S(1)}, u32[]{:S(2)}, u32[]{:S(2)}) collective-permute-start(f32[1088,128]{1,0:T(8,128)S(1)} %get-tuple-element.15), channel_id=1, source_target_pairs={{0,8},{1,25},{8,0},{9,17},{16,24},{17,9},{24,16},{25,1},{32,40},{3... | collective-permute-start | bytes 1671176 | tf_op jit(solution)/shard_map/terms_along_x/ppermute | solution.py:457
  11.1 9.7 %collective-permute-start.4 = (f32[1088,128]{1,0:T(8,128)S(1)}, f32[1088,128]{1,0:T(8,128)S(1)}, u32[]{:S(2)}, u32[]{:S(2)}) collective-permute-start(f32[1088,128]{1,0:T(8,128)S(1)} %get-tuple-element.16), channel_id=1, source_target_pairs={{0,32},{1,97},{8,40},{9,105},{16,48},{17,113},{24,56},{25,121},{32... | collective-permute-start | bytes 1671176 | tf_op jit(solution)/shard_map/terms_along_y/ppermute | solution.py:457
  13.8 10.7 %collective-permute-start.5 = (f32[1088,128]{1,0:T(8,128)S(1)}, f32[1088,128]{1,0:T(8,128)S(1)}, u32[]{:S(2)}, u32[]{:S(2)}) collective-permute-start(f32[1088,128]{1,0:T(8,128)S(1)} %get-tuple-element.17), channel_id=1, source_target_pairs={{0,2},{1,7},{2,0},{3,5},{4,6},{5,3},{6,4},{7,1},{8,10},{9,15},{10,... | collective-permute-start | bytes 1671176 | tf_op jit(solution)/shard_map/terms_along_z/ppermute | solution.py:457
  57.9 9.2 %copy-start.2 = (f32[128,512]{1,0:T(8,128)S(1)}, f32[128,512]{1,0:T(8,128)}, u32[]{:S(2)}) copy-start(f32[128,512]{1,0:T(8,128)} %panel_ref.3) | copy-start | bytes 786436
  57.9 6.4 %collective-permute-start.6 = (f32[1536,128]{1,0:T(8,128)S(1)}, f32[1536,128]{1,0:T(8,128)S(1)}, u32[]{:S(2)}, u32[]{:S(2)}) collective-permute-start(f32[1536,128]{1,0:T(8,128)S(1)} %bitcast.11), channel_id=1, source_target_pairs={{0,1},{1,0},{2,3},{3,2},{4,5},{5,4},{6,7},{7,6},{8,9},{9,8},{10,11... | collective-permute-start | bytes 2359304 | tf_op jit(solution)/shard_map/swap_copies/ppermute | solution.py:465
  64.6 18.4 %collective-permute-start.9 = (f32[2,896,128]{2,1,0:T(8,128)S(1)}, f32[2,896,128]{2,1,0:T(8,128)S(1)}, u32[]{:S(2)}, u32[]{:S(2)}) collective-permute-start(f32[2,896,128]{2,1,0:T(8,128)S(1)} %get-tuple-element.22.refs_0_), channel_id=1, source_target_pairs={{0,2},{1,7},{2,0},{3,5},{4,6},{5,3},{6,4},{7,1},{8,10},{9,15},{10,... | collective-permute-start | bytes 2752520 | tf_op jit(solution)/shard_map/quarters_along_z/ppermute | solution.py:471
  65.2 17.7 %collective-permute-start.8 = (f32[2,896,128]{2,1,0:T(8,128)S(1)}, f32[2,896,128]{2,1,0:T(8,128)S(1)}, u32[]{:S(2)}, u32[]{:S(2)}) collective-permute-start(f32[2,896,128]{2,1,0:T(8,128)S(1)} %get-tuple-element.22.refs_0_), channel_id=1, source_target_pairs={{0,32},{1,97},{8,40},{9,105},{16,48},{17,113},{24,56},{25,121},{32... | collective-permute-start | bytes 2752520 | tf_op jit(solution)/shard_map/quarters_along_y/ppermute | solution.py:471
  65.7 17.2 %collective-permute-start.7 = (f32[2,896,128]{2,1,0:T(8,128)S(1)}, f32[2,896,128]{2,1,0:T(8,128)S(1)}, u32[]{:S(2)}, u32[]{:S(2)}) collective-permute-start(f32[2,896,128]{2,1,0:T(8,128)S(1)} %get-tuple-element.22.refs_0_), channel_id=1, source_target_pairs={{0,8},{1,25},{8,0},{9,17},{16,24},{17,9},{24,16},{25,1},{32,40},{3... | collective-permute-start | bytes 2752520 | tf_op jit(solution)/shard_map/quarters_along_x/ppermute | solution.py:471

commit v8 on v7

--- a/solution.py
+++ b/solution.py
@@ -11,6 +11,7 @@
 HIGHEST = lax.Precision.HIGHEST
 tile = 128
 strip = 32
+half_strip = 16
 chips = ("grp", "z")
 classes = 4
 shares = (3, 3, 2, 2)
@@ -65,26 +66,37 @@
     for r in range(0, tile, strip):
         left = [work[r + 8 * g : r + 8 * g + 8, 0:tile] for g in range(groups)]
         right = [work[r + 8 * g : r + 8 * g + 8, tile : 2 * tile] for g in range(groups)]
+        pivots = [jnp.ones((8, tile), jnp.float32)] * groups
         if later:
             later.pop(0)()
-        col = {}
-        for c in range(strip):
-            for g in range(c // 8, groups):
-                col[c, g] = jnp.broadcast_to(left[g][:, r + c : r + c + 1], (8, tile))
-        for k in range(strip):
-            at, row = k // 8, k % 8
-            inv = lax.rsqrt(spread_row(col[k, at], row))
-            low = {g: col[k, g] * inv for g in range(at, groups)}
-            for c in range(k + 1, strip):
-                factor_c = spread_row(low[c // 8], c % 8)
+        for first in range(0, strip, half_strip):
+            col = {}
+            for c in range(first, first + half_strip):
                 for g in range(c // 8, groups):
-                    col[c, g] = col[c, g] - low[g] * factor_c
-            below = jnp.where(sub > row, low[at], 0.0)
-            for side in (left, right):
-                pivot = spread_row(side[at], row) * inv
-                side[at] = jnp.where(sub == row, pivot, side[at] - below * pivot)
-                for g in range(at + 1, groups):
-                    side[g] = side[g] - low[g] * pivot
+                    col[c, g] = jnp.broadcast_to(left[g][:, r + c : r + c + 1], (8, tile))
+            for k in range(first, first + half_strip):
+                at, row = k // 8, k % 8
+                pivot = spread_row(col[k, at], row)
+                inv = 1.0 / pivot
+                pivots[at] = jnp.where(sub == row, pivot, pivots[at])
+                low = {g: col[k, g] * inv for g in range(at, groups)}
+                for c in range(k + 1, first + half_strip):
+                    factor_c = spread_row(col[k, c // 8], c % 8)
+                    for g in range(c // 8, groups):
+                        if c == k + 1 and g == c // 8:
+                            col[c, g] = col[c, g] - (col[k, g] * factor_c) * inv
+                        else:
+                            col[c, g] = col[c, g] - low[g] * factor_c
+                below = jnp.where(sub > row, low[at], 0.0)
+                for side in (left, right):
+                    pivot_row = spread_row(side[at], row)
+                    side[at] = side[at] - below * pivot_row
+                    for g in range(at + 1, groups):
+                        side[g] = side[g] - low[g] * pivot_row
+        for g in range(groups):
+            scale = lax.rsqrt(pivots[g])
+            left[g] = left[g] * scale
+            right[g] = right[g] * scale
         new_left = jnp.concatenate(left, 0)
         new_right = jnp.concatenate(right, 0)
         work[r : r + strip, 0:tile] = new_left

time: 86.2 us -> 84.7 us (0.983)
  Pallas kernels: 21.6 us -> 20 us
    pallas_call x1, Pallas kernels: 15.9 us -> 14.3 us  [factor(): pl.pallas_call(factor_kernel, out_shape=(jax.ShapeDtypeStruct((width // t...]
  transfers between devices with their start and end apart: 10 -> 10, of which waited for: 6 -> 6; matrix products, arithmetic and copies ran while one was open for 0% -> 0% of each run, Pallas kernels for 18% -> 17%
where the time goes in v8:
time: 84.7 us; the launch traced here: 84.4 us
  blocking collectives  33.1 us (39%)
  Pallas kernels  20 us (24%)
  starting transfers between devices  18.2 us (21%)
  waiting for transfers between devices  10.2 us (12%)
  local copies, waits for them, and re-layouts  2.18 us (3%)
    all_to_all x2, blocking collectives, exchange(): lax.all_to_all(rows.reshape(chip_count, 1, -1), chips, 0, 0, tiled=True)  33.1 us
    pallas_call x1, Pallas kernels, factor(): pl.pallas_call(factor_kernel, out_shape=(jax.ShapeDtypeStruct((width // t...  14.3 us
    ppermute x3, starting transfers between devices, local(): parts.append(lax.ppermute(terms[1 + m], axis, pairs(before, after)))  9.13 us
    ppermute x3, waiting for transfers between devices, local(): parts.append(lax.ppermute(terms[1 + m], axis, pairs(before, after)))  6.92 us
    ppermute x1, starting transfers between devices, local(): far_copies = lax.ppermute(copies, 'core', swap)  4.53 us
    pallas_call x1, Pallas kernels, finish(): pl.pallas_call(finish_kernel, out_shape=(jax.ShapeDtypeStruct((own, trail...  3.01 us
    ppermute x3, starting transfers between devices, local(): quarters.append(lax.ppermute(quarter, axis, pairs(before, after)))  2.48 us
    pallas_call x1, Pallas kernels, products(): pl.pallas_call(functools.partial(products_kernel, total_rows=total_rows),...  2.15 us
  transfers between devices with their start and end apart: 10, of which 6 were waited for; matrix products, arithmetic and copies ran while one was open for 0% of the time, Pallas kernels for 17%

profile of v8, /device:TPU:1, one launch (start us, length us, event | category | flops | bytes accessed | tf_op | source)
XLA Modules:
  0.0 84.4 jit_solution(17550366654265543623)
XLA Ops:
  0.6 0.0 copy-start
  0.6 1.1 %constant_dynamic-slice_fusion = f32[128,896]{1,0:T(8,128)S(1)} fusion(f32[128,1792]{1,0:T(8,128)} %refs_4_.1, s32[]{:T(128)S(6)} %select_n.31), kind=kLoop, calls=%fused_computation | loop fusion | bytes 917508 | tf_op jit(solution)/shard_map/dynamic_slice | solution.py:436
  1.8 0.0 copy-start.3
  1.8 1.5 %collective-permute-start.1 = (f32[128,896]{1,0:T(8,128)S(1)}, f32[128,896]{1,0:T(8,128)S(1)}, u32[]{:S(2)}, u32[]{:S(2)}) collective-permute-start(f32[128,896]{1,0:T(8,128)S(1)} %constant_dynamic-slice_fusion), channel_id=1, source_target_pairs={{0,1},{1,0},{2,3},{3,2},{4,5},{5,4},{6,7},{7,6},{8,9},{9,8},{10,11... | collective-permute-start | bytes 1376264 | tf_op jit(solution)/shard_map/swap_inputs/ppermute | solution.py:440
  3.3 0.1 collective-permute-start
  3.4 0.0 copy-done.3
  3.4 0.5 collective-permute-start.2
  3.9 0.1 stack.27.place_ref
  3.9 0.8 collective-permute-done.2.far_counts_ref
  4.7 0.6 collective-permute-done.other_ref
  5.3 0.0 collective-permute-done.1.far_ref
  5.3 0.0 copy-done
  5.3 0.0 copy-start.1
  5.3 0.9 %copy-done.1 = f32[128,512]{1,0:T(8,128)S(1)} copy-done((f32[128,512]{1,0:T(8,128)S(1)}, f32[128,512]{1,0:T(8,128)}, u32[]{:S(2)}) %copy-start.1) | copy-done | bytes 262168
  6.3 2.2 %local_products.1 = (f32[1088,128]{1,0:T(8,128)S(1)}, f32[1088,128]{1,0:T(8,128)S(1)}, f32[1088,128]{1,0:T(8,128)S(1)}, f32[1088,128]{1,0:T(8,128)S(1)}) custom-call(s32[6]{0:T(128)S(1)} %stack.27.place_ref, f32[128,512]{1,0:T(8,128)S(1)} %copy-done.1, f32[128,512]{1,0:T(8,128)S(1)} %collective-permute-done.other_ref, f32[128,1792]{1,0:T(8,128)S(1)} %copy-done, ...), custom_call_target="tpu_custom_call" | custom-call | tf_op jit(solution)/shard_map/local_products/pallas_call | solution.py:164
  8.4 2.6 %collective-permute-start.3 = (f32[1088,128]{1,0:T(8,128)S(1)}, f32[1088,128]{1,0:T(8,128)S(1)}, u32[]{:S(2)}, u32[]{:S(2)}) collective-permute-start(f32[1088,128]{1,0:T(8,128)S(1)} %get-tuple-element.15), channel_id=1, source_target_pairs={{0,8},{1,25},{8,0},{9,17},{16,24},{17,9},{24,16},{25,1},{32,40},{3... | collective-permute-start | bytes 1671176 | tf_op jit(solution)/shard_map/terms_along_x/ppermute | solution.py:469
  11.1 2.7 %collective-permute-start.4 = (f32[1088,128]{1,0:T(8,128)S(1)}, f32[1088,128]{1,0:T(8,128)S(1)}, u32[]{:S(2)}, u32[]{:S(2)}) collective-permute-start(f32[1088,128]{1,0:T(8,128)S(1)} %get-tuple-element.16), channel_id=1, source_target_pairs={{0,32},{1,97},{8,40},{9,105},{16,48},{17,113},{24,56},{25,121},{32... | collective-permute-start | bytes 1671176 | tf_op jit(solution)/shard_map/terms_along_y/ppermute | solution.py:469
  13.8 3.8 %collective-permute-start.5 = (f32[1088,128]{1,0:T(8,128)S(1)}, f32[1088,128]{1,0:T(8,128)S(1)}, u32[]{:S(2)}, u32[]{:S(2)}) collective-permute-start(f32[1088,128]{1,0:T(8,128)S(1)} %get-tuple-element.17), channel_id=1, source_target_pairs={{0,2},{1,7},{2,0},{3,5},{4,6},{5,3},{6,4},{7,1},{8,10},{9,15},{10,... | collective-permute-start | bytes 1671176 | tf_op jit(solution)/shard_map/terms_along_z/ppermute | solution.py:469
  17.6 0.5 collective-permute-done.3.refs_1_
  18.1 2.6 %collective-permute-done.4.refs_2_ = f32[1088,128]{1,0:T(8,128)S(1)} collective-permute-done((f32[1088,128]{1,0:T(8,128)S(1)}, f32[1088,128]{1,0:T(8,128)S(1)}, u32[]{:S(2)}, u32[]{:S(2)}) %collective-permute-start.4) | collective-permute-done | bytes 557088 | tf_op jit(solution)/shard_map/terms_along_y/ppermute | solution.py:469
  20.7 3.8 %collective-permute-done.5.refs_3_ = f32[1088,128]{1,0:T(8,128)S(1)} collective-permute-done((f32[1088,128]{1,0:T(8,128)S(1)}, f32[1088,128]{1,0:T(8,128)S(1)}, u32[]{:S(2)}, u32[]{:S(2)}) %collective-permute-start.5) | collective-permute-done | bytes 557088 | tf_op jit(solution)/shard_map/terms_along_z/ppermute | solution.py:469
  24.5 0.2 combine_terms.1
  24.7 16.1 %all_to_all.10 = f32[64,1,2176]{2,1,0:T(1,128)S(1)} all-to-all(f32[64,1,2176]{2,1,0:T(1,128)S(1)} %bitcast.14), channel_id=1, replica_groups=mesh['grp'=16,'z'=4,'core'=2] {'grp','z'}, dimensions={0} | all-to-all | bytes 1114112 | tf_op jit(solution)/shard_map/exchange/all_to_all | solution.py:463
  40.8 0.1 sum_pieces.1
  40.9 17.0 %all_to_all.11 = f32[64,1,3072]{2,1,0:T(1,128)S(1)} all-to-all(f32[64,1,3072]{2,1,0:T(1,128)S(1)} %bitcast.13), channel_id=1, replica_groups=mesh['grp'=16,'z'=4,'core'=2] {'grp','z'}, dimensions={0} | all-to-all | bytes 1572864 | tf_op jit(solution)/shard_map/exchange/all_to_all | solution.py:463
  57.9 0.0 copy-start.2
  57.9 4.5 %collective-permute-start.6 = (f32[1536,128]{1,0:T(8,128)S(1)}, f32[1536,128]{1,0:T(8,128)S(1)}, u32[]{:S(2)}, u32[]{:S(2)}) collective-permute-start(f32[1536,128]{1,0:T(8,128)S(1)} %bitcast.11), channel_id=1, source_target_pairs={{0,1},{1,0},{2,3},{3,2},{4,5},{5,4},{6,7},{7,6},{8,9},{9,8},{10,11... | collective-permute-start | bytes 2359304 | tf_op jit(solution)/shard_map/swap_copies/ppermute | solution.py:477
  62.4 1.9 %collective-permute-done.6.far_ref = f32[1536,128]{1,0:T(8,128)S(1)} collective-permute-done((f32[1536,128]{1,0:T(8,128)S(1)}, f32[1536,128]{1,0:T(8,128)S(1)}, u32[]{:S(2)}, u32[]{:S(2)}) %collective-permute-start.6) | collective-permute-done | bytes 786464 | tf_op jit(solution)/shard_map/swap_copies/ppermute | solution.py:477
  64.3 0.2 unpack_sums.1
  64.6 0.6 collective-permute-start.9
  65.2 0.5 collective-permute-start.8
  65.7 1.3 %collective-permute-start.7 = (f32[2,896,128]{2,1,0:T(8,128)S(1)}, f32[2,896,128]{2,1,0:T(8,128)S(1)}, u32[]{:S(2)}, u32[]{:S(2)}) collective-permute-start(f32[2,896,128]{2,1,0:T(8,128)S(1)} %get-tuple-element.22.refs_0_), channel_id=1, source_target_pairs={{0,8},{1,25},{8,0},{9,17},{16,24},{17,9},{24,16},{25,1},{32,40},{3... | collective-permute-start | bytes 2752520 | tf_op jit(solution)/shard_map/quarters_along_x/ppermute | solution.py:483
  67.0 0.0 copy-done.2
  67.0 14.3 %factor_gram.1 = (f32[4,192,128]{2,1,0:T(8,128)S(1)}, f32[64,512]{1,0:T(8,128)}) custom-call(s32[6]{0:T(128)S(1)} %stack.27.place_ref, f32[640,128]{1,0:T(8,128)S(1)} %get-tuple-element.18.near_ref, f32[640,128]{1,0:T(8,128)S(1)} %get-tuple-element.19.far_ref, f32[128,512]{1,0:T(8,128)S(1)} %copy-done.2), custom_call_target="tpu_custom_call" | custom-call | flops 20000000000 | bytes 4000000 | tf_op jit(solution)/shard_map/factor_gram/pallas_call | solution.py:350
  81.4 0.0 collective-permute-done.9.refs_3_
  81.4 0.0 collective-permute-done.8.refs_2_
  81.4 0.0 collective-permute-done.7.refs_1_
  81.4 3.0 %apply_factor.1 = (f32[128,1792]{1,0:T(8,128)}, f32[64,1792]{1,0:T(8,128)}) custom-call(s32[6]{0:T(128)S(1)} %stack.27.place_ref, f32[4,192,128]{2,1,0:T(8,128)S(1)} %get-tuple-element.21.mixed_ref, f32[2,896,128]{2,1,0:T(8,128)S(1)} %get-tuple-element.22.refs_0_, f32[2,896,128]{2,1,0:T(8,128)S(1)} %collective-permute-done.7.refs_1_, ...), custom_call_target="tpu_custom_call" | custom-call | tf_op jit(solution)/shard_map/apply_factor/pallas_call | solution.py:402
Async XLA Ops:
  0.6 4.7 %copy-start = (f32[128,1792]{1,0:T(8,128)S(1)}, f32[128,1792]{1,0:T(8,128)}, u32[]{:S(2)}) copy-start(f32[128,1792]{1,0:T(8,128)} %refs_4_.1) | copy-start | bytes 2752516
  1.8 1.6 %copy-start.3 = (s32[128]{0:T(128)S(1)}, s32[128]{0:T(128)}, u32[]{:S(2)}) copy-start(s32[128]{0:T(128)} %param.5) | copy-start | bytes 1540
  1.8 3.5 %collective-permute-start.1 = (f32[128,896]{1,0:T(8,128)S(1)}, f32[128,896]{1,0:T(8,128)S(1)}, u32[]{:S(2)}, u32[]{:S(2)}) collective-permute-start(f32[128,896]{1,0:T(8,128)S(1)} %constant_dynamic-slice_fusion), channel_id=1, source_target_pairs={{0,1},{1,0},{2,3},{3,2},{4,5},{5,4},{6,7},{7,6},{8,9},{9,8},{10,11... | collective-permute-start | bytes 1376264 | tf_op jit(solution)/shard_map/swap_inputs/ppermute | solution.py:440
  3.3 2.0 %collective-permute-start = (f32[128,512]{1,0:T(8,128)}, f32[128,512]{1,0:T(8,128)S(1)}, u32[]{:S(2)}, u32[]{:S(2)}) collective-permute-start(f32[128,512]{1,0:T(8,128)} %panel_ref.3), channel_id=1, source_target_pairs={{0,1},{1,0},{2,3},{3,2},{4,5},{5,4},{6,7},{7,6},{8,9},{9,8},{10,11... | collective-permute-start | bytes 786440 | tf_op jit(solution)/shard_map/swap_inputs/ppermute | solution.py:439
  3.4 1.3 %collective-permute-start.2 = (s32[1,128]{1,0:T(1,128)S(1)}, s32[1,128]{1,0:T(1,128)S(1)}, u32[]{:S(2)}, u32[]{:S(2)}) collective-permute-start(s32[1,128]{1,0:T(1,128)S(1)} %bitcast.16), channel_id=1, source_target_pairs={{0,1},{1,0},{2,3},{3,2},{4,5},{5,4},{6,7},{7,6},{8,9},{9,8},{10,11... | collective-permute-start | bytes 1544 | tf_op jit(solution)/shard_map/swap_inputs/ppermute | solution.py:438
  5.3 1.0 %copy-start.1 = (f32[128,512]{1,0:T(8,128)S(1)}, f32[128,512]{1,0:T(8,128)}, u32[]{:S(2)}) copy-start(f32[128,512]{1,0:T(8,128)} %panel_ref.3) | copy-start | bytes 786436
  8.4 9.7 %collective-permute-start.3 = (f32[1088,128]{1,0:T(8,128)S(1)}, f32[1088,128]{1,0:T(8,128)S(1)}, u32[]{:S(2)}, u32[]{:S(2)}) collective-permute-start(f32[1088,128]{1,0:T(8,128)S(1)} %get-tuple-element.15), channel_id=1, source_target_pairs={{0,8},{1,25},{8,0},{9,17},{16,24},{17,9},{24,16},{25,1},{32,40},{3... | collective-permute-start | bytes 1671176 | tf_op jit(solution)/shard_map/terms_along_x/ppermute | solution.py:469
  11.1 9.7 %collective-permute-start.4 = (f32[1088,128]{1,0:T(8,128)S(1)}, f32[1088,128]{1,0:T(8,128)S(1)}, u32[]{:S(2)}, u32[]{:S(2)}) collective-permute-start(f32[1088,128]{1,0:T(8,128)S(1)} %get-tuple-element.16), channel_id=1, source_target_pairs={{0,32},{1,97},{8,40},{9,105},{16,48},{17,113},{24,56},{25,121},{32... | collective-permute-start | bytes 1671176 | tf_op jit(solution)/shard_map/terms_along_y/ppermute | solution.py:469
  13.8 10.7 %collective-permute-start.5 = (f32[1088,128]{1,0:T(8,128)S(1)}, f32[1088,128]{1,0:T(8,128)S(1)}, u32[]{:S(2)}, u32[]{:S(2)}) collective-permute-start(f32[1088,128]{1,0:T(8,128)S(1)} %get-tuple-element.17), channel_id=1, source_target_pairs={{0,2},{1,7},{2,0},{3,5},{4,6},{5,3},{6,4},{7,1},{8,10},{9,15},{10,... | collective-permute-start | bytes 1671176 | tf_op jit(solution)/shard_map/terms_along_z/ppermute | solution.py:469
  57.9 9.2 %copy-start.2 = (f32[128,512]{1,0:T(8,128)S(1)}, f32[128,512]{1,0:T(8,128)}, u32[]{:S(2)}) copy-start(f32[128,512]{1,0:T(8,128)} %panel_ref.3) | copy-start | bytes 786436
  57.9 6.4 %collective-permute-start.6 = (f32[1536,128]{1,0:T(8,128)S(1)}, f32[1536,128]{1,0:T(8,128)S(1)}, u32[]{:S(2)}, u32[]{:S(2)}) collective-permute-start(f32[1536,128]{1,0:T(8,128)S(1)} %bitcast.11), channel_id=1, source_target_pairs={{0,1},{1,0},{2,3},{3,2},{4,5},{5,4},{6,7},{7,6},{8,9},{9,8},{10,11... | collective-permute-start | bytes 2359304 | tf_op jit(solution)/shard_map/swap_copies/ppermute | solution.py:477
  64.6 16.8 %collective-permute-start.9 = (f32[2,896,128]{2,1,0:T(8,128)S(1)}, f32[2,896,128]{2,1,0:T(8,128)S(1)}, u32[]{:S(2)}, u32[]{:S(2)}) collective-permute-start(f32[2,896,128]{2,1,0:T(8,128)S(1)} %get-tuple-element.22.refs_0_), channel_id=1, source_target_pairs={{0,2},{1,7},{2,0},{3,5},{4,6},{5,3},{6,4},{7,1},{8,10},{9,15},{10,... | collective-permute-start | bytes 2752520 | tf_op jit(solution)/shard_map/quarters_along_z/ppermute | solution.py:483
  65.2 16.2 %collective-permute-start.8 = (f32[2,896,128]{2,1,0:T(8,128)S(1)}, f32[2,896,128]{2,1,0:T(8,128)S(1)}, u32[]{:S(2)}, u32[]{:S(2)}) collective-permute-start(f32[2,896,128]{2,1,0:T(8,128)S(1)} %get-tuple-element.22.refs_0_), channel_id=1, source_target_pairs={{0,32},{1,97},{8,40},{9,105},{16,48},{17,113},{24,56},{25,121},{32... | collective-permute-start | bytes 2752520 | tf_op jit(solution)/shard_map/quarters_along_y/ppermute | solution.py:483
  65.7 15.7 %collective-permute-start.7 = (f32[2,896,128]{2,1,0:T(8,128)S(1)}, f32[2,896,128]{2,1,0:T(8,128)S(1)}, u32[]{:S(2)}, u32[]{:S(2)}) collective-permute-start(f32[2,896,128]{2,1,0:T(8,128)S(1)} %get-tuple-element.22.refs_0_), channel_id=1, source_target_pairs={{0,8},{1,25},{8,0},{9,17},{16,24},{17,9},{24,16},{25,1},{32,40},{3... | collective-permute-start | bytes 2752520 | tf_op jit(solution)/shard_map/quarters_along_x/ppermute | solution.py:483

commit v9 on v8

--- a/solution.py
+++ b/solution.py
@@ -109,19 +109,52 @@
 gram_blocks = (((0, 0), (1, 1), (0, 1), (0, 2), (0, 3)), ((2, 2), (3, 3), (2, 3), (1, 2), (1, 3)))
 
 
-def products_kernel(place_ref, panel_ref, other_ref, trail_ref, far_ref, counts_ref, far_counts_ref, *refs, total_rows):
+def weigh(rows, trail, count, total_rows, at, pt, wp, wt):
+    own, width = rows.shape
+    weight = jnp.transpose(jnp.broadcast_to(count[...].astype(jnp.float32) / total_rows, (own, own)))
+    for c in range(0, width, tile):
+        block = rows[:, c : c + tile]
+        pt[c : c + tile, at : at + own] = jnp.transpose(block)
+        wp[at : at + own, c : c + tile] = block * weight
+    for c in range(0, trail.shape[1], tile):
+        wt[at : at + own, c : c + tile] = trail[:, c : c + tile] * weight
+
+
+def prepare_kernel(place_ref, panel_ref, trail_ref, counts_ref, pt, wp, wt, *, total_rows):
+    weigh(panel_ref, trail_ref, counts_ref, total_rows, 0, pt, wp, wt)
+
+
+def prepare(place, panel, trailing, counts, total_rows):
+    own, width = panel.shape
+    half = trailing.shape[1] // 2
+    whole = lambda shape: pl.BlockSpec(shape, lambda i, place: (0, 0))
+    shapes = [(width, own), (own, width), (own, half)]
+    return pl.pallas_call(
+        functools.partial(prepare_kernel, total_rows=total_rows),
+        out_shape=[jax.ShapeDtypeStruct(shape, jnp.float32) for shape in shapes],
+        grid_spec=pltpu.PrefetchScalarGridSpec(
+            num_scalar_prefetch=1,
+            grid=(1,),
+            in_specs=[
+                whole((own, width)),
+                pl.BlockSpec((own, half), lambda i, place: (0, place[0])),
+                whole((1, own)),
+            ],
+            out_specs=[whole(shape) for shape in shapes],
+        ),
+        compiler_params=pltpu.CompilerParams(vmem_limit_bytes=16 * 1024 * 1024),
+    )(place, panel, trailing, counts)
+
+
+def products_kernel(place_ref, own_pt, own_wp, own_wt, other_ref, far_ref, far_counts_ref, *refs, total_rows):
     outs, (pt, wp, wt, quarters, gram, shared) = refs[:classes], refs[classes:]
     core = place_ref[0]
-    own, width = panel_ref.shape
-    half = trail_ref.shape[1]
-    for at, rows, trail, count in ((0, panel_ref, trail_ref, counts_ref), (own, other_ref, far_ref, far_counts_ref)):
-        weight = jnp.transpose(jnp.broadcast_to(count[...].astype(jnp.float32) / total_rows, (own, own)))
-        for c in range(0, width, tile):
-            block = rows[:, c : c + tile]
-            pt[c : c + tile, at : at + own] = jnp.transpose(block)
-            wp[at : at + own, c : c + tile] = block * weight
-        for c in range(0, half, tile):
-            wt[at : at + own, c : c + tile] = trail[:, c : c + tile] * weight
+    own = other_ref.shape[0]
+    half = far_ref.shape[1]
+    pt[:, 0:own] = own_pt[...]
+    wp[0:own, :] = own_wp[...]
+    wt[0:own, :] = own_wt[...]
+    weigh(other_ref, far_ref, far_counts_ref, total_rows, own, pt, wp, wt)
     step = 2 * tile
     for c in range(0, half, step):
         n = min(step, half - c)
@@ -155,8 +188,8 @@
         outs[m][half:, :] = shared[place_ref[1 + m]]
 
 
-def products(place, panel, other, trailing, far, counts, far_counts, chip_count, total_rows):
-    own, width = panel.shape
+def products(place, prepared, other, far, far_counts, chip_count, total_rows):
+    own, width = other.shape
     half = far.shape[1]
     gram_rows = len(gram_blocks[0]) * tile
     sent_rows = half + max(shares) * chip_count
@@ -168,11 +201,11 @@
             num_scalar_prefetch=1,
             grid=(1,),
             in_specs=[
+                whole((width, own)),
                 whole((own, width)),
+                whole((own, half)),
                 whole((own, width)),
-                pl.BlockSpec((own, half), lambda i, place: (0, place[0])),
                 whole((own, half)),
-                whole((1, own)),
                 whole((1, own)),
             ],
             out_specs=[whole((sent_rows, tile))] * classes,
@@ -186,7 +219,7 @@
             ],
         ),
         compiler_params=pltpu.CompilerParams(vmem_limit_bytes=32 * 1024 * 1024),
-    )(place, panel, other, trailing, far, counts, far_counts)
+    )(place, *prepared, other, far, far_counts)
 
 
 def combine_kernel(*refs, chip_count, chunk):
@@ -438,10 +471,10 @@
         far_counts = lax.ppermute(count_row, "core", swap)
         other_panel = lax.ppermute(panel, "core", swap)
         far_trail = lax.ppermute(sent_trail, "core", swap)
+    with jax.named_scope("own_operands"):
+        prepared = prepare(place, panel, trailing, count_row, own * groups * members)
     with jax.named_scope("local_products"):
-        terms = products(
-            place, panel, other_panel, trailing, far_trail, count_row, far_counts, chip_count, own * groups * members
-        )
+        terms = products(place, prepared, other_panel, far_trail, far_counts, chip_count, own * groups * members)
     def pairs(before, after):
         out = []
         for a in range(before):

time: 84.7 us -> 84 us (level)
  waiting for transfers between devices: 10.2 us -> 8.85 us
  transfers between devices with their start and end apart: 10 -> 10, of which waited for: 6 -> 4; matrix products, arithmetic and copies ran while one was open for 0% -> 0% of each run, Pallas kernels for 17% -> 18%
where the time goes in v9:
time: 84 us; the launch traced here: 83.7 us
  blocking collectives  33.1 us (39%)
  Pallas kernels  20.7 us (25%)
  starting transfers between devices  18.1 us (22%)
  waiting for transfers between devices  8.85 us (11%)
  local copies, waits for them, and re-layouts  2.18 us (3%)
    all_to_all x2, blocking collectives, exchange(): lax.all_to_all(rows.reshape(chip_count, 1, -1), chips, 0, 0, tiled=True)  33.1 us
    pallas_call x1, Pallas kernels, factor(): pl.pallas_call(factor_kernel, out_shape=(jax.ShapeDtypeStruct((width // t...  14.3 us
    ppermute x3, starting transfers between devices, local(): parts.append(lax.ppermute(terms[1 + m], axis, pairs(before, after)))  9.13 us
    ppermute x3, waiting for transfers between devices, local(): parts.append(lax.ppermute(terms[1 + m], axis, pairs(before, after)))  6.92 us
    ppermute x1, starting transfers between devices, local(): far_copies = lax.ppermute(copies, 'core', swap)  4.51 us
    pallas_call x1, Pallas kernels, finish(): pl.pallas_call(finish_kernel, out_shape=(jax.ShapeDtypeStruct((own, trail...  3.01 us
    ppermute x3, starting transfers between devices, local(): quarters.append(lax.ppermute(quarter, axis, pairs(before, after)))  2.37 us
    pallas_call x1, Pallas kernels, products(): pl.pallas_call(functools.partial(products_kernel, total_rows=total_rows),...  2.15 us
  transfers between devices with their start and end apart: 10, of which 4 were waited for; matrix products, arithmetic and copies ran while one was open for 0% of the time, Pallas kernels for 18%

profile of v9, /device:TPU:1, one launch (start us, length us, event | category | flops | bytes accessed | tf_op | source)
XLA Modules:
  0.0 83.7 jit_solution(4946062249734308967)
XLA Ops:
  0.6 0.0 copy-start
  0.6 1.1 %constant_dynamic-slice_fusion = f32[128,896]{1,0:T(8,128)S(1)} fusion(f32[128,1792]{1,0:T(8,128)} %refs_4_.1, s32[]{:T(128)S(6)} %select_n.31), kind=kLoop, calls=%fused_computation | loop fusion | bytes 917508 | tf_op jit(solution)/shard_map/dynamic_slice | solution.py:469
  1.8 0.0 copy-start.3
  1.8 1.5 %collective-permute-start.1 = (f32[128,896]{1,0:T(8,128)S(1)}, f32[128,896]{1,0:T(8,128)S(1)}, u32[]{:S(2)}, u32[]{:S(2)}) collective-permute-start(f32[128,896]{1,0:T(8,128)S(1)} %constant_dynamic-slice_fusion), channel_id=1, source_target_pairs={{0,1},{1,0},{2,3},{3,2},{4,5},{5,4},{6,7},{7,6},{8,9},{9,8},{10,11... | collective-permute-start | bytes 1376264 | tf_op jit(solution)/shard_map/swap_inputs/ppermute | solution.py:473
  3.3 0.1 collective-permute-start
  3.4 0.0 copy-done.3
  3.4 0.5 collective-permute-start.2
  3.9 0.1 stack.27.place_ref
  3.9 0.0 copy-done
  3.9 0.0 copy-start.1
  4.0 1.0 %copy-done.1 = f32[128,512]{1,0:T(8,128)S(1)} copy-done((f32[128,512]{1,0:T(8,128)S(1)}, f32[128,512]{1,0:T(8,128)}, u32[]{:S(2)}) %copy-start.1) | copy-done | bytes 262168
  4.9 0.7 own_operands.1
  5.6 0.0 collective-permute-done.2.far_counts_ref
  5.6 0.0 collective-permute-done.other_ref
  5.6 0.0 collective-permute-done.1.far_ref
  5.6 2.2 %local_products.1 = (f32[1088,128]{1,0:T(8,128)S(1)}, f32[1088,128]{1,0:T(8,128)S(1)}, f32[1088,128]{1,0:T(8,128)S(1)}, f32[1088,128]{1,0:T(8,128)S(1)}) custom-call(s32[6]{0:T(128)S(1)} %stack.27.place_ref, f32[512,128]{1,0:T(8,128)S(1)} %get-tuple-element.17.own_pt, f32[128,512]{1,0:T(8,128)S(1)} %get-tuple-element.18.own_wp, ...), custom_call_target="tpu_custom_call" | custom-call | tf_op jit(solution)/shard_map/local_products/pallas_call | solution.py:197
  7.8 2.6 %collective-permute-start.3 = (f32[1088,128]{1,0:T(8,128)S(1)}, f32[1088,128]{1,0:T(8,128)S(1)}, u32[]{:S(2)}, u32[]{:S(2)}) collective-permute-start(f32[1088,128]{1,0:T(8,128)S(1)} %get-tuple-element.21), channel_id=1, source_target_pairs={{0,8},{1,25},{8,0},{9,17},{16,24},{17,9},{24,16},{25,1},{32,40},{3... | collective-permute-start | bytes 1671176 | tf_op jit(solution)/shard_map/terms_along_x/ppermute | solution.py:502
  10.4 2.7 %collective-permute-start.4 = (f32[1088,128]{1,0:T(8,128)S(1)}, f32[1088,128]{1,0:T(8,128)S(1)}, u32[]{:S(2)}, u32[]{:S(2)}) collective-permute-start(f32[1088,128]{1,0:T(8,128)S(1)} %get-tuple-element.22), channel_id=1, source_target_pairs={{0,32},{1,97},{8,40},{9,105},{16,48},{17,113},{24,56},{25,121},{32... | collective-permute-start | bytes 1671176 | tf_op jit(solution)/shard_map/terms_along_y/ppermute | solution.py:502
  13.2 3.8 %collective-permute-start.5 = (f32[1088,128]{1,0:T(8,128)S(1)}, f32[1088,128]{1,0:T(8,128)S(1)}, u32[]{:S(2)}, u32[]{:S(2)}) collective-permute-start(f32[1088,128]{1,0:T(8,128)S(1)} %get-tuple-element.23), channel_id=1, source_target_pairs={{0,2},{1,7},{2,0},{3,5},{4,6},{5,3},{6,4},{7,1},{8,10},{9,15},{10,... | collective-permute-start | bytes 1671176 | tf_op jit(solution)/shard_map/terms_along_z/ppermute | solution.py:502
  16.9 0.5 collective-permute-done.3.refs_1_
  17.5 2.6 %collective-permute-done.4.refs_2_ = f32[1088,128]{1,0:T(8,128)S(1)} collective-permute-done((f32[1088,128]{1,0:T(8,128)S(1)}, f32[1088,128]{1,0:T(8,128)S(1)}, u32[]{:S(2)}, u32[]{:S(2)}) %collective-permute-start.4) | collective-permute-done | bytes 557088 | tf_op jit(solution)/shard_map/terms_along_y/ppermute | solution.py:502
  20.1 3.8 %collective-permute-done.5.refs_3_ = f32[1088,128]{1,0:T(8,128)S(1)} collective-permute-done((f32[1088,128]{1,0:T(8,128)S(1)}, f32[1088,128]{1,0:T(8,128)S(1)}, u32[]{:S(2)}, u32[]{:S(2)}) %collective-permute-start.5) | collective-permute-done | bytes 557088 | tf_op jit(solution)/shard_map/terms_along_z/ppermute | solution.py:502
  23.9 0.2 combine_terms.1
  24.1 16.3 %all_to_all.10 = f32[64,1,2176]{2,1,0:T(1,128)S(1)} all-to-all(f32[64,1,2176]{2,1,0:T(1,128)S(1)} %bitcast.14), channel_id=1, replica_groups=mesh['grp'=16,'z'=4,'core'=2] {'grp','z'}, dimensions={0} | all-to-all | bytes 1114112 | tf_op jit(solution)/shard_map/exchange/all_to_all | solution.py:496
  40.3 0.1 sum_pieces.1
  40.4 16.9 %all_to_all.11 = f32[64,1,3072]{2,1,0:T(1,128)S(1)} all-to-all(f32[64,1,3072]{2,1,0:T(1,128)S(1)} %bitcast.13), channel_id=1, replica_groups=mesh['grp'=16,'z'=4,'core'=2] {'grp','z'}, dimensions={0} | all-to-all | bytes 1572864 | tf_op jit(solution)/shard_map/exchange/all_to_all | solution.py:496
  57.3 0.0 copy-start.2
  57.3 4.5 %collective-permute-start.6 = (f32[1536,128]{1,0:T(8,128)S(1)}, f32[1536,128]{1,0:T(8,128)S(1)}, u32[]{:S(2)}, u32[]{:S(2)}) collective-permute-start(f32[1536,128]{1,0:T(8,128)S(1)} %bitcast.11), channel_id=1, source_target_pairs={{0,1},{1,0},{2,3},{3,2},{4,5},{5,4},{6,7},{7,6},{8,9},{9,8},{10,11... | collective-permute-start | bytes 2359304 | tf_op jit(solution)/shard_map/swap_copies/ppermute | solution.py:510
  61.8 1.9 %collective-permute-done.6.far_ref = f32[1536,128]{1,0:T(8,128)S(1)} collective-permute-done((f32[1536,128]{1,0:T(8,128)S(1)}, f32[1536,128]{1,0:T(8,128)S(1)}, u32[]{:S(2)}, u32[]{:S(2)}) %collective-permute-start.6) | collective-permute-done | bytes 786464 | tf_op jit(solution)/shard_map/swap_copies/ppermute | solution.py:510
  63.7 0.2 unpack_sums.1
  64.0 0.3 collective-permute-start.9
  64.2 0.8 collective-permute-start.8
  65.0 1.3 %collective-permute-start.7 = (f32[2,896,128]{2,1,0:T(8,128)S(1)}, f32[2,896,128]{2,1,0:T(8,128)S(1)}, u32[]{:S(2)}, u32[]{:S(2)}) collective-permute-start(f32[2,896,128]{2,1,0:T(8,128)S(1)} %get-tuple-element.28.refs_0_), channel_id=1, source_target_pairs={{0,8},{1,25},{8,0},{9,17},{16,24},{17,9},{24,16},{25,1},{32,40},{3... | collective-permute-start | bytes 2752520 | tf_op jit(solution)/shard_map/quarters_along_x/ppermute | solution.py:516
  66.4 0.0 copy-done.2
  66.4 14.3 %factor_gram.1 = (f32[4,192,128]{2,1,0:T(8,128)S(1)}, f32[64,512]{1,0:T(8,128)}) custom-call(s32[6]{0:T(128)S(1)} %stack.27.place_ref, f32[640,128]{1,0:T(8,128)S(1)} %get-tuple-element.24.near_ref, f32[640,128]{1,0:T(8,128)S(1)} %get-tuple-element.25.far_ref, f32[128,512]{1,0:T(8,128)S(1)} %copy-done.2), custom_call_target="tpu_custom_call" | custom-call | flops 20000000000 | bytes 4000000 | tf_op jit(solution)/shard_map/factor_gram/pallas_call | solution.py:383
  80.7 0.0 collective-permute-done.9.refs_3_
  80.7 0.0 collective-permute-done.8.refs_2_
  80.7 0.0 collective-permute-done.7.refs_1_
  80.7 3.0 %apply_factor.1 = (f32[128,1792]{1,0:T(8,128)}, f32[64,1792]{1,0:T(8,128)}) custom-call(s32[6]{0:T(128)S(1)} %stack.27.place_ref, f32[4,192,128]{2,1,0:T(8,128)S(1)} %get-tuple-element.27.mixed_ref, f32[2,896,128]{2,1,0:T(8,128)S(1)} %get-tuple-element.28.refs_0_, f32[2,896,128]{2,1,0:T(8,128)S(1)} %collective-permute-done.7.refs_1_, ...), custom_call_target="tpu_custom_call" | custom-call | tf_op jit(solution)/shard_map/apply_factor/pallas_call | solution.py:435
Async XLA Ops:
  0.6 3.3 %copy-start = (f32[128,1792]{1,0:T(8,128)S(1)}, f32[128,1792]{1,0:T(8,128)}, u32[]{:S(2)}) copy-start(f32[128,1792]{1,0:T(8,128)} %refs_4_.1) | copy-start | bytes 2752516
  1.8 1.6 %copy-start.3 = (s32[128]{0:T(128)S(1)}, s32[128]{0:T(128)}, u32[]{:S(2)}) copy-start(s32[128]{0:T(128)} %param.5) | copy-start | bytes 1540
  1.8 3.8 %collective-permute-start.1 = (f32[128,896]{1,0:T(8,128)S(1)}, f32[128,896]{1,0:T(8,128)S(1)}, u32[]{:S(2)}, u32[]{:S(2)}) collective-permute-start(f32[128,896]{1,0:T(8,128)S(1)} %constant_dynamic-slice_fusion), channel_id=1, source_target_pairs={{0,1},{1,0},{2,3},{3,2},{4,5},{5,4},{6,7},{7,6},{8,9},{9,8},{10,11... | collective-permute-start | bytes 1376264 | tf_op jit(solution)/shard_map/swap_inputs/ppermute | solution.py:473
  3.3 2.3 %collective-permute-start = (f32[128,512]{1,0:T(8,128)}, f32[128,512]{1,0:T(8,128)S(1)}, u32[]{:S(2)}, u32[]{:S(2)}) collective-permute-start(f32[128,512]{1,0:T(8,128)} %panel_ref.3), channel_id=1, source_target_pairs={{0,1},{1,0},{2,3},{3,2},{4,5},{5,4},{6,7},{7,6},{8,9},{9,8},{10,11... | collective-permute-start | bytes 786440 | tf_op jit(solution)/shard_map/swap_inputs/ppermute | solution.py:472
  3.4 2.2 %collective-permute-start.2 = (s32[1,128]{1,0:T(1,128)S(1)}, s32[1,128]{1,0:T(1,128)S(1)}, u32[]{:S(2)}, u32[]{:S(2)}) collective-permute-start(s32[1,128]{1,0:T(1,128)S(1)} %bitcast.16), channel_id=1, source_target_pairs={{0,1},{1,0},{2,3},{3,2},{4,5},{5,4},{6,7},{7,6},{8,9},{9,8},{10,11... | collective-permute-start | bytes 1544 | tf_op jit(solution)/shard_map/swap_inputs/ppermute | solution.py:471
  3.9 1.0 %copy-start.1 = (f32[128,512]{1,0:T(8,128)S(1)}, f32[128,512]{1,0:T(8,128)}, u32[]{:S(2)}) copy-start(f32[128,512]{1,0:T(8,128)} %panel_ref.3) | copy-start | bytes 786436
  7.8 9.7 %collective-permute-start.3 = (f32[1088,128]{1,0:T(8,128)S(1)}, f32[1088,128]{1,0:T(8,128)S(1)}, u32[]{:S(2)}, u32[]{:S(2)}) collective-permute-start(f32[1088,128]{1,0:T(8,128)S(1)} %get-tuple-element.21), channel_id=1, source_target_pairs={{0,8},{1,25},{8,0},{9,17},{16,24},{17,9},{24,16},{25,1},{32,40},{3... | collective-permute-start | bytes 1671176 | tf_op jit(solution)/shard_map/terms_along_x/ppermute | solution.py:502
  10.4 9.7 %collective-permute-start.4 = (f32[1088,128]{1,0:T(8,128)S(1)}, f32[1088,128]{1,0:T(8,128)S(1)}, u32[]{:S(2)}, u32[]{:S(2)}) collective-permute-start(f32[1088,128]{1,0:T(8,128)S(1)} %get-tuple-element.22), channel_id=1, source_target_pairs={{0,32},{1,97},{8,40},{9,105},{16,48},{17,113},{24,56},{25,121},{32... | collective-permute-start | bytes 1671176 | tf_op jit(solution)/shard_map/terms_along_y/ppermute | solution.py:502
  13.2 10.7 %collective-permute-start.5 = (f32[1088,128]{1,0:T(8,128)S(1)}, f32[1088,128]{1,0:T(8,128)S(1)}, u32[]{:S(2)}, u32[]{:S(2)}) collective-permute-start(f32[1088,128]{1,0:T(8,128)S(1)} %get-tuple-element.23), channel_id=1, source_target_pairs={{0,2},{1,7},{2,0},{3,5},{4,6},{5,3},{6,4},{7,1},{8,10},{9,15},{10,... | collective-permute-start | bytes 1671176 | tf_op jit(solution)/shard_map/terms_along_z/ppermute | solution.py:502
  57.3 9.1 %copy-start.2 = (f32[128,512]{1,0:T(8,128)S(1)}, f32[128,512]{1,0:T(8,128)}, u32[]{:S(2)}) copy-start(f32[128,512]{1,0:T(8,128)} %panel_ref.3) | copy-start | bytes 786436
  57.3 6.4 %collective-permute-start.6 = (f32[1536,128]{1,0:T(8,128)S(1)}, f32[1536,128]{1,0:T(8,128)S(1)}, u32[]{:S(2)}, u32[]{:S(2)}) collective-permute-start(f32[1536,128]{1,0:T(8,128)S(1)} %bitcast.11), channel_id=1, source_target_pairs={{0,1},{1,0},{2,3},{3,2},{4,5},{5,4},{6,7},{7,6},{8,9},{9,8},{10,11... | collective-permute-start | bytes 2359304 | tf_op jit(solution)/shard_map/swap_copies/ppermute | solution.py:510
  64.0 16.7 %collective-permute-start.9 = (f32[2,896,128]{2,1,0:T(8,128)S(1)}, f32[2,896,128]{2,1,0:T(8,128)S(1)}, u32[]{:S(2)}, u32[]{:S(2)}) collective-permute-start(f32[2,896,128]{2,1,0:T(8,128)S(1)} %get-tuple-element.28.refs_0_), channel_id=1, source_target_pairs={{0,2},{1,7},{2,0},{3,5},{4,6},{5,3},{6,4},{7,1},{8,10},{9,15},{10,... | collective-permute-start | bytes 2752520 | tf_op jit(solution)/shard_map/quarters_along_z/ppermute | solution.py:516
  64.2 16.5 %collective-permute-start.8 = (f32[2,896,128]{2,1,0:T(8,128)S(1)}, f32[2,896,128]{2,1,0:T(8,128)S(1)}, u32[]{:S(2)}, u32[]{:S(2)}) collective-permute-start(f32[2,896,128]{2,1,0:T(8,128)S(1)} %get-tuple-element.28.refs_0_), channel_id=1, source_target_pairs={{0,32},{1,97},{8,40},{9,105},{16,48},{17,113},{24,56},{25,121},{32... | collective-permute-start | bytes 2752520 | tf_op jit(solution)/shard_map/quarters_along_y/ppermute | solution.py:516
  65.0 15.7 %collective-permute-start.7 = (f32[2,896,128]{2,1,0:T(8,128)S(1)}, f32[2,896,128]{2,1,0:T(8,128)S(1)}, u32[]{:S(2)}, u32[]{:S(2)}) collective-permute-start(f32[2,896,128]{2,1,0:T(8,128)S(1)} %get-tuple-element.28.refs_0_), channel_id=1, source_target_pairs={{0,8},{1,25},{8,0},{9,17},{16,24},{17,9},{24,16},{25,1},{32,40},{3... | collective-permute-start | bytes 2752520 | tf_op jit(solution)/shard_map/quarters_along_x/ppermute | solution.py:516

commit v10 on v9

--- a/solution.py
+++ b/solution.py
@@ -8,23 +8,12 @@
 from jax.sharding import Mesh, PartitionSpec as P
 
 ridge_shift = 0.05
-HIGHEST = lax.Precision.HIGHEST
 tile = 128
 strip = 32
 half_strip = 16
 chips = ("grp", "z")
 classes = 4
 shares = (3, 3, 2, 2)
-
-
-def product(left, right, left_dim=1, right_dim=0):
-    return lax.dot_general(
-        left,
-        right,
-        (((left_dim,), (right_dim,)), ((), ())),
-        precision=HIGHEST,
-        preferred_element_type=jnp.float32,
-    )
 
 
 def three_parts(x):
@@ -163,13 +152,13 @@
             for j in range(0, n, tile):
                 quarters[k, c + j : c + j + tile, :] = part[k * tile : (k + 1) * tile, j : j + tile]
     near = pl.multiple_of(core * step, tile)
-    first = product(pt[pl.ds(near, tile), :], wp[:, pl.ds(near, step)])
+    first = stacked(pt[pl.ds(near, tile), :], wp[:, pl.ds(near, step)])
     gram[0:tile, :] = first[:, :tile]
     gram[2 * tile : 3 * tile, :] = first[:, tile:]
     near = pl.multiple_of(core * step + tile, tile)
-    gram[tile : 2 * tile, :] = product(pt[pl.ds(near, tile), :], wp[:, pl.ds(near, tile)])
+    gram[tile : 2 * tile, :] = stacked(pt[pl.ds(near, tile), :], wp[:, pl.ds(near, tile)])
     near = pl.multiple_of(core * tile, tile)
-    last = product(pt[pl.ds(near, tile), :], wp[:, step:])
+    last = stacked(pt[pl.ds(near, tile), :], wp[:, step:])
     gram[3 * tile : 4 * tile, :] = last[:, :tile]
     gram[4 * tile :, :] = last[:, tile:]
     most = max(shares)
@@ -310,20 +299,25 @@
     eye = jnp.where(rows == cols, 1.0, 0.0).astype(jnp.float32)
     own, width = panel_ref.shape
     picked = r_ref.shape[0]
-    for core, blocks in enumerate(gram_blocks):
-        for at, (i, j) in enumerate(blocks):
-            side = slice(at * tile, (at + 1) * tile)
-            block = jnp.where(place_ref[0] == core, near_ref[side, :], far_ref[side, :])
-            if i == j:
-                block = block + ridge_shift * eye
-            a_ref[i * tile : (i + 1) * tile, j * tile : (j + 1) * tile] = block
-    upper[...] = jnp.zeros_like(upper)
-    linv[...] = jnp.zeros_like(linv)
-    z_ref[...] = jnp.zeros_like(z_ref)
-    rows_ref[...] = panel_ref[...]
-    work[:, 0:tile] = a_ref[0:tile, 0:tile]
+    def block_of(core, at):
+        side = slice(at * tile, (at + 1) * tile)
+        block = jnp.where(place_ref[0] == core, near_ref[side, :], far_ref[side, :])
+        i, j = gram_blocks[core][at]
+        return block + ridge_shift * eye if i == j else block
+
+    def prepare():
+        for core, blocks in enumerate(gram_blocks):
+            for at, (i, j) in enumerate(blocks):
+                if j:
+                    a_ref[i * tile : (i + 1) * tile, j * tile : (j + 1) * tile] = block_of(core, at)
+        rows_ref[...] = panel_ref[...]
+        upper[...] = jnp.zeros_like(upper)
+        linv[...] = jnp.zeros_like(linv)
+        z_ref[...] = jnp.zeros_like(z_ref)
+
+    work[:, 0:tile] = block_of(0, 0)
     work[:, tile:] = eye
-    later = []
+    later = [prepare]
     for b in range(0, width, tile):
         e = b + tile
         n = e + tile
@@ -337,7 +331,7 @@
             y = stacked(rows_ref[:, b:e], inverse, 1, 1)
             last = jnp.concatenate([-stacked(inverse, w_ref[:, 0:b]), inverse], 1)
             linv[b:e, :] = last
-            z_ref[...] = z_ref[...] + stacked(y, last)
+            z_ref[...] = z_ref[...] + stacked_two(y, last)
             break
         beside = stacked(inverse, a_ref[b:e, e:n])
         work[:, 0:tile] = a_ref[e:n, e:n] - stacked(beside, beside, 0, 0)
@@ -365,7 +359,7 @@
 
         def inverses(b=b, e=e, n=n):
             w_ref[:, 0:e] = stacked(upper[0:e, e:n], linv[0:e, 0:e], 0, 0)
-            z_ref[:, 0:e] = z_ref[:, 0:e] + stacked(y_ref[:, b:e], linv[b:e, 0:e])
+            z_ref[:, 0:e] = z_ref[:, 0:e] + stacked_two(y_ref[:, b:e], linv[b:e, 0:e])
 
         later = [rows_of_tiles, remainder, inverses]
     at = pl.ds(pl.multiple_of(place_ref[1 + classes], picked), picked)

time: 84 us -> 83.8 us (level)
  no operation moved by 1% of the time
where the time goes in v10:
time: 83.8 us; the launch traced here: 83.5 us
  blocking collectives  33.1 us (39%)
  Pallas kernels  20.6 us (25%)
  starting transfers between devices  18.1 us (22%)
  waiting for transfers between devices  8.85 us (11%)
  local copies, waits for them, and re-layouts  2.18 us (3%)
    all_to_all x2, blocking collectives, exchange(): lax.all_to_all(rows.reshape(chip_count, 1, -1), chips, 0, 0, tiled=True)  33.1 us
    pallas_call x1, Pallas kernels, factor(): pl.pallas_call(factor_kernel, out_shape=(jax.ShapeDtypeStruct((width // t...  14.2 us
    ppermute x3, starting transfers between devices, local(): parts.append(lax.ppermute(terms[1 + m], axis, pairs(before, after)))  9.13 us
    ppermute x3, waiting for transfers between devices, local(): parts.append(lax.ppermute(terms[1 + m], axis, pairs(before, after)))  6.92 us
    ppermute x1, starting transfers between devices, local(): far_copies = lax.ppermute(copies, 'core', swap)  4.51 us
    pallas_call x1, Pallas kernels, finish(): pl.pallas_call(finish_kernel, out_shape=(jax.ShapeDtypeStruct((own, trail...  3.01 us
    ppermute x3, starting transfers between devices, local(): quarters.append(lax.ppermute(quarter, axis, pairs(before, after)))  2.37 us
    pallas_call x1, Pallas kernels, products(): pl.pallas_call(functools.partial(products_kernel, total_rows=total_rows),...  2.11 us
  transfers between devices with their start and end apart: 10, of which 4 were waited for; matrix products, arithmetic and copies ran while one was open for 0% of the time, Pallas kernels for 18%

profile of v10, /device:TPU:1, one launch (start us, length us, event | category | flops | bytes accessed | tf_op | source)
XLA Modules:
  0.0 83.5 jit_solution(7360834802038617650)
XLA Ops:
  0.6 0.0 copy-start
  0.6 1.1 %constant_dynamic-slice_fusion = f32[128,896]{1,0:T(8,128)S(1)} fusion(f32[128,1792]{1,0:T(8,128)} %refs_4_.1, s32[]{:T(128)S(6)} %select_n.31), kind=kLoop, calls=%fused_computation | loop fusion | bytes 917508 | tf_op jit(solution)/shard_map/dynamic_slice | solution.py:463
  1.8 0.0 copy-start.3
  1.8 1.5 %collective-permute-start.1 = (f32[128,896]{1,0:T(8,128)S(1)}, f32[128,896]{1,0:T(8,128)S(1)}, u32[]{:S(2)}, u32[]{:S(2)}) collective-permute-start(f32[128,896]{1,0:T(8,128)S(1)} %constant_dynamic-slice_fusion), channel_id=1, source_target_pairs={{0,1},{1,0},{2,3},{3,2},{4,5},{5,4},{6,7},{7,6},{8,9},{9,8},{10,11... | collective-permute-start | bytes 1376264 | tf_op jit(solution)/shard_map/swap_inputs/ppermute | solution.py:467
  3.3 0.1 collective-permute-start
  3.4 0.0 copy-done.3
  3.4 0.5 collective-permute-start.2
  3.9 0.1 stack.27.place_ref
  3.9 0.0 copy-done
  3.9 0.0 copy-start.1
  4.0 1.0 %copy-done.1 = f32[128,512]{1,0:T(8,128)S(1)} copy-done((f32[128,512]{1,0:T(8,128)S(1)}, f32[128,512]{1,0:T(8,128)}, u32[]{:S(2)}) %copy-start.1) | copy-done | bytes 262168
  4.9 0.7 own_operands.1
  5.6 0.0 collective-permute-done.2.far_counts_ref
  5.6 0.0 collective-permute-done.other_ref
  5.6 0.0 collective-permute-done.1.far_ref
  5.6 2.1 %local_products.1 = (f32[1088,128]{1,0:T(8,128)S(1)}, f32[1088,128]{1,0:T(8,128)S(1)}, f32[1088,128]{1,0:T(8,128)S(1)}, f32[1088,128]{1,0:T(8,128)S(1)}) custom-call(s32[6]{0:T(128)S(1)} %stack.27.place_ref, f32[512,128]{1,0:T(8,128)S(1)} %get-tuple-element.17.own_pt, f32[128,512]{1,0:T(8,128)S(1)} %get-tuple-element.18.own_wp, ...), custom_call_target="tpu_custom_call" | custom-call | tf_op jit(solution)/shard_map/local_products/pallas_call | solution.py:186
  7.8 2.6 %collective-permute-start.3 = (f32[1088,128]{1,0:T(8,128)S(1)}, f32[1088,128]{1,0:T(8,128)S(1)}, u32[]{:S(2)}, u32[]{:S(2)}) collective-permute-start(f32[1088,128]{1,0:T(8,128)S(1)} %get-tuple-element.21), channel_id=1, source_target_pairs={{0,8},{1,25},{8,0},{9,17},{16,24},{17,9},{24,16},{25,1},{32,40},{3... | collective-permute-start | bytes 1671176 | tf_op jit(solution)/shard_map/terms_along_x/ppermute | solution.py:496
  10.4 2.7 %collective-permute-start.4 = (f32[1088,128]{1,0:T(8,128)S(1)}, f32[1088,128]{1,0:T(8,128)S(1)}, u32[]{:S(2)}, u32[]{:S(2)}) collective-permute-start(f32[1088,128]{1,0:T(8,128)S(1)} %get-tuple-element.22), channel_id=1, source_target_pairs={{0,32},{1,97},{8,40},{9,105},{16,48},{17,113},{24,56},{25,121},{32... | collective-permute-start | bytes 1671176 | tf_op jit(solution)/shard_map/terms_along_y/ppermute | solution.py:496
  13.1 3.8 %collective-permute-start.5 = (f32[1088,128]{1,0:T(8,128)S(1)}, f32[1088,128]{1,0:T(8,128)S(1)}, u32[]{:S(2)}, u32[]{:S(2)}) collective-permute-start(f32[1088,128]{1,0:T(8,128)S(1)} %get-tuple-element.23), channel_id=1, source_target_pairs={{0,2},{1,7},{2,0},{3,5},{4,6},{5,3},{6,4},{7,1},{8,10},{9,15},{10,... | collective-permute-start | bytes 1671176 | tf_op jit(solution)/shard_map/terms_along_z/ppermute | solution.py:496
  16.9 0.5 collective-permute-done.3.refs_1_
  17.4 2.6 %collective-permute-done.4.refs_2_ = f32[1088,128]{1,0:T(8,128)S(1)} collective-permute-done((f32[1088,128]{1,0:T(8,128)S(1)}, f32[1088,128]{1,0:T(8,128)S(1)}, u32[]{:S(2)}, u32[]{:S(2)}) %collective-permute-start.4) | collective-permute-done | bytes 557088 | tf_op jit(solution)/shard_map/terms_along_y/ppermute | solution.py:496
  20.1 3.8 %collective-permute-done.5.refs_3_ = f32[1088,128]{1,0:T(8,128)S(1)} collective-permute-done((f32[1088,128]{1,0:T(8,128)S(1)}, f32[1088,128]{1,0:T(8,128)S(1)}, u32[]{:S(2)}, u32[]{:S(2)}) %collective-permute-start.5) | collective-permute-done | bytes 557088 | tf_op jit(solution)/shard_map/terms_along_z/ppermute | solution.py:496
  23.8 0.2 combine_terms.1
  24.0 16.3 %all_to_all.10 = f32[64,1,2176]{2,1,0:T(1,128)S(1)} all-to-all(f32[64,1,2176]{2,1,0:T(1,128)S(1)} %bitcast.14), channel_id=1, replica_groups=mesh['grp'=16,'z'=4,'core'=2] {'grp','z'}, dimensions={0} | all-to-all | bytes 1114112 | tf_op jit(solution)/shard_map/exchange/all_to_all | solution.py:490
  40.3 0.1 sum_pieces.1
  40.4 16.9 %all_to_all.11 = f32[64,1,3072]{2,1,0:T(1,128)S(1)} all-to-all(f32[64,1,3072]{2,1,0:T(1,128)S(1)} %bitcast.13), channel_id=1, replica_groups=mesh['grp'=16,'z'=4,'core'=2] {'grp','z'}, dimensions={0} | all-to-all | bytes 1572864 | tf_op jit(solution)/shard_map/exchange/all_to_all | solution.py:490
  57.3 0.0 copy-start.2
  57.3 4.5 %collective-permute-start.6 = (f32[1536,128]{1,0:T(8,128)S(1)}, f32[1536,128]{1,0:T(8,128)S(1)}, u32[]{:S(2)}, u32[]{:S(2)}) collective-permute-start(f32[1536,128]{1,0:T(8,128)S(1)} %bitcast.11), channel_id=1, source_target_pairs={{0,1},{1,0},{2,3},{3,2},{4,5},{5,4},{6,7},{7,6},{8,9},{9,8},{10,11... | collective-permute-start | bytes 2359304 | tf_op jit(solution)/shard_map/swap_copies/ppermute | solution.py:504
  61.8 1.9 %collective-permute-done.6.far_ref = f32[1536,128]{1,0:T(8,128)S(1)} collective-permute-done((f32[1536,128]{1,0:T(8,128)S(1)}, f32[1536,128]{1,0:T(8,128)S(1)}, u32[]{:S(2)}, u32[]{:S(2)}) %collective-permute-start.6) | collective-permute-done | bytes 786464 | tf_op jit(solution)/shard_map/swap_copies/ppermute | solution.py:504
  63.7 0.2 unpack_sums.1
  63.9 0.3 collective-permute-start.9
  64.2 0.8 collective-permute-start.8
  65.0 1.3 %collective-permute-start.7 = (f32[2,896,128]{2,1,0:T(8,128)S(1)}, f32[2,896,128]{2,1,0:T(8,128)S(1)}, u32[]{:S(2)}, u32[]{:S(2)}) collective-permute-start(f32[2,896,128]{2,1,0:T(8,128)S(1)} %get-tuple-element.28.refs_0_), channel_id=1, source_target_pairs={{0,8},{1,25},{8,0},{9,17},{16,24},{17,9},{24,16},{25,1},{32,40},{3... | collective-permute-start | bytes 2752520 | tf_op jit(solution)/shard_map/quarters_along_x/ppermute | solution.py:510
  66.3 0.0 copy-done.2
  66.3 14.2 %factor_gram.1 = (f32[4,192,128]{2,1,0:T(8,128)S(1)}, f32[64,512]{1,0:T(8,128)}) custom-call(s32[6]{0:T(128)S(1)} %stack.27.place_ref, f32[640,128]{1,0:T(8,128)S(1)} %get-tuple-element.24.near_ref, f32[640,128]{1,0:T(8,128)S(1)} %get-tuple-element.25.far_ref, f32[128,512]{1,0:T(8,128)S(1)} %copy-done.2), custom_call_target="tpu_custom_call" | custom-call | flops 20000000000 | bytes 4000000 | tf_op jit(solution)/shard_map/factor_gram/pallas_call | solution.py:377
  80.5 0.0 collective-permute-done.9.refs_3_
  80.5 0.0 collective-permute-done.8.refs_2_
  80.5 0.0 collective-permute-done.7.refs_1_
  80.5 3.0 %apply_factor.1 = (f32[128,1792]{1,0:T(8,128)}, f32[64,1792]{1,0:T(8,128)}) custom-call(s32[6]{0:T(128)S(1)} %stack.27.place_ref, f32[4,192,128]{2,1,0:T(8,128)S(1)} %get-tuple-element.27.mixed_ref, f32[2,896,128]{2,1,0:T(8,128)S(1)} %get-tuple-element.28.refs_0_, f32[2,896,128]{2,1,0:T(8,128)S(1)} %collective-permute-done.7.refs_1_, ...), custom_call_target="tpu_custom_call" | custom-call | tf_op jit(solution)/shard_map/apply_factor/pallas_call | solution.py:429
Async XLA Ops:
  0.6 3.3 %copy-start = (f32[128,1792]{1,0:T(8,128)S(1)}, f32[128,1792]{1,0:T(8,128)}, u32[]{:S(2)}) copy-start(f32[128,1792]{1,0:T(8,128)} %refs_4_.1) | copy-start | bytes 2752516
  1.8 1.6 %copy-start.3 = (s32[128]{0:T(128)S(1)}, s32[128]{0:T(128)}, u32[]{:S(2)}) copy-start(s32[128]{0:T(128)} %param.5) | copy-start | bytes 1540
  1.8 3.8 %collective-permute-start.1 = (f32[128,896]{1,0:T(8,128)S(1)}, f32[128,896]{1,0:T(8,128)S(1)}, u32[]{:S(2)}, u32[]{:S(2)}) collective-permute-start(f32[128,896]{1,0:T(8,128)S(1)} %constant_dynamic-slice_fusion), channel_id=1, source_target_pairs={{0,1},{1,0},{2,3},{3,2},{4,5},{5,4},{6,7},{7,6},{8,9},{9,8},{10,11... | collective-permute-start | bytes 1376264 | tf_op jit(solution)/shard_map/swap_inputs/ppermute | solution.py:467
  3.3 2.3 %collective-permute-start = (f32[128,512]{1,0:T(8,128)}, f32[128,512]{1,0:T(8,128)S(1)}, u32[]{:S(2)}, u32[]{:S(2)}) collective-permute-start(f32[128,512]{1,0:T(8,128)} %panel_ref.3), channel_id=1, source_target_pairs={{0,1},{1,0},{2,3},{3,2},{4,5},{5,4},{6,7},{7,6},{8,9},{9,8},{10,11... | collective-permute-start | bytes 786440 | tf_op jit(solution)/shard_map/swap_inputs/ppermute | solution.py:466
  3.4 2.2 %collective-permute-start.2 = (s32[1,128]{1,0:T(1,128)S(1)}, s32[1,128]{1,0:T(1,128)S(1)}, u32[]{:S(2)}, u32[]{:S(2)}) collective-permute-start(s32[1,128]{1,0:T(1,128)S(1)} %bitcast.16), channel_id=1, source_target_pairs={{0,1},{1,0},{2,3},{3,2},{4,5},{5,4},{6,7},{7,6},{8,9},{9,8},{10,11... | collective-permute-start | bytes 1544 | tf_op jit(solution)/shard_map/swap_inputs/ppermute | solution.py:465
  3.9 1.0 %copy-start.1 = (f32[128,512]{1,0:T(8,128)S(1)}, f32[128,512]{1,0:T(8,128)}, u32[]{:S(2)}) copy-start(f32[128,512]{1,0:T(8,128)} %panel_ref.3) | copy-start | bytes 786436
  7.8 9.7 %collective-permute-start.3 = (f32[1088,128]{1,0:T(8,128)S(1)}, f32[1088,128]{1,0:T(8,128)S(1)}, u32[]{:S(2)}, u32[]{:S(2)}) collective-permute-start(f32[1088,128]{1,0:T(8,128)S(1)} %get-tuple-element.21), channel_id=1, source_target_pairs={{0,8},{1,25},{8,0},{9,17},{16,24},{17,9},{24,16},{25,1},{32,40},{3... | collective-permute-start | bytes 1671176 | tf_op jit(solution)/shard_map/terms_along_x/ppermute | solution.py:496
  10.4 9.7 %collective-permute-start.4 = (f32[1088,128]{1,0:T(8,128)S(1)}, f32[1088,128]{1,0:T(8,128)S(1)}, u32[]{:S(2)}, u32[]{:S(2)}) collective-permute-start(f32[1088,128]{1,0:T(8,128)S(1)} %get-tuple-element.22), channel_id=1, source_target_pairs={{0,32},{1,97},{8,40},{9,105},{16,48},{17,113},{24,56},{25,121},{32... | collective-permute-start | bytes 1671176 | tf_op jit(solution)/shard_map/terms_along_y/ppermute | solution.py:496
  13.1 10.7 %collective-permute-start.5 = (f32[1088,128]{1,0:T(8,128)S(1)}, f32[1088,128]{1,0:T(8,128)S(1)}, u32[]{:S(2)}, u32[]{:S(2)}) collective-permute-start(f32[1088,128]{1,0:T(8,128)S(1)} %get-tuple-element.23), channel_id=1, source_target_pairs={{0,2},{1,7},{2,0},{3,5},{4,6},{5,3},{6,4},{7,1},{8,10},{9,15},{10,... | collective-permute-start | bytes 1671176 | tf_op jit(solution)/shard_map/terms_along_z/ppermute | solution.py:496
  57.3 9.1 %copy-start.2 = (f32[128,512]{1,0:T(8,128)S(1)}, f32[128,512]{1,0:T(8,128)}, u32[]{:S(2)}) copy-start(f32[128,512]{1,0:T(8,128)} %panel_ref.3) | copy-start | bytes 786436
  57.3 6.4 %collective-permute-start.6 = (f32[1536,128]{1,0:T(8,128)S(1)}, f32[1536,128]{1,0:T(8,128)S(1)}, u32[]{:S(2)}, u32[]{:S(2)}) collective-permute-start(f32[1536,128]{1,0:T(8,128)S(1)} %bitcast.11), channel_id=1, source_target_pairs={{0,1},{1,0},{2,3},{3,2},{4,5},{5,4},{6,7},{7,6},{8,9},{9,8},{10,11... | collective-permute-start | bytes 2359304 | tf_op jit(solution)/shard_map/swap_copies/ppermute | solution.py:504
  63.9 16.6 %collective-permute-start.9 = (f32[2,896,128]{2,1,0:T(8,128)S(1)}, f32[2,896,128]{2,1,0:T(8,128)S(1)}, u32[]{:S(2)}, u32[]{:S(2)}) collective-permute-start(f32[2,896,128]{2,1,0:T(8,128)S(1)} %get-tuple-element.28.refs_0_), channel_id=1, source_target_pairs={{0,2},{1,7},{2,0},{3,5},{4,6},{5,3},{6,4},{7,1},{8,10},{9,15},{10,... | collective-permute-start | bytes 2752520 | tf_op jit(solution)/shard_map/quarters_along_z/ppermute | solution.py:510
  64.2 16.3 %collective-permute-start.8 = (f32[2,896,128]{2,1,0:T(8,128)S(1)}, f32[2,896,128]{2,1,0:T(8,128)S(1)}, u32[]{:S(2)}, u32[]{:S(2)}) collective-permute-start(f32[2,896,128]{2,1,0:T(8,128)S(1)} %get-tuple-element.28.refs_0_), channel_id=1, source_target_pairs={{0,32},{1,97},{8,40},{9,105},{16,48},{17,113},{24,56},{25,121},{32... | collective-permute-start | bytes 2752520 | tf_op jit(solution)/shard_map/quarters_along_y/ppermute | solution.py:510
  65.0 15.5 %collective-permute-start.7 = (f32[2,896,128]{2,1,0:T(8,128)S(1)}, f32[2,896,128]{2,1,0:T(8,128)S(1)}, u32[]{:S(2)}, u32[]{:S(2)}) collective-permute-start(f32[2,896,128]{2,1,0:T(8,128)S(1)} %get-tuple-element.28.refs_0_), channel_id=1, source_target_pairs={{0,8},{1,25},{8,0},{9,17},{16,24},{17,9},{24,16},{25,1},{32,40},{3... | collective-permute-start | bytes 2752520 | tf_op jit(solution)/shard_map/quarters_along_x/ppermute | solution.py:510
